TPU v7x, 32 devices: a whole 2x2x4 slice. The times are simulated.
32 devices in a mesh: gx: 8 (over z, core), gy: 4 (over y, x).
Axes of the slice: x: 2, y: 2, z: 4, core: 2. Of those that a mesh axis runs over, the one named last changes fastest.
Arguments:
- u_field: float32 [256, 1024], P('gx', 'gy'), may hold values from -6 to 6
- v_field: float32 [256, 1024], P('gx', 'gy'), may hold values from -6 to 6
- w_first: bfloat16 [9, 64, 2], replicated, may hold values from -1.5 to 1.5
- b_first: float32 [64], replicated, may hold values from -3 to 3
- w_second: bfloat16 [9, 64, 64], replicated, may hold values from -0.25 to 0.25
- b_second: float32 [64], replicated, may hold values from -3 to 3
- w_third: bfloat16 [9, 16, 64], replicated, may hold values from -0.25 to 0.25
- b_third: float32 [16], replicated, may hold values from -3 to 3
Outputs:
- u_next: float32 [256, 1024], P('gx', 'gy')
- v_next: float32 [256, 1024], P('gx', 'gy')
All inputs are finite; a program needn't handle non-finite values.
Results may differ from a plain program's by a relative error of at most 0.0023.
Values sent between devices are 32-bit elements; how exact they have to be, the bound alone decides.
No kernel may reach another device: no remote copies, remote signals or barrier semaphores. Data moves between devices by JAX's collectives and lax.ppermute only.
A program may use at most 64 MiB of HBM per device.

v0:
```python
import functools
import math

import jax
import jax.numpy as jnp
import ml_dtypes
import numpy as np
from jax import lax
from jax.experimental import pallas as pl
from jax.experimental.pallas import tpu as pltpu
from jax.sharding import PartitionSpec as P

step_ratio = 0.4
stencil_base = (-0.0625, 0.5625, 0.5625, -0.0625)
f32 = jnp.float32
bf16 = jnp.bfloat16

vmem_limit = 48 * 1024 * 1024


def split(value):
    high = value.astype(bf16)
    return high, (value - high.astype(f32)).astype(bf16)


def split_table(table):
    high = table.astype(ml_dtypes.bfloat16)
    low = (table - high.astype(np.float64)).astype(ml_dtypes.bfloat16)
    return high, low


def dot(a, b):
    return jnp.dot(a, b, preferred_element_type=f32)


def product_3(value, high, low):
    rows = value.shape[0]
    first, second = split(value)
    both = dot(jnp.concatenate([first, second], axis=0), high)
    return both[:rows] + both[rows:] + dot(first, low)


def parity(shape):
    rows = lax.broadcasted_iota(jnp.int32, shape, 0)
    return jnp.where(rows < shape[0] // 2, 1.0, -1.0).astype(f32)


def swap(value):
    half = value.shape[0] // 2
    return jnp.concatenate([value[half:], value[:half]], axis=0)


def fetch(sources, targets, sems):
    copies = [pltpu.make_async_copy(a, b, sems.at[i]) for i, (a, b) in enumerate(zip(sources, targets))]
    for copy in copies:
        copy.start()
    for copy in copies:
        copy.wait()


def rows_kernel(u_hbm, v_hbm, last_ref, first_ref, u_ref, v_ref, sems):
    fetch((u_hbm, v_hbm), (u_ref, v_ref), sems)
    height = u_ref.shape[0]
    for q, ref in enumerate((u_ref, v_ref)):
        last_ref[4 * q : 4 * q + 4, :] = ref[height - 4 : height, :]
        first_ref[4 * q : 4 * q + 4, :] = ref[0:4, :]


def columns_kernel(u_ref, v_ref, bot_ref, top_ref, last_ref, first_ref, strip):
    height, breadth = u_ref.shape
    rows = height + 8
    for side, out in ((0, first_ref), (breadth - 128, last_ref)):
        strip[...] = jnp.zeros_like(strip)
        for q, ref in enumerate((u_ref, v_ref)):
            start = rows * q
            strip[start : start + height, :] = ref[:, side : side + 128]
            strip[start + height : start + height + 4, :] = bot_ref[4 * q : 4 * q + 4, side : side + 128]
            strip[start + height + 4 : start + rows, :] = top_ref[4 * q : 4 * q + 4, side : side + 128]
        turned = strip[...].T
        out[...] = turned[0:8] if side == 0 else turned[120:128]


def weights_kernel(
    w1_hbm, w2_hbm, w3_hbm, b1_hbm, b2_hbm, b3_hbm, k1_ref, k2_ref, even_ref, odd_ref, c1_ref, c2_ref, c3_ref,
    w1_ref, w2_ref, w3_ref, b1_ref, b2_ref, b3_ref, sems, *, rows
):
    fetch(
        (w1_hbm, w2_hbm, w3_hbm, b1_hbm, b2_hbm, b3_hbm), (w1_ref, w2_ref, w3_ref, b1_ref, b2_ref, b3_ref), sems
    )
    groups, depth, _ = k1_ref.shape
    c1_ref[...] = jnp.concatenate([b1_ref[...]] * 4, axis=1)
    c2_ref[...] = jnp.concatenate([b2_ref[...]] * 4, axis=1)
    place = lax.broadcasted_iota(jnp.int32, (64, 16), 0) // 4
    channel = 8 * (place // 8) + 4 * (place % 2) + (place // 2) % 4
    hit = channel == lax.broadcasted_iota(jnp.int32, (64, 16), 1)
    c3_ref[...] = jnp.sum(jnp.where(hit, b3_ref[...], 0.0), axis=1, keepdims=True)

    pick = lax.broadcasted_iota(jnp.int32, (8, 2), 0) == lax.broadcasted_iota(jnp.int32, (8, 2), 1)
    pick = jnp.where(pick, 1.0, 0.0).astype(bf16)
    turned = [
        lax.dot_general(pick, w1_ref[tap], (((1,), (1,)), ((), ())), preferred_element_type=f32) for tap in range(9)
    ]
    turned = [jnp.concatenate([tap] * 4, axis=1) for tap in turned]
    spread = []
    for d in range(3):
        parts = [
            jnp.broadcast_to(turned[3 * d + s][q : q + 1, :], (rows, 256))
            for s in range(3)
            for q in range(2)
        ]
        parts.append(jnp.zeros((depth - 6 * rows, 256), f32))
        spread.append(jnp.concatenate(parts, axis=0))
    row = lax.broadcasted_iota(jnp.int32, (rows, 256), 0) - lax.broadcasted_iota(jnp.int32, (rows, 256), 1) // 64
    row = jnp.where(row < 0, row + rows, row)
    row = jnp.concatenate([row] * 6 + [jnp.full((depth - 6 * rows, 256), -1, jnp.int32)], axis=0)
    for r in range(groups):
        near = [row == (4 * r + d - 1) % rows for d in range(3)]
        block = jnp.where(near[0], spread[0], jnp.where(near[1], spread[1], jnp.where(near[2], spread[2], 0.0)))
        k1_ref[r] = block.astype(bf16)

    k2_ref[...] = jnp.zeros(k2_ref.shape, bf16)
    slots = {-1: 5, 0: 0, 1: 1, 2: 2, 3: 3, 4: 6}
    blank = jnp.zeros((64, 64), f32)
    for c in range(3):
        taps = [w2_ref[3 * d + c].astype(f32) for d in range(3)]
        two = [(taps[0], blank), (taps[1], taps[0]), (taps[2], taps[1]), (blank, taps[2])]
        two = [jnp.concatenate(pair, axis=0).T.astype(bf16) for pair in two]
        for h in range(2):
            for d in range(4):
                slot = slots[d + 2 * h - 1]
                k2_ref[64 * slot : 64 * slot + 64, 256 * c + 128 * h : 256 * c + 128 * h + 128] = two[d]

    taps = [[w3_ref[3 * d + c].astype(f32) for d in range(3)] for c in range(3)]
    blank = jnp.zeros((16, 64), f32)
    filler = jnp.zeros((64, 256), bf16)
    parts = [filler] * 8
    for k, slot in slots.items():
        pieces = [taps[c][k - t + 1] if 0 <= k - t + 1 < 3 else blank for c in range(3) for t in range(4)]
        pieces += [blank] * 4
        parts[slot] = jnp.concatenate(pieces, axis=0).T.astype(bf16)
    raw = jnp.concatenate(parts, axis=0)
    source = lax.broadcasted_iota(jnp.int32, (256, 256), 0)
    target = lax.broadcasted_iota(jnp.int32, (256, 256), 1)
    inner = target % 64
    place = inner // 4
    channel = 8 * (place // 8) + 4 * (place % 2) + (place // 2) % 4
    lane = 16 * (inner % 4) + channel
    part = target // 64
    column_even = jnp.where(part == 3, -1, 64 * part + lane)
    column_odd = jnp.where(
        part == 2, -1, jnp.where(part == 3, 128 + lane, jnp.where(part == 0, 64 + lane, lane))
    )
    even_ref[...] = dot(raw, jnp.where(source == column_even, 1.0, 0.0).astype(bf16)).astype(bf16)
    odd_ref[...] = dot(raw, jnp.where(source == column_odd, 1.0, 0.0).astype(bf16)).astype(bf16)


def advance_kernel(
    u_ref, v_ref, bot_ref, top_ref, right_ref, left_ref, w1_ref, w2_ref, w3e_ref, w3o_ref,
    b1_ref, b2_ref, b3_ref, star_ref, field, first, second, coeff, strip,
):
    height, breadth = u_ref.shape
    rows = height + 8
    groups = rows // 4
    lanes = breadth + 128
    strip[...] = jnp.zeros_like(strip)
    strip[0:4, :] = right_ref[0:4, :]
    strip[124:128, :] = left_ref[4:8, :]
    beside = strip[...].T
    for q, ref in enumerate((u_ref, v_ref)):
        field[q, 8 : 8 + height, :breadth] = ref[...]
        field[q, 8 + height : 12 + height, :breadth] = bot_ref[4 * q : 4 * q + 4, :]
        field[q, 12 + height : 16 + height, :breadth] = top_ref[4 * q : 4 * q + 4, :]
        field[q, 8 : 8 + rows, breadth:] = beside[rows * q : rows * q + rows]
        field[q, 0:8, :] = field[q, rows : rows + 8, :]
        field[q, 8 + rows : 16 + rows, :] = field[q, 8:16, :]
    whole = jnp.concatenate([field[0, 8 : 8 + rows], field[1, 8 : 8 + rows]], axis=0)
    pieces = [pltpu.roll(whole, 1, 1), whole, pltpu.roll(whole, lanes - 1, 1)]
    depth = w1_ref.shape[1]
    pieces.append(jnp.zeros((depth - 6 * rows, lanes), f32))
    turned = jnp.concatenate(pieces, axis=0).T
    patches = jnp.concatenate([turned[: breadth + 8], turned[lanes - 8 :]], axis=0).astype(bf16)
    span = breadth + 16
    for r in range(groups):
        first[r] = jnp.maximum(dot(patches, w1_ref[r]) + b1_ref[...], 0.0).astype(bf16)

    def gathered(source, r):
        before, after = (r - 1) % groups, (r + 1) % groups
        beside = jnp.concatenate([source[before, :, 128:], source[after, :, :128]], axis=1)
        return source[r], beside

    for r in range(groups):
        own, beside = gathered(first, r)
        total = dot(own, w2_ref[:256]) + dot(beside, w2_ref[256:])
        total = pltpu.roll(total[:, :256], 1, 0) + total[:, 256:512] + pltpu.roll(total[:, 512:], span - 1, 0)
        second[r] = jnp.maximum(total + b2_ref[...], 0.0).astype(bf16)

    def last(r, ref):
        own, beside = gathered(second, r)
        total = dot(own, ref[:256]) + dot(beside, ref[256:])
        left_part = total[:, :128]
        return pltpu.roll(left_part, 1, 0) + pltpu.roll(left_part, 64, 1) + pltpu.roll(total[:, 128:], span - 1, 0)

    def keep(r, block):
        coeff[r, :, :breadth] = block[:, :breadth]
        coeff[r, :, breadth:] = block[:, breadth:]

    pairs = [(i, i + 1) for i in range(0, groups - 2, 2)] + [(groups - 1, None)]
    for even, odd in pairs:
        block = last(even, w3e_ref)
        if odd is not None:
            other = last(odd, w3o_ref)
            lower = lax.broadcasted_iota(jnp.int32, block.shape, 1) < 64
            block = jnp.where(lower, block, other)
        block = jnp.concatenate(
            [block[: breadth + 8], jnp.zeros((lanes - span, 128), f32), block[breadth + 8 :]], axis=0
        ).T
        keep(even, block[:64])
        if odd is not None:
            keep(odd, block[64:])

    offsets = b3_ref[...]
    sub = lax.broadcasted_iota(jnp.int32, (8, breadth), 0) % 4

    def stacked(r, shift, qs=(0, 1)):
        start = 8 + 4 * r + shift
        return jnp.concatenate([field[q, start : start + 4, :] for q in qs], axis=0)

    previous = None
    for r in [groups - 1] + list(range(groups - 2)):
        weights = coeff[r] + offsets
        weights = [weights[8 * i : 8 * i + 8] for i in range(8)]
        centre = stacked(r, 0)

        def stencil(d):
            four = weights[4 * d : 4 * d + 4]
            mean = (four[0] + four[1] + four[2] + four[3]) * 0.25
            return [base + w - mean for base, w in zip(stencil_base, four)]

        east = stencil(0)
        flow_x = (
            east[0] * stacked(r, -1) + east[1] * centre + east[2] * stacked(r, 1) + east[3] * stacked(r, 2)
        )
        flow_x = flow_x * (0.5 * (stacked(r, 0, (0, 0)) + stacked(r, 1, (0, 0))))
        flow_x = flow_x[:, :breadth]
        if previous is not None:
            north = stencil(1)
            flow_y = (
                north[0] * pltpu.roll(centre, 1, 1)
                + north[1] * centre
                + north[2] * pltpu.roll(centre, lanes - 1, 1)
                + north[3] * pltpu.roll(centre, lanes - 2, 1)
            )
            carrier = stacked(r, 0, (1, 1))
            flow_y = flow_y * (0.5 * (carrier + pltpu.roll(carrier, lanes - 1, 1)))
            change_y = (flow_y - pltpu.roll(flow_y, 1, 1))[:, :breadth]
            above = jnp.where(sub == 0, pltpu.roll(previous, 5, 0), pltpu.roll(flow_x, 1, 0))
            star = centre[:, :breadth] - step_ratio * (flow_x - above + change_y)
            star_ref[4 * r : 4 * r + 4, :] = star[:4]
            star_ref[height + 4 * r : height + 4 * r + 4, :] = star[4:]
        previous = flow_x


def own_twiddle(ref):
    own = ref[lax.axis_index("gy")]
    half = own.shape[0] // 2
    return own[:half], own[half:]


def column_kernel(*refs):
    *blocks, twiddle_ref, high_ref, low_ref, out_ref = refs
    rows, breadth = out_ref.shape
    cosine, sine = own_twiddle(twiddle_ref)
    sign = parity((rows, breadth))
    mixed = None
    for k, ref in enumerate(blocks):
        block = ref[...] * sign
        term = block * cosine[k : k + 1, :] + swap(block) * (sign * sine[k : k + 1, :])
        mixed = term if mixed is None else mixed + term
    spectra = product_3(mixed, high_ref[...], low_ref[...])
    out_ref[...] = spectra[:, :breadth] + sign * swap(spectra[:, breadth:])


def row_kernel(*refs, scale):
    *blocks, table_ref, table_low_ref, high_ref, low_ref, out_ref, gathered = refs
    rows, breadth = out_ref.shape
    height = rows // 2
    length = len(blocks) * height
    own_index = lax.axis_index("gx")
    for k, ref in enumerate(blocks):
        start = pl.multiple_of((own_index ^ k) * height, height)
        gathered[pl.ds(start, height), :breadth] = ref[:height, :]
        gathered[pl.ds(start, height), breadth:] = ref[height:, :]
    data = gathered[...]
    data, data_low = split(data)
    spectra = dot(table_ref[...], data) + dot(table_ref[...], data_low) + dot(table_low_ref[...], data)
    real_part = spectra[:length, :breadth] + spectra[length:, breadth:]
    imag_part = spectra[:length, breadth:] - spectra[length:, :breadth]
    index = lax.broadcasted_iota(jnp.int32, (length, breadth), 0)
    wave_x = jnp.where(index >= length // 2, index - length, index).astype(f32) * (2.0 * math.pi / length)
    members_y = lax.axis_size("gy")
    grid_y = members_y * breadth
    number_y = lax.axis_index("gy") + members_y * lax.broadcasted_iota(jnp.int32, (1, breadth), 1)
    wave_y = jnp.where(number_y >= grid_y // 2, number_y - grid_y, number_y).astype(f32) * (2.0 * math.pi / grid_y)
    edge_y = number_y == grid_y // 2
    edge_x = index == length // 2
    total = wave_x * wave_x + wave_y * wave_y
    zero = total == 0.0
    inverse = scale / jnp.where(zero, 1.0, total)
    same = (0.5 * inverse) * (wave_y * wave_y - wave_x * wave_x)
    cross = jnp.where(edge_x != edge_y, 0.0, -inverse * wave_x * wave_y)
    same_real = jnp.where(zero, 0.5 * scale, same)
    same_imag = jnp.where(zero, -0.5 * scale, same)
    kept_real = same_real * real_part - cross * imag_part
    kept_imag = same_imag * imag_part + cross * real_part
    kept, kept_low = split(jnp.concatenate([kept_real, kept_imag], axis=1))
    start = pl.multiple_of(own_index * height, height)

    def own(ref):
        parts = [ref[pl.ds(start, height), :], ref[pl.ds(pl.multiple_of(length + start, height), height), :]]
        return jnp.concatenate(parts, axis=0)

    table, table_low = own(table_ref), own(table_low_ref)
    home = dot(table, kept) + dot(table, kept_low) + dot(table_low, kept)
    home = jnp.concatenate(
        [
            home[:height, :breadth] - home[height:, breadth:],
            home[:height, breadth:] + home[height:, :breadth],
        ],
        axis=0,
    )
    columns = product_3(home, high_ref[...], low_ref[...])
    out_ref[...] = columns[:, :breadth] - parity((rows, breadth)) * swap(columns[:, breadth:])


def home_kernel(*refs):
    *blocks, twiddle_ref, star_ref, u_ref, v_ref = refs
    rows, breadth = star_ref.shape
    cosine, sine = own_twiddle(twiddle_ref)
    sign = parity((rows, breadth))
    result = 0.5 * star_ref[...]
    for k, ref in enumerate(blocks):
        block = ref[...]
        result = result + block * cosine[k : k + 1, :] - swap(block) * (sign * sine[k : k + 1, :])
    u_ref[...] = result[: rows // 2]
    v_ref[...] = result[rows // 2 :]


def call(kernel, shapes, scratch=(), flops=10**7, outside=0):
    specs = {"in_specs": [pl.BlockSpec(memory_space=pltpu.HBM)] * outside} if outside else {}
    return pl.pallas_call(
        kernel,
        out_shape=shapes,
        scratch_shapes=list(scratch),
        compiler_params=pltpu.CompilerParams(vmem_limit_bytes=vmem_limit),
        cost_estimate=pl.CostEstimate(flops=flops, bytes_accessed=2**20, transcendentals=0),
        **specs,
    )


@functools.lru_cache(None)
def tables(height, breadth, members_x, members_y):
    turn = 2.0 * math.pi
    j = np.arange(breadth)
    phase = turn * (np.outer(j, j) % breadth) / breadth
    column = split_table(np.concatenate([np.cos(phase), np.sin(phase)], axis=1))
    length = height * members_x
    k = np.arange(length)
    phase = turn * (np.outer(k, k) % length) / length
    row = split_table(np.concatenate([np.cos(phase), np.sin(phase)], axis=0))
    g = np.arange(members_y)[:, None, None]
    partner = g ^ np.arange(members_y)[None, :, None]
    whole = breadth * members_y
    out = turn * ((partner * breadth + j) * g % whole) / whole
    home = turn * ((g * breadth + j) * partner % whole) / whole
    twiddle_out, twiddle_home = [
        np.concatenate([np.cos(phase), np.sin(phase)], axis=1).astype(np.float32) for phase in (out, home)
    ]
    return column, row, twiddle_out, twiddle_home


def partner(block, axis, k):
    return lax.ppermute(block, axis, [(i, i ^ k) for i in range(lax.axis_size(axis))])


def gather_y(block):
    return [block] + [partner(block, "gy", k) for k in range(1, lax.axis_size("gy"))]


def gather_x(block):
    own = [block] + [partner(block, "gx", k) for k in range(2, lax.axis_size("gx"), 2)]
    return [other for held in own for other in (held, partner(held, "gx", 1))]


def on_device(u_field, v_field, w_first, b_first, w_second, b_second, w_third, b_third):
    height, breadth = u_field.shape
    members_x, members_y = lax.axis_size("gx"), lax.axis_size("gy")
    grid_x, grid_y = height * members_x, breadth * members_y
    rows = height + 8
    groups = rows // 4
    span = breadth + 16
    shape = jax.ShapeDtypeStruct

    def shifted(value, axis, distance):
        peers = lax.axis_size(axis)
        return lax.ppermute(value, axis, [(i, (i + distance) % peers) for i in range(peers)])

    with jax.named_scope("surroundings"):
        edge = shape((8, breadth), f32)
        block = shape((height, breadth), f32)
        last, first, u_field, v_field = call(
            rows_kernel, (edge, edge, block, block), (pltpu.SemaphoreType.DMA((2,)),), outside=2
        )(u_field, v_field)
        top, bottom = shifted(last, "gx", 1), shifted(first, "gx", -1)
        edge = shape((8, 128), f32)
        last, first = call(columns_kernel, (edge, edge), (pltpu.VMEM((128, 128), f32),))(
            u_field, v_field, bottom, top
        )
        left, right = shifted(last, "gy", 1), shifted(first, "gy", -1)

    with jax.named_scope("weights"):
        weights = call(
            functools.partial(weights_kernel, rows=rows),
            (
                shape((groups, -(-6 * rows // 128) * 128, 256), bf16),
                shape((512, 768), bf16),
                shape((512, 256), bf16),
                shape((512, 256), bf16),
                shape((1, 256), f32),
                shape((1, 256), f32),
                shape((64, 1), f32),
            ),
            (
                pltpu.VMEM(w_first.shape, bf16),
                pltpu.VMEM(w_second.shape, bf16),
                pltpu.VMEM(w_third.shape, bf16),
                pltpu.VMEM((1, 64), f32),
                pltpu.VMEM((1, 64), f32),
                pltpu.VMEM((1, 16), f32),
                pltpu.SemaphoreType.DMA((6,)),
            ),
            outside=6,
        )(w_first, w_second, w_third, b_first[None], b_second[None], b_third[None])

    block = shape((2 * height, breadth), f32)
    with jax.named_scope("advance"):
        star = call(
            advance_kernel,
            block,
            (
                pltpu.VMEM((2, rows + 16, breadth + 128), f32),
                pltpu.VMEM((groups, span, 256), bf16),
                pltpu.VMEM((groups, span, 256), bf16),
                pltpu.VMEM((groups, 64, breadth + 128), f32),
                pltpu.VMEM((128, 128), f32),
            ),
            flops=10**9,
        )(u_field, v_field, bottom, top, right, left, *weights)

    column, row, twiddle_out, twiddle_home = tables(height, breadth, members_x, members_y)
    column, row = [[jnp.asarray(t) for t in pair] for pair in (column, row)]
    spectra = call(column_kernel, block)(*gather_y(star), jnp.asarray(twiddle_out), *column)
    columns = call(
        functools.partial(row_kernel, scale=1.0 / (grid_x * grid_y)),
        block,
        (pltpu.VMEM((grid_x, 2 * breadth), f32),),
    )(*gather_x(spectra), *row, *column)
    part = shape((height, breadth), f32)
    return tuple(call(home_kernel, (part, part))(*gather_y(columns), jnp.asarray(twiddle_home), star))


def solution(mesh):
    return jax.shard_map(
        on_device,
        mesh=mesh,
        in_specs=(P("gx", "gy"), P("gx", "gy"), P(), P(), P(), P(), P(), P()),
        out_specs=(P("gx", "gy"), P("gx", "gy")),
        check_vma=False,
    )
```

profile of v0, /device:TPU:0, one launch (start us, length us, event | category | flops | bytes accessed | tf_op | source)
XLA Modules:
  0.0 49.3 jit_solution(33094809712103793)
XLA Ops:
  0.6 0.7 %copy-done.7 = f32[32,256]{1,0:T(8,128)S(1)} copy-done((f32[32,256]{1,0:T(8,128)S(1)}, f32[32,256]{1,0:T(8,128)}, u32[]{:S(2)}) %copy-start.7) | copy-done | bytes 32792
  1.4 0.8 %copy-done.8 = f32[32,256]{1,0:T(8,128)S(1)} copy-done((f32[32,256]{1,0:T(8,128)S(1)}, f32[32,256]{1,0:T(8,128)}, u32[]{:S(2)}) %copy-start.8) | copy-done | bytes 32792
  2.2 4.5 %collective-permute-start = (f32[8,256]{1,0:T(8,128)S(1)}, f32[8,256]{1,0:T(8,128)S(1)}, u32[]{:S(2)}, u32[]{:S(2)}) collective-permute-start(f32[8,256]{1,0:T(8,128)S(1)} %get-tuple-element.17), channel_id=1, source_target_pairs={{0,28},{4,0},{8,4},{12,8},{16,12},{20,16},{24,20},{28,24},{1,29},{... | collective-permute-start | bytes 24584 | tf_op jit(solution)/shard_map/surroundings/ppermute | solution.py:405
  6.8 1.4 %collective-permute-done.bot_ref = f32[8,256]{1,0:T(8,128)S(1)} collective-permute-done((f32[8,256]{1,0:T(8,128)S(1)}, f32[8,256]{1,0:T(8,128)S(1)}, u32[]{:S(2)}, u32[]{:S(2)}) %collective-permute-start) | collective-permute-done | bytes 8224 | tf_op jit(solution)/shard_map/surroundings/ppermute | solution.py:405
  8.1 3.5 %collective-permute-done.1.top_ref = f32[8,256]{1,0:T(8,128)S(1)} collective-permute-done((f32[8,256]{1,0:T(8,128)S(1)}, f32[8,256]{1,0:T(8,128)S(1)}, u32[]{:S(2)}, u32[]{:S(2)}) %collective-permute-start.1) | collective-permute-done | bytes 8224 | tf_op jit(solution)/shard_map/surroundings/ppermute | solution.py:405
  11.7 2.5 %collective-permute-start.2 = (f32[8,128]{1,0:T(8,128)S(1)}, f32[8,128]{1,0:T(8,128)S(1)}, u32[]{:S(2)}, u32[]{:S(2)}) collective-permute-start(f32[8,128]{1,0:T(8,128)S(1)} %get-tuple-element.19), channel_id=1, source_target_pairs={{0,3},{1,0},{2,1},{3,2},{4,7},{5,4},{6,5},{7,6},{8,11},{9,8},{10,9... | collective-permute-start | bytes 12296 | tf_op jit(solution)/shard_map/surroundings/ppermute | solution.py:405
  14.2 0.9 %copy.16.w1_hbm = bf16[9,64,2]{2,1,0:T(8,128)(2,1)S(1)} copy(bf16[9,64,2]{1,2,0:T(2,128)(2,1)} %param.16) | data formatting | bytes 4608 | tf_op args[2]
  15.1 0.9 %copy-done.4 = bf16[9,64,64]{2,1,0:T(8,128)(2,1)S(1)} copy-done((bf16[9,64,64]{2,1,0:T(8,128)(2,1)S(1)}, bf16[9,64,64]{2,1,0:T(8,128)(2,1)}, u32[]{:S(2)}) %copy-start.4) | copy-done | bytes 73752
  16.0 0.8 %copy-done.5 = bf16[9,16,64]{2,1,0:T(8,128)(2,1)S(1)} copy-done((bf16[9,16,64]{2,1,0:T(8,128)(2,1)S(1)}, bf16[9,16,64]{2,1,0:T(8,128)(2,1)}, u32[]{:S(2)}) %copy-start.5) | copy-done | bytes 18456
  16.8 0.7 %copy-done.10 = f32[64]{0:T(128)S(1)} copy-done((f32[64]{0:T(128)S(1)}, f32[64]{0:T(128)}, u32[]{:S(2)}) %copy-start.10) | copy-done | bytes 280
  18.7 1.3 %weights.1 = (bf16[10,256,256]{2,1,0:T(8,128)(2,1)S(1)}, bf16[512,768]{1,0:T(8,128)(2,1)S(1)}, bf16[512,256]{1,0:T(8,128)(2,1)S(1)}, bf16[512,256]{1,0:T(8,128)(...) custom-call(bf16[9,64,2]{2,1,0:T(8,128)(2,1)S(1)} %copy.16.w1_hbm, ...), custom_call_target="tpu_custom_call" | custom-call | flops 10000000 | bytes 1048576 | tf_op jit(solution)/shard_map/weights/pallas_call | solution.py:421
  20.1 4.4 %advance.1.refs_0_.refs_5_ = f32[64,256]{1,0:T(8,128)S(1)} custom-call(f32[32,256]{1,0:T(8,128)S(1)} %get-tuple-element.15.u_ref, f32[32,256]{1,0:T(8,128)S(1)} %get-tuple-element.16.v_ref, f32[8,256]{1,0:T(8,128)S(1)} %collective-permute-done.bot_ref, f32[8,256]{1,0:T(8,128)S(1)} %collective-permute-done.1.top_ref, ...), custom_call_target="tpu_custom_call" | custom-call | flops 1000000000 | bytes 1048576 | tf_op jit(solution)/shard_map/advance/pallas_call | solution.py:446
  24.6 3.0 %collective-permute-start.6 = (f32[64,256]{1,0:T(8,128)S(1)}, f32[64,256]{1,0:T(8,128)S(1)}, u32[]{:S(2)}, u32[]{:S(2)}) collective-permute-start(f32[64,256]{1,0:T(8,128)S(1)} %advance.1.refs_0_.refs_5_), channel_id=1, source_target_pairs={{0,3},{1,2},{2,1},{3,0},{4,7},{5,6},{6,5},{7,4},{8,11},{9,10},{10,... | collective-permute-start | bytes 196616 | tf_op jit(solution)/shard_map/ppermute | solution.py:382
  28.2 1.6 %collective-permute-done.6.refs_3_ = f32[64,256]{1,0:T(8,128)S(1)} collective-permute-done((f32[64,256]{1,0:T(8,128)S(1)}, f32[64,256]{1,0:T(8,128)S(1)}, u32[]{:S(2)}, u32[]{:S(2)}) %collective-permute-start.6) | collective-permute-done | bytes 65568 | tf_op jit(solution)/shard_map/ppermute | solution.py:382
  29.8 2.0 %collective-permute-done.5.refs_2_ = f32[64,256]{1,0:T(8,128)S(1)} collective-permute-done((f32[64,256]{1,0:T(8,128)S(1)}, f32[64,256]{1,0:T(8,128)S(1)}, u32[]{:S(2)}, u32[]{:S(2)}) %collective-permute-start.5) | collective-permute-done | bytes 65568 | tf_op jit(solution)/shard_map/ppermute | solution.py:382
  32.7 4.3 %collective-permute-start.8 = (f32[64,256]{1,0:T(8,128)S(1)}, f32[64,256]{1,0:T(8,128)S(1)}, u32[]{:S(2)}, u32[]{:S(2)}) collective-permute-start(f32[64,256]{1,0:T(8,128)S(1)} %shard_map.149.refs_0_), channel_id=1, source_target_pairs={{0,8},{4,12},{8,0},{12,4},{16,24},{20,28},{24,16},{28,20},{1,9},{5... | collective-permute-start | bytes 196616 | tf_op jit(solution)/shard_map/ppermute | solution.py:382
  37.0 1.7 %collective-permute-done.12.refs_6_ = f32[64,256]{1,0:T(8,128)S(1)} collective-permute-done((f32[64,256]{1,0:T(8,128)S(1)}, f32[64,256]{1,0:T(8,128)S(1)}, u32[]{:S(2)}, u32[]{:S(2)}) %collective-permute-start.12) | collective-permute-done | bytes 65568 | tf_op jit(solution)/shard_map/ppermute | solution.py:382
  40.6 1.4 %shard_map.150.refs_0_ = f32[64,256]{1,0:T(8,128)S(1)} custom-call(f32[64,256]{1,0:T(8,128)S(1)} %shard_map.149.refs_0_, f32[64,256]{1,0:T(8,128)S(1)} %collective-permute-done.7.refs_1_, f32[64,256]{1,0:T(8,128)S(1)} %collective-permute-done.8.refs_2_, f32[64,256]{1,0:T(8,128)S(1)} %collective-permute-done.9.refs_3_, ...), custom_call_target="tpu_custom_call" | custom-call | flops 10000000 | bytes 1048576 | tf_op jit(solution)/shard_map/pallas_call | solution.py:462
  42.0 1.0 %collective-permute-start.16 = (f32[64,256]{1,0:T(8,128)S(1)}, f32[64,256]{1,0:T(8,128)S(1)}, u32[]{:S(2)}, u32[]{:S(2)}) collective-permute-start(f32[64,256]{1,0:T(8,128)S(1)} %shard_map.150.refs_0_), channel_id=1, source_target_pairs={{0,3},{1,2},{2,1},{3,0},{4,7},{5,6},{6,5},{7,4},{8,11},{9,10},{10,... | collective-permute-start | bytes 196616 | tf_op jit(solution)/shard_map/ppermute | solution.py:382
  43.1 0.8 %collective-permute-start.15 = (f32[64,256]{1,0:T(8,128)S(1)}, f32[64,256]{1,0:T(8,128)S(1)}, u32[]{:S(2)}, u32[]{:S(2)}) collective-permute-start(f32[64,256]{1,0:T(8,128)S(1)} %shard_map.150.refs_0_), channel_id=1, source_target_pairs={{0,2},{1,3},{2,0},{3,1},{4,6},{5,7},{6,4},{7,5},{8,10},{9,11},{10,... | collective-permute-start | bytes 196616 | tf_op jit(solution)/shard_map/ppermute | solution.py:382
  43.8 1.7 %collective-permute-start.14 = (f32[64,256]{1,0:T(8,128)S(1)}, f32[64,256]{1,0:T(8,128)S(1)}, u32[]{:S(2)}, u32[]{:S(2)}) collective-permute-start(f32[64,256]{1,0:T(8,128)S(1)} %shard_map.150.refs_0_), channel_id=1, source_target_pairs={{0,1},{1,0},{2,3},{3,2},{4,5},{5,4},{6,7},{7,6},{8,9},{9,8},{10,11... | collective-permute-start | bytes 196616 | tf_op jit(solution)/shard_map/ppermute | solution.py:382
  45.6 2.0 %collective-permute-done.16.refs_3_ = f32[64,256]{1,0:T(8,128)S(1)} collective-permute-done((f32[64,256]{1,0:T(8,128)S(1)}, f32[64,256]{1,0:T(8,128)S(1)}, u32[]{:S(2)}, u32[]{:S(2)}) %collective-permute-start.16) | collective-permute-done | bytes 65568 | tf_op jit(solution)/shard_map/ppermute | solution.py:382
  47.6 0.7 %collective-permute-done.15.refs_2_ = f32[64,256]{1,0:T(8,128)S(1)} collective-permute-done((f32[64,256]{1,0:T(8,128)S(1)}, f32[64,256]{1,0:T(8,128)S(1)}, u32[]{:S(2)}, u32[]{:S(2)}) %collective-permute-start.15) | collective-permute-done | bytes 65568 | tf_op jit(solution)/shard_map/ppermute | solution.py:382
  48.6 0.7 %shard_map.151 = (f32[32,256]{1,0:T(8,128)}, f32[32,256]{1,0:T(8,128)}) custom-call(f32[64,256]{1,0:T(8,128)S(1)} %shard_map.150.refs_0_, f32[64,256]{1,0:T(8,128)S(1)} %collective-permute-done.14.refs_1_, f32[64,256]{1,0:T(8,128)S(1)} %collective-permute-done.15.refs_2_, f32[64,256]{1,0:T(8,128)S(1)} %collective-permute-done.16.refs_3_, ...), custom_call_target="tpu_custom_call" | custom-call | flops 10000000 | bytes 1048576 | tf_op jit(solution)/shard_map/pallas_call | solution.py:468
  (44 shorter events, 5.3 us)
Async XLA Ops:
  2.2 5.9 %collective-permute-start = (f32[8,256]{1,0:T(8,128)S(1)}, f32[8,256]{1,0:T(8,128)S(1)}, u32[]{:S(2)}, u32[]{:S(2)}) collective-permute-start(f32[8,256]{1,0:T(8,128)S(1)} %get-tuple-element.17), channel_id=1, source_target_pairs={{0,28},{4,0},{8,4},{12,8},{16,12},{20,16},{24,20},{28,24},{1,29},{... | collective-permute-start | bytes 24584 | tf_op jit(solution)/shard_map/surroundings/ppermute | solution.py:405
  6.8 4.9 %collective-permute-start.1 = (f32[8,256]{1,0:T(8,128)S(1)}, f32[8,256]{1,0:T(8,128)S(1)}, u32[]{:S(2)}, u32[]{:S(2)}) collective-permute-start(f32[8,256]{1,0:T(8,128)S(1)} %get-tuple-element.18), channel_id=1, source_target_pairs={{0,4},{4,8},{8,12},{12,16},{16,20},{20,24},{24,28},{28,0},{1,5},{5... | collective-permute-start | bytes 24584 | tf_op jit(solution)/shard_map/surroundings/ppermute | solution.py:405
  11.7 8.3 %collective-permute-start.2 = (f32[8,128]{1,0:T(8,128)S(1)}, f32[8,128]{1,0:T(8,128)S(1)}, u32[]{:S(2)}, u32[]{:S(2)}) collective-permute-start(f32[8,128]{1,0:T(8,128)S(1)} %get-tuple-element.19), channel_id=1, source_target_pairs={{0,3},{1,0},{2,1},{3,2},{4,7},{5,4},{6,5},{7,6},{8,11},{9,8},{10,9... | collective-permute-start | bytes 12296 | tf_op jit(solution)/shard_map/surroundings/ppermute | solution.py:405
  14.2 5.8 %collective-permute-start.3 = (f32[8,128]{1,0:T(8,128)S(1)}, f32[8,128]{1,0:T(8,128)S(1)}, u32[]{:S(2)}, u32[]{:S(2)}) collective-permute-start(f32[8,128]{1,0:T(8,128)S(1)} %get-tuple-element.20), channel_id=1, source_target_pairs={{0,1},{1,2},{2,3},{3,0},{4,5},{5,6},{6,7},{7,4},{8,9},{9,10},{10,1... | collective-permute-start | bytes 12296 | tf_op jit(solution)/shard_map/surroundings/ppermute | solution.py:405
  15.1 0.9 %copy-start.4 = (bf16[9,64,64]{2,1,0:T(8,128)(2,1)S(1)}, bf16[9,64,64]{2,1,0:T(8,128)(2,1)}, u32[]{:S(2)}) copy-start(bf16[9,64,64]{2,1,0:T(8,128)(2,1)} %w2_hbm.1) | copy-start | bytes 221188
  20.1 12.2 %copy-start = (bf16[256,512]{1,0:T(8,128)(2,1)S(1)}, bf16[256,512]{1,0:T(8,128)(2,1)}, u32[]{:S(2)}) copy-start(bf16[256,512]{1,0:T(8,128)(2,1)} %constant.13.clone.refs_6_.refs_11_) | copy-start | bytes 786436
  20.1 12.2 %copy-start.1 = (bf16[256,512]{1,0:T(8,128)(2,1)S(1)}, bf16[256,512]{1,0:T(8,128)(2,1)}, u32[]{:S(2)}) copy-start(bf16[256,512]{1,0:T(8,128)(2,1)} %constant.12.clone.refs_5_.refs_10_) | copy-start | bytes 786436
  20.1 12.2 %copy-start.6 = (f32[4,8,256]{2,1,0:T(8,128)S(1)}, f32[4,8,256]{2,1,0:T(8,128)}, u32[]{:S(2)}) copy-start(f32[4,8,256]{2,1,0:T(8,128)} %constant.16.clone.refs_4_) | copy-start | bytes 98308
  20.1 20.5 %copy-start.2 = (bf16[512,256]{1,0:T(8,128)(2,1)S(1)}, bf16[512,256]{1,0:T(8,128)(2,1)}, u32[]{:S(2)}) copy-start(bf16[512,256]{1,0:T(8,128)(2,1)} %constant.15.clone.refs_9_) | copy-start | bytes 786436
  20.1 20.5 %copy-start.3 = (bf16[512,256]{1,0:T(8,128)(2,1)S(1)}, bf16[512,256]{1,0:T(8,128)(2,1)}, u32[]{:S(2)}) copy-start(bf16[512,256]{1,0:T(8,128)(2,1)} %constant.14.clone.refs_8_) | copy-start | bytes 786436
  24.6 24.1 %copy-start.9 = (f32[4,8,256]{2,1,0:T(8,128)S(1)}, f32[4,8,256]{2,1,0:T(8,128)}, u32[]{:S(2)}) copy-start(f32[4,8,256]{2,1,0:T(8,128)} %constant.17.clone.refs_4_) | copy-start | bytes 98308
  24.6 5.2 %collective-permute-start.6 = (f32[64,256]{1,0:T(8,128)S(1)}, f32[64,256]{1,0:T(8,128)S(1)}, u32[]{:S(2)}, u32[]{:S(2)}) collective-permute-start(f32[64,256]{1,0:T(8,128)S(1)} %advance.1.refs_0_.refs_5_), channel_id=1, source_target_pairs={{0,3},{1,2},{2,1},{3,0},{4,7},{5,6},{6,5},{7,4},{8,11},{9,10},{10,... | collective-permute-start | bytes 196616 | tf_op jit(solution)/shard_map/ppermute | solution.py:382
  27.5 4.3 %collective-permute-start.5 = (f32[64,256]{1,0:T(8,128)S(1)}, f32[64,256]{1,0:T(8,128)S(1)}, u32[]{:S(2)}, u32[]{:S(2)}) collective-permute-start(f32[64,256]{1,0:T(8,128)S(1)} %advance.1.refs_0_.refs_5_), channel_id=1, source_target_pairs={{0,2},{1,3},{2,0},{3,1},{4,6},{5,7},{6,4},{7,5},{8,10},{9,11},{10,... | collective-permute-start | bytes 196616 | tf_op jit(solution)/shard_map/ppermute | solution.py:382
  28.0 4.3 %collective-permute-start.4 = (f32[64,256]{1,0:T(8,128)S(1)}, f32[64,256]{1,0:T(8,128)S(1)}, u32[]{:S(2)}, u32[]{:S(2)}) collective-permute-start(f32[64,256]{1,0:T(8,128)S(1)} %advance.1.refs_0_.refs_5_), channel_id=1, source_target_pairs={{0,1},{1,0},{2,3},{3,2},{4,5},{5,4},{6,7},{7,6},{8,9},{9,8},{10,11... | collective-permute-start | bytes 196616 | tf_op jit(solution)/shard_map/ppermute | solution.py:382
  32.6 6.1 %collective-permute-start.12 = (f32[64,256]{1,0:T(8,128)S(1)}, f32[64,256]{1,0:T(8,128)S(1)}, u32[]{:S(2)}, u32[]{:S(2)}) collective-permute-start(f32[64,256]{1,0:T(8,128)S(1)} %shard_map.149.refs_0_), channel_id=1, source_target_pairs={{0,24},{4,28},{8,16},{12,20},{16,8},{20,12},{24,0},{28,4},{1,25},{... | collective-permute-start | bytes 196616 | tf_op jit(solution)/shard_map/ppermute | solution.py:382
  32.6 6.1 %collective-permute-start.10 = (f32[64,256]{1,0:T(8,128)S(1)}, f32[64,256]{1,0:T(8,128)S(1)}, u32[]{:S(2)}, u32[]{:S(2)}) collective-permute-start(f32[64,256]{1,0:T(8,128)S(1)} %shard_map.149.refs_0_), channel_id=1, source_target_pairs={{0,16},{4,20},{8,24},{12,28},{16,0},{20,4},{24,8},{28,12},{1,17},{... | collective-permute-start | bytes 196616 | tf_op jit(solution)/shard_map/ppermute | solution.py:382
  32.7 6.7 %collective-permute-start.8 = (f32[64,256]{1,0:T(8,128)S(1)}, f32[64,256]{1,0:T(8,128)S(1)}, u32[]{:S(2)}, u32[]{:S(2)}) collective-permute-start(f32[64,256]{1,0:T(8,128)S(1)} %shard_map.149.refs_0_), channel_id=1, source_target_pairs={{0,8},{4,12},{8,0},{12,4},{16,24},{20,28},{24,16},{28,20},{1,9},{5... | collective-permute-start | bytes 196616 | tf_op jit(solution)/shard_map/ppermute | solution.py:382
  37.0 2.4 %collective-permute-start.7 = (f32[64,256]{1,0:T(8,128)S(1)}, f32[64,256]{1,0:T(8,128)S(1)}, u32[]{:S(2)}, u32[]{:S(2)}) collective-permute-start(f32[64,256]{1,0:T(8,128)S(1)} %shard_map.149.refs_0_), channel_id=1, source_target_pairs={{0,4},{4,0},{8,12},{12,8},{16,20},{20,16},{24,28},{28,24},{1,5},{5... | collective-permute-start | bytes 196616 | tf_op jit(solution)/shard_map/ppermute | solution.py:382
  38.7 1.3 %collective-permute-start.13 = (f32[64,256]{1,0:T(8,128)S(1)}, f32[64,256]{1,0:T(8,128)S(1)}, u32[]{:S(2)}, u32[]{:S(2)}) collective-permute-start(f32[64,256]{1,0:T(8,128)S(1)} %collective-permute-done.12.refs_6_), channel_id=1, source_target_pairs={{0,4},{4,0},{8,12},{12,8},{16,20},{20,16},{24,28},{28,24},{1,5},{5... | collective-permute-start | bytes 196616 | tf_op jit(solution)/shard_map/ppermute | solution.py:382
  38.7 1.4 %collective-permute-start.11 = (f32[64,256]{1,0:T(8,128)S(1)}, f32[64,256]{1,0:T(8,128)S(1)}, u32[]{:S(2)}, u32[]{:S(2)}) collective-permute-start(f32[64,256]{1,0:T(8,128)S(1)} %collective-permute-done.10.refs_4_), channel_id=1, source_target_pairs={{0,4},{4,0},{8,12},{12,8},{16,20},{20,16},{24,28},{28,24},{1,5},{5... | collective-permute-start | bytes 196616 | tf_op jit(solution)/shard_map/ppermute | solution.py:382
  39.4 1.3 %collective-permute-start.9 = (f32[64,256]{1,0:T(8,128)S(1)}, f32[64,256]{1,0:T(8,128)S(1)}, u32[]{:S(2)}, u32[]{:S(2)}) collective-permute-start(f32[64,256]{1,0:T(8,128)S(1)} %collective-permute-done.8.refs_2_), channel_id=1, source_target_pairs={{0,4},{4,0},{8,12},{12,8},{16,20},{20,16},{24,28},{28,24},{1,5},{5... | collective-permute-start | bytes 196616 | tf_op jit(solution)/shard_map/ppermute | solution.py:382
  42.0 5.6 %collective-permute-start.16 = (f32[64,256]{1,0:T(8,128)S(1)}, f32[64,256]{1,0:T(8,128)S(1)}, u32[]{:S(2)}, u32[]{:S(2)}) collective-permute-start(f32[64,256]{1,0:T(8,128)S(1)} %shard_map.150.refs_0_), channel_id=1, source_target_pairs={{0,3},{1,2},{2,1},{3,0},{4,7},{5,6},{6,5},{7,4},{8,11},{9,10},{10,... | collective-permute-start | bytes 196616 | tf_op jit(solution)/shard_map/ppermute | solution.py:382
  43.1 5.3 %collective-permute-start.15 = (f32[64,256]{1,0:T(8,128)S(1)}, f32[64,256]{1,0:T(8,128)S(1)}, u32[]{:S(2)}, u32[]{:S(2)}) collective-permute-start(f32[64,256]{1,0:T(8,128)S(1)} %shard_map.150.refs_0_), channel_id=1, source_target_pairs={{0,2},{1,3},{2,0},{3,1},{4,6},{5,7},{6,4},{7,5},{8,10},{9,11},{10,... | collective-permute-start | bytes 196616 | tf_op jit(solution)/shard_map/ppermute | solution.py:382
  43.8 4.8 %collective-permute-start.14 = (f32[64,256]{1,0:T(8,128)S(1)}, f32[64,256]{1,0:T(8,128)S(1)}, u32[]{:S(2)}, u32[]{:S(2)}) collective-permute-start(f32[64,256]{1,0:T(8,128)S(1)} %shard_map.150.refs_0_), channel_id=1, source_target_pairs={{0,1},{1,0},{2,3},{3,2},{4,5},{5,4},{6,7},{7,6},{8,9},{9,8},{10,11... | collective-permute-start | bytes 196616 | tf_op jit(solution)/shard_map/ppermute | solution.py:382
  (6 other events, 4.3 us)
where the time goes:
time: 49.7 us; the launch traced here: 49.3 us
  starting transfers between devices  19.2 us (39%)
  waiting for transfers between devices  15.1 us (30%)
  Pallas kernels  8.14 us (16%)
  local copies, waits for them, and re-layouts  6.03 us (12%)
  between operations  0.79 us (2%)
    ppermute x13, starting transfers between devices, partner(): lax.ppermute(block, axis, [(i, i ^ k) for i in range(lax.axis_size(axis))])  12.1 us
    ppermute x13, waiting for transfers between devices, partner(): lax.ppermute(block, axis, [(i, i ^ k) for i in range(lax.axis_size(axis))])  10.3 us
    ppermute x4, starting transfers between devices, shifted(): lax.ppermute(value, axis, [(i, (i + distance) % peers) for i in range(pee...  7.05 us
    unnamed x27, local copies, waits for them, and re-layouts  6.03 us
    ppermute x4, waiting for transfers between devices, shifted(): lax.ppermute(value, axis, [(i, (i + distance) % peers) for i in range(pee...  4.88 us
    pallas_call x1, Pallas kernels, on_device(): call(advance_kernel, block, (pltpu.VMEM((2, rows + 16, breadth + 128), f3...  4.42 us
    pallas_call x1, Pallas kernels, on_device(): call(functools.partial(row_kernel, scale=1.0 / (grid_x * grid_y)), block,...  1.37 us
    pallas_call x1, Pallas kernels, on_device(): call(functools.partial(weights_kernel, rows=rows), (shape((groups, -(-6 *...  1.31 us
  transfers between devices with their start and end apart: 17, of which 13 were waited for; matrix products, arithmetic and copies ran while one was open for 2% of the time, Pallas kernels for 3%

commit v1 on v0

--- a/solution.py
+++ b/solution.py
@@ -50,61 +50,41 @@
     return jnp.concatenate([value[half:], value[:half]], axis=0)
 
 
-def fetch(sources, targets, sems):
-    copies = [pltpu.make_async_copy(a, b, sems.at[i]) for i, (a, b) in enumerate(zip(sources, targets))]
-    for copy in copies:
-        copy.start()
-    for copy in copies:
-        copy.wait()
-
-
-def rows_kernel(u_hbm, v_hbm, last_ref, first_ref, u_ref, v_ref, sems):
-    fetch((u_hbm, v_hbm), (u_ref, v_ref), sems)
-    height = u_ref.shape[0]
-    for q, ref in enumerate((u_ref, v_ref)):
-        last_ref[4 * q : 4 * q + 4, :] = ref[height - 4 : height, :]
-        first_ref[4 * q : 4 * q + 4, :] = ref[0:4, :]
-
-
-def columns_kernel(u_ref, v_ref, bot_ref, top_ref, last_ref, first_ref, strip):
-    height, breadth = u_ref.shape
+def rows_kernel(both_ref, last_ref, first_ref):
+    height = both_ref.shape[0] // 2
+    for q in range(2):
+        last_ref[4 * q : 4 * q + 4, :] = both_ref[height * (q + 1) - 4 : height * (q + 1), :]
+        first_ref[4 * q : 4 * q + 4, :] = both_ref[height * q : height * q + 4, :]
+
+
+def columns_kernel(both_ref, bot_ref, top_ref, order_ref, last_ref, first_ref, strip):
+    height, breadth = both_ref.shape[0] // 2, both_ref.shape[1]
     rows = height + 8
     for side, out in ((0, first_ref), (breadth - 128, last_ref)):
         strip[...] = jnp.zeros_like(strip)
-        for q, ref in enumerate((u_ref, v_ref)):
+        for q in range(2):
             start = rows * q
-            strip[start : start + height, :] = ref[:, side : side + 128]
+            strip[start : start + height, :] = both_ref[height * q : height * (q + 1), side : side + 128]
             strip[start + height : start + height + 4, :] = bot_ref[4 * q : 4 * q + 4, side : side + 128]
             strip[start + height + 4 : start + rows, :] = top_ref[4 * q : 4 * q + 4, side : side + 128]
         turned = strip[...].T
         out[...] = turned[0:8] if side == 0 else turned[120:128]
 
 
-def weights_kernel(
-    w1_hbm, w2_hbm, w3_hbm, b1_hbm, b2_hbm, b3_hbm, k1_ref, k2_ref, even_ref, odd_ref, c1_ref, c2_ref, c3_ref,
-    w1_ref, w2_ref, w3_ref, b1_ref, b2_ref, b3_ref, sems, *, rows
-):
-    fetch(
-        (w1_hbm, w2_hbm, w3_hbm, b1_hbm, b2_hbm, b3_hbm), (w1_ref, w2_ref, w3_ref, b1_ref, b2_ref, b3_ref), sems
-    )
+def first_weights_kernel(packed_ref, k1_ref, c1_ref, c2_ref, c3_ref, *, rows):
     groups, depth, _ = k1_ref.shape
-    c1_ref[...] = jnp.concatenate([b1_ref[...]] * 4, axis=1)
-    c2_ref[...] = jnp.concatenate([b2_ref[...]] * 4, axis=1)
-    place = lax.broadcasted_iota(jnp.int32, (64, 16), 0) // 4
+    packed = packed_ref[...]
+    wide = jnp.concatenate([packed] * 4, axis=1)
+    c1_ref[...] = wide[18:19]
+    c2_ref[...] = wide[19:20]
+    place = lax.broadcasted_iota(jnp.int32, (64, 64), 0) // 4
     channel = 8 * (place // 8) + 4 * (place % 2) + (place // 2) % 4
-    hit = channel == lax.broadcasted_iota(jnp.int32, (64, 16), 1)
-    c3_ref[...] = jnp.sum(jnp.where(hit, b3_ref[...], 0.0), axis=1, keepdims=True)
-
-    pick = lax.broadcasted_iota(jnp.int32, (8, 2), 0) == lax.broadcasted_iota(jnp.int32, (8, 2), 1)
-    pick = jnp.where(pick, 1.0, 0.0).astype(bf16)
-    turned = [
-        lax.dot_general(pick, w1_ref[tap], (((1,), (1,)), ((), ())), preferred_element_type=f32) for tap in range(9)
-    ]
-    turned = [jnp.concatenate([tap] * 4, axis=1) for tap in turned]
+    hit = channel == lax.broadcasted_iota(jnp.int32, (64, 64), 1)
+    c3_ref[...] = jnp.sum(jnp.where(hit, packed[20:21], 0.0), axis=1, keepdims=True)
     spread = []
     for d in range(3):
         parts = [
-            jnp.broadcast_to(turned[3 * d + s][q : q + 1, :], (rows, 256))
+            jnp.broadcast_to(wide[(3 * d + s) * 2 + q : (3 * d + s) * 2 + q + 1, :], (rows, 256))
             for s in range(3)
             for q in range(2)
         ]
@@ -118,11 +98,13 @@
         block = jnp.where(near[0], spread[0], jnp.where(near[1], spread[1], jnp.where(near[2], spread[2], 0.0)))
         k1_ref[r] = block.astype(bf16)
 
+
+def other_weights_kernel(packed_ref, k2_ref, even_ref, odd_ref):
     k2_ref[...] = jnp.zeros(k2_ref.shape, bf16)
     slots = {-1: 5, 0: 0, 1: 1, 2: 2, 3: 3, 4: 6}
     blank = jnp.zeros((64, 64), f32)
     for c in range(3):
-        taps = [w2_ref[3 * d + c].astype(f32) for d in range(3)]
+        taps = [packed_ref[64 * (3 * d + c) : 64 * (3 * d + c) + 64, :].astype(f32) for d in range(3)]
         two = [(taps[0], blank), (taps[1], taps[0]), (taps[2], taps[1]), (blank, taps[2])]
         two = [jnp.concatenate(pair, axis=0).T.astype(bf16) for pair in two]
         for h in range(2):
@@ -130,7 +112,10 @@
                 slot = slots[d + 2 * h - 1]
                 k2_ref[64 * slot : 64 * slot + 64, 256 * c + 128 * h : 256 * c + 128 * h + 128] = two[d]
 
-    taps = [[w3_ref[3 * d + c].astype(f32) for d in range(3)] for c in range(3)]
+    taps = [
+        [packed_ref[576 + 16 * (3 * d + c) : 592 + 16 * (3 * d + c), :].astype(f32) for d in range(3)]
+        for c in range(3)
+    ]
     blank = jnp.zeros((16, 64), f32)
     filler = jnp.zeros((64, 256), bf16)
     parts = [filler] * 8
@@ -155,10 +140,10 @@
 
 
 def advance_kernel(
-    u_ref, v_ref, bot_ref, top_ref, right_ref, left_ref, w1_ref, w2_ref, w3e_ref, w3o_ref,
+    both_ref, bot_ref, top_ref, right_ref, left_ref, w1_ref, w2_ref, w3e_ref, w3o_ref,
     b1_ref, b2_ref, b3_ref, star_ref, field, first, second, coeff, strip,
 ):
-    height, breadth = u_ref.shape
+    height, breadth = both_ref.shape[0] // 2, both_ref.shape[1]
     rows = height + 8
     groups = rows // 4
     lanes = breadth + 128
@@ -166,8 +151,8 @@
     strip[0:4, :] = right_ref[0:4, :]
     strip[124:128, :] = left_ref[4:8, :]
     beside = strip[...].T
-    for q, ref in enumerate((u_ref, v_ref)):
-        field[q, 8 : 8 + height, :breadth] = ref[...]
+    for q in range(2):
+        field[q, 8 : 8 + height, :breadth] = both_ref[height * q : height * (q + 1), :]
         field[q, 8 + height : 12 + height, :breadth] = bot_ref[4 * q : 4 * q + 4, :]
         field[q, 12 + height : 16 + height, :breadth] = top_ref[4 * q : 4 * q + 4, :]
         field[q, 8 : 8 + rows, breadth:] = beside[rows * q : rows * q + rows]
@@ -345,15 +330,13 @@
     v_ref[...] = result[rows // 2 :]
 
 
-def call(kernel, shapes, scratch=(), flops=10**7, outside=0):
-    specs = {"in_specs": [pl.BlockSpec(memory_space=pltpu.HBM)] * outside} if outside else {}
+def call(kernel, shapes, scratch=(), flops=10**7):
     return pl.pallas_call(
         kernel,
         out_shape=shapes,
         scratch_shapes=list(scratch),
         compiler_params=pltpu.CompilerParams(vmem_limit_bytes=vmem_limit),
         cost_estimate=pl.CostEstimate(flops=flops, bytes_accessed=2**20, transcendentals=0),
-        **specs,
     )
 
 
@@ -404,42 +387,38 @@
         peers = lax.axis_size(axis)
         return lax.ppermute(value, axis, [(i, (i + distance) % peers) for i in range(peers)])
 
-    with jax.named_scope("surroundings"):
+    with jax.named_scope("rows_around"):
+        component = lax.broadcasted_iota(jnp.int32, (2, height, breadth), 0)
+        both = jnp.where(component == 0, u_field[None], v_field[None]).reshape(2 * height, breadth)
         edge = shape((8, breadth), f32)
-        block = shape((height, breadth), f32)
-        last, first, u_field, v_field = call(
-            rows_kernel, (edge, edge, block, block), (pltpu.SemaphoreType.DMA((2,)),), outside=2
-        )(u_field, v_field)
+        last, first = call(rows_kernel, (edge, edge))(both)
         top, bottom = shifted(last, "gx", 1), shifted(first, "gx", -1)
-        edge = shape((8, 128), f32)
-        last, first = call(columns_kernel, (edge, edge), (pltpu.VMEM((128, 128), f32),))(
-            u_field, v_field, bottom, top
-        )
-        left, right = shifted(last, "gy", 1), shifted(first, "gy", -1)
 
     with jax.named_scope("weights"):
-        weights = call(
-            functools.partial(weights_kernel, rows=rows),
+        biases = jnp.stack([b_first, b_second, jnp.pad(b_third, (0, 64 - b_third.shape[0]))])
+        packed = jnp.concatenate([w_first.transpose(0, 2, 1).reshape(18, 64).astype(f32), biases], axis=0)
+        kernel_1, *biases = call(
+            functools.partial(first_weights_kernel, rows=rows),
             (
                 shape((groups, -(-6 * rows // 128) * 128, 256), bf16),
-                shape((512, 768), bf16),
-                shape((512, 256), bf16),
-                shape((512, 256), bf16),
                 shape((1, 256), f32),
                 shape((1, 256), f32),
                 shape((64, 1), f32),
             ),
-            (
-                pltpu.VMEM(w_first.shape, bf16),
-                pltpu.VMEM(w_second.shape, bf16),
-                pltpu.VMEM(w_third.shape, bf16),
-                pltpu.VMEM((1, 64), f32),
-                pltpu.VMEM((1, 64), f32),
-                pltpu.VMEM((1, 16), f32),
-                pltpu.SemaphoreType.DMA((6,)),
-            ),
-            outside=6,
-        )(w_first, w_second, w_third, b_first[None], b_second[None], b_third[None])
+        )(packed)
+
+    with jax.named_scope("columns_around"):
+        edge = shape((8, 128), f32)
+        last, first = call(columns_kernel, (edge, edge), (pltpu.VMEM((128, 128), f32),))(
+            both, bottom, top, biases[2]
+        )
+        left, right = shifted(last, "gy", 1), shifted(first, "gy", -1)
+
+    with jax.named_scope("weights"):
+        packed = jnp.concatenate([w_second.reshape(576, 64), w_third.reshape(144, 64)], axis=0)
+        others = call(
+            other_weights_kernel, (shape((512, 768), bf16), shape((512, 256), bf16), shape((512, 256), bf16))
+        )(packed)
 
     block = shape((2 * height, breadth), f32)
     with jax.named_scope("advance"):
@@ -454,7 +433,7 @@
                 pltpu.VMEM((128, 128), f32),
             ),
             flops=10**9,
-        )(u_field, v_field, bottom, top, right, left, *weights)
+        )(both, bottom, top, right, left, kernel_1, *others, *biases)
 
     column, row, twiddle_out, twiddle_home = tables(height, breadth, members_x, members_y)
     column, row = [[jnp.asarray(t) for t in pair] for pair in (column, row)]

time: 49.7 us -> 46.9 us (0.944)
  local copies, waits for them, and re-layouts: 6.03 us -> 0.86 us
  other arithmetic: 0 us -> 3.2 us
  Pallas kernels: 8.14 us -> 7.58 us
    unnamed x27 -> x12, local copies, waits for them, and re-layouts: 6.03 us -> 0.03 us
    concatenate x0 -> x2, other arithmetic: none -> 1.65 us  [the longest x1 0.97 us: on_device(): jnp.concatenate([w_second.reshape(576, 64), w_third.reshape(144, 64)], ax...]
    select_n x0 -> x1, other arithmetic: none -> 0.85 us  [on_device(): jnp.where(component == 0, u_field[None], v_field[None])]
    convert_element_type x0 -> x1, other arithmetic: none -> 0.69 us  [on_device(): w_first.transpose(0, 2, 1).reshape(18, 64).astype(f32)]
    ppermute x4, waiting for transfers between devices: 4.88 us -> 5.55 us  [shifted(): lax.ppermute(value, axis, [(i, (i + distance) % peers) for i in range(pee...]
    another operation x0 -> x1, local copies, waits for them, and re-layouts: none -> 0.66 us  [on_device(): jnp.stack([b_first, b_second, jnp.pad(b_third, (0, 64 - b_third.shape[0]))])]
    ppermute x13, waiting for transfers between devices: 10.3 us -> 9.61 us  [partner(): lax.ppermute(block, axis, [(i, i ^ k) for i in range(lax.axis_size(axis))])]
    pallas_call x2 -> x3, Pallas kernels: 1.38 us -> 0.78 us  [the longest x1 0.46 us: on_device(): call(other_weights_kernel, (shape((512, 768), bf16), shape((512, 256), bf...]
  transfers between devices with their start and end apart: 17 -> 17, of which waited for: 13 -> 12; matrix products, arithmetic and copies ran while one was open for 2% -> 6% of each run, Pallas kernels for 3% -> 2%
where the time goes in v1:
time: 46.9 us; the launch traced here: 46.7 us
  starting transfers between devices  19.1 us (41%)
  waiting for transfers between devices  15.2 us (32%)
  Pallas kernels  7.58 us (16%)
  other arithmetic  3.2 us (7%)
  local copies, waits for them, and re-layouts  0.86 us (2%)
  between operations  0.76 us (2%)
    ppermute x13, starting transfers between devices, partner(): lax.ppermute(block, axis, [(i, i ^ k) for i in range(lax.axis_size(axis))])  12.1 us
    ppermute x13, waiting for transfers between devices, partner(): lax.ppermute(block, axis, [(i, i ^ k) for i in range(lax.axis_size(axis))])  9.61 us
    ppermute x4, starting transfers between devices, shifted(): lax.ppermute(value, axis, [(i, (i + distance) % peers) for i in range(pee...  7.05 us
    ppermute x4, waiting for transfers between devices, shifted(): lax.ppermute(value, axis, [(i, (i + distance) % peers) for i in range(pee...  5.55 us
    pallas_call x1, Pallas kernels, on_device(): call(advance_kernel, block, (pltpu.VMEM((2, rows + 16, breadth + 128), f3...  4.46 us
    pallas_call x1, Pallas kernels, on_device(): call(functools.partial(row_kernel, scale=1.0 / (grid_x * grid_y)), block,...  1.37 us
    concatenate x1, other arithmetic, on_device(): jnp.concatenate([w_second.reshape(576, 64), w_third.reshape(144, 64)], ax...  0.97 us
  transfers between devices with their start and end apart: 17, of which 12 were waited for; matrix products, arithmetic and copies ran while one was open for 6% of the time, Pallas kernels for 2%

profile of v1, /device:TPU:0, one launch (start us, length us, event | category | flops | bytes accessed | tf_op | source)
XLA Modules:
  0.0 46.7 jit_solution(10175935820151979691)
XLA Ops:
  0.8 0.8 %bitcast_select_fusion.both_ref = f32[64,256]{1,0:T(8,128)S(1)} fusion(f32[32,256]{1,0:T(8,128)} %param.15, f32[32,256]{1,0:T(8,128)} %param.14, pred[64]{0:T(512)(128)(4,1)S(1)} %iota.12), kind=kLoop, calls=%fused_computation.1 | loop fusion | flops 16384 | bytes 131136 | tf_op jit(solution)/shard_map/rows_around/jit(_where)/select_n | solution.py:392
  1.7 4.5 %collective-permute-start = (f32[8,256]{1,0:T(8,128)S(1)}, f32[8,256]{1,0:T(8,128)S(1)}, u32[]{:S(2)}, u32[]{:S(2)}) collective-permute-start(f32[8,256]{1,0:T(8,128)S(1)} %get-tuple-element.13), channel_id=1, source_target_pairs={{0,28},{4,0},{8,4},{12,8},{16,12},{20,16},{24,20},{28,24},{1,29},{... | collective-permute-start | bytes 24584 | tf_op jit(solution)/shard_map/rows_around/ppermute | solution.py:388
  6.2 0.7 %pad_bitcast_fusion = f32[1,64]{1,0:T(1,128)S(1)} fusion(f32[16]{0:T(128)} %param.21), kind=kLoop, calls=%fused_computation.4 | loop fusion | bytes 320 | tf_op jit(solution)/shard_map/weights/stack | solution.py:398
  6.9 0.7 %convert_bitcast_fusion = f32[9,2,64]{2,1,0:T(2,128)S(1)} fusion(bf16[9,64,2]{1,2,0:T(2,128)(2,1)} %param.16), kind=kLoop, calls=%fused_computation.3 | loop fusion | flops 1152 | bytes 6912 | tf_op jit(solution)/shard_map/weights/convert_element_type | solution.py:399
  7.6 0.7 %pad_maximum_fusion.1.packed_ref = f32[21,64]{1,0:T(8,128)S(1)} fusion(f32[1,64]{1,0:T(1,128)S(1)} %pad_bitcast_fusion, f32[1,64]{1,0:T(1,128)} %bitcast.14, f32[1,64]{1,0:T(1,128)} %bitcast.15, f32[18,64]{1,0:T(8,128)S(1)} %reshape.21), kind=kLoop, calls=%fused_computation.2 | loop fusion | flops 4032 | bytes 10752 | tf_op jit(solution)/shard_map/weights/concatenate | solution.py:399
  8.6 2.5 %collective-permute-done.1.top_ref = f32[8,256]{1,0:T(8,128)S(1)} collective-permute-done((f32[8,256]{1,0:T(8,128)S(1)}, f32[8,256]{1,0:T(8,128)S(1)}, u32[]{:S(2)}, u32[]{:S(2)}) %collective-permute-start.1) | collective-permute-done | bytes 8224 | tf_op jit(solution)/shard_map/rows_around/ppermute | solution.py:388
  11.2 2.5 %collective-permute-start.2 = (f32[8,128]{1,0:T(8,128)S(1)}, f32[8,128]{1,0:T(8,128)S(1)}, u32[]{:S(2)}, u32[]{:S(2)}) collective-permute-start(f32[8,128]{1,0:T(8,128)S(1)} %get-tuple-element.16), channel_id=1, source_target_pairs={{0,3},{1,0},{2,1},{3,2},{4,7},{5,4},{6,5},{7,6},{8,11},{9,8},{10,9... | collective-permute-start | bytes 12296 | tf_op jit(solution)/shard_map/columns_around/ppermute | solution.py:388
  13.7 1.0 %pad_maximum_fusion.packed_ref = bf16[720,64]{1,0:T(8,128)(2,1)S(1)} fusion(bf16[144,64]{1,0:T(8,128)(2,1)} %bitcast.13, bf16[576,64]{1,0:T(8,128)(2,1)} %bitcast.12), kind=kLoop, calls=%fused_computation | loop fusion | flops 184320 | bytes 184320 | tf_op jit(solution)/shard_map/weights/concatenate | solution.py:418
  15.1 3.1 %collective-permute-done.3.left_ref = f32[8,128]{1,0:T(8,128)S(1)} collective-permute-done((f32[8,128]{1,0:T(8,128)S(1)}, f32[8,128]{1,0:T(8,128)S(1)}, u32[]{:S(2)}, u32[]{:S(2)}) %collective-permute-start.3) | collective-permute-done | bytes 4128 | tf_op jit(solution)/shard_map/columns_around/ppermute | solution.py:388
  18.2 4.5 %advance.1.refs_0_.refs_5_ = f32[64,256]{1,0:T(8,128)S(1)} custom-call(f32[64,256]{1,0:T(8,128)S(1)} %bitcast_select_fusion.both_ref, f32[8,256]{1,0:T(8,128)S(1)} %collective-permute-done.bot_ref, f32[8,256]{1,0:T(8,128)S(1)} %collective-permute-done.1.top_ref, f32[8,128]{1,0:T(8,128)S(1)} %collective-permute-done.2.right_ref, ...), custom_call_target="tpu_custom_call" | custom-call | flops 1000000000 | bytes 1048576 | tf_op jit(solution)/shard_map/advance/pallas_call | solution.py:425
  22.8 0.6 %collective-permute-start.5 = (f32[64,256]{1,0:T(8,128)S(1)}, f32[64,256]{1,0:T(8,128)S(1)}, u32[]{:S(2)}, u32[]{:S(2)}) collective-permute-start(f32[64,256]{1,0:T(8,128)S(1)} %advance.1.refs_0_.refs_5_), channel_id=1, source_target_pairs={{0,2},{1,3},{2,0},{3,1},{4,6},{5,7},{6,4},{7,5},{8,10},{9,11},{10,... | collective-permute-start | bytes 196616 | tf_op jit(solution)/shard_map/ppermute | solution.py:365
  23.3 2.9 %collective-permute-start.4 = (f32[64,256]{1,0:T(8,128)S(1)}, f32[64,256]{1,0:T(8,128)S(1)}, u32[]{:S(2)}, u32[]{:S(2)}) collective-permute-start(f32[64,256]{1,0:T(8,128)S(1)} %advance.1.refs_0_.refs_5_), channel_id=1, source_target_pairs={{0,1},{1,0},{2,3},{3,2},{4,5},{5,4},{6,7},{7,6},{8,9},{9,8},{10,11... | collective-permute-start | bytes 196616 | tf_op jit(solution)/shard_map/ppermute | solution.py:365
  26.2 1.7 %collective-permute-done.6.refs_3_ = f32[64,256]{1,0:T(8,128)S(1)} collective-permute-done((f32[64,256]{1,0:T(8,128)S(1)}, f32[64,256]{1,0:T(8,128)S(1)}, u32[]{:S(2)}, u32[]{:S(2)}) %collective-permute-start.6) | collective-permute-done | bytes 65568 | tf_op jit(solution)/shard_map/ppermute | solution.py:365
  27.9 0.6 %collective-permute-done.4.refs_1_ = f32[64,256]{1,0:T(8,128)S(1)} collective-permute-done((f32[64,256]{1,0:T(8,128)S(1)}, f32[64,256]{1,0:T(8,128)S(1)}, u32[]{:S(2)}, u32[]{:S(2)}) %collective-permute-start.4) | collective-permute-done | bytes 65568 | tf_op jit(solution)/shard_map/ppermute | solution.py:365
  28.9 4.3 %collective-permute-start.8 = (f32[64,256]{1,0:T(8,128)S(1)}, f32[64,256]{1,0:T(8,128)S(1)}, u32[]{:S(2)}, u32[]{:S(2)}) collective-permute-start(f32[64,256]{1,0:T(8,128)S(1)} %shard_map.149.refs_0_), channel_id=1, source_target_pairs={{0,8},{4,12},{8,0},{12,4},{16,24},{20,28},{24,16},{28,20},{1,9},{5... | collective-permute-start | bytes 196616 | tf_op jit(solution)/shard_map/ppermute | solution.py:365
  33.2 1.7 %collective-permute-done.12.refs_6_ = f32[64,256]{1,0:T(8,128)S(1)} collective-permute-done((f32[64,256]{1,0:T(8,128)S(1)}, f32[64,256]{1,0:T(8,128)S(1)}, u32[]{:S(2)}, u32[]{:S(2)}) %collective-permute-start.12) | collective-permute-done | bytes 65568 | tf_op jit(solution)/shard_map/ppermute | solution.py:365
  35.5 0.6 %collective-permute-done.13.refs_7_ = f32[64,256]{1,0:T(8,128)S(1)} collective-permute-done((f32[64,256]{1,0:T(8,128)S(1)}, f32[64,256]{1,0:T(8,128)S(1)}, u32[]{:S(2)}, u32[]{:S(2)}) %collective-permute-start.13) | collective-permute-done | bytes 65568 | tf_op jit(solution)/shard_map/ppermute | solution.py:365
  36.8 1.4 %shard_map.150.refs_0_ = f32[64,256]{1,0:T(8,128)S(1)} custom-call(f32[64,256]{1,0:T(8,128)S(1)} %shard_map.149.refs_0_, f32[64,256]{1,0:T(8,128)S(1)} %collective-permute-done.7.refs_1_, f32[64,256]{1,0:T(8,128)S(1)} %collective-permute-done.8.refs_2_, f32[64,256]{1,0:T(8,128)S(1)} %collective-permute-done.9.refs_3_, ...), custom_call_target="tpu_custom_call" | custom-call | flops 10000000 | bytes 1048576 | tf_op jit(solution)/shard_map/pallas_call | solution.py:441
  38.2 2.0 %collective-permute-start.16 = (f32[64,256]{1,0:T(8,128)S(1)}, f32[64,256]{1,0:T(8,128)S(1)}, u32[]{:S(2)}, u32[]{:S(2)}) collective-permute-start(f32[64,256]{1,0:T(8,128)S(1)} %shard_map.150.refs_0_), channel_id=1, source_target_pairs={{0,3},{1,2},{2,1},{3,0},{4,7},{5,6},{6,5},{7,4},{8,11},{9,10},{10,... | collective-permute-start | bytes 196616 | tf_op jit(solution)/shard_map/ppermute | solution.py:365
  40.2 1.5 %collective-permute-start.15 = (f32[64,256]{1,0:T(8,128)S(1)}, f32[64,256]{1,0:T(8,128)S(1)}, u32[]{:S(2)}, u32[]{:S(2)}) collective-permute-start(f32[64,256]{1,0:T(8,128)S(1)} %shard_map.150.refs_0_), channel_id=1, source_target_pairs={{0,2},{1,3},{2,0},{3,1},{4,6},{5,7},{6,4},{7,5},{8,10},{9,11},{10,... | collective-permute-start | bytes 196616 | tf_op jit(solution)/shard_map/ppermute | solution.py:365
  41.7 1.8 %collective-permute-done.16.refs_3_ = f32[64,256]{1,0:T(8,128)S(1)} collective-permute-done((f32[64,256]{1,0:T(8,128)S(1)}, f32[64,256]{1,0:T(8,128)S(1)}, u32[]{:S(2)}, u32[]{:S(2)}) %collective-permute-start.16) | collective-permute-done | bytes 65568 | tf_op jit(solution)/shard_map/ppermute | solution.py:365
  43.5 1.3 %collective-permute-done.15.refs_2_ = f32[64,256]{1,0:T(8,128)S(1)} collective-permute-done((f32[64,256]{1,0:T(8,128)S(1)}, f32[64,256]{1,0:T(8,128)S(1)}, u32[]{:S(2)}, u32[]{:S(2)}) %collective-permute-start.15) | collective-permute-done | bytes 65568 | tf_op jit(solution)/shard_map/ppermute | solution.py:365
  44.8 1.2 %collective-permute-done.14.refs_1_ = f32[64,256]{1,0:T(8,128)S(1)} collective-permute-done((f32[64,256]{1,0:T(8,128)S(1)}, f32[64,256]{1,0:T(8,128)S(1)}, u32[]{:S(2)}, u32[]{:S(2)}) %collective-permute-start.14) | collective-permute-done | bytes 65568 | tf_op jit(solution)/shard_map/ppermute | solution.py:365
  46.0 0.7 %shard_map.151 = (f32[32,256]{1,0:T(8,128)}, f32[32,256]{1,0:T(8,128)}) custom-call(f32[64,256]{1,0:T(8,128)S(1)} %shard_map.150.refs_0_, f32[64,256]{1,0:T(8,128)S(1)} %collective-permute-done.14.refs_1_, f32[64,256]{1,0:T(8,128)S(1)} %collective-permute-done.15.refs_2_, f32[64,256]{1,0:T(8,128)S(1)} %collective-permute-done.16.refs_3_, ...), custom_call_target="tpu_custom_call" | custom-call | flops 10000000 | bytes 1048576 | tf_op jit(solution)/shard_map/pallas_call | solution.py:447
  (39 shorter events, 2.9 us)
Async XLA Ops:
  1.7 6.9 %collective-permute-start = (f32[8,256]{1,0:T(8,128)S(1)}, f32[8,256]{1,0:T(8,128)S(1)}, u32[]{:S(2)}, u32[]{:S(2)}) collective-permute-start(f32[8,256]{1,0:T(8,128)S(1)} %get-tuple-element.13), channel_id=1, source_target_pairs={{0,28},{4,0},{8,4},{12,8},{16,12},{20,16},{24,20},{28,24},{1,29},{... | collective-permute-start | bytes 24584 | tf_op jit(solution)/shard_map/rows_around/ppermute | solution.py:388
  6.2 4.9 %collective-permute-start.1 = (f32[8,256]{1,0:T(8,128)S(1)}, f32[8,256]{1,0:T(8,128)S(1)}, u32[]{:S(2)}, u32[]{:S(2)}) collective-permute-start(f32[8,256]{1,0:T(8,128)S(1)} %get-tuple-element.14), channel_id=1, source_target_pairs={{0,4},{4,8},{8,12},{12,16},{16,20},{20,24},{24,28},{28,0},{1,5},{5... | collective-permute-start | bytes 24584 | tf_op jit(solution)/shard_map/rows_around/ppermute | solution.py:388
  11.2 3.9 %collective-permute-start.2 = (f32[8,128]{1,0:T(8,128)S(1)}, f32[8,128]{1,0:T(8,128)S(1)}, u32[]{:S(2)}, u32[]{:S(2)}) collective-permute-start(f32[8,128]{1,0:T(8,128)S(1)} %get-tuple-element.16), channel_id=1, source_target_pairs={{0,3},{1,0},{2,1},{3,2},{4,7},{5,4},{6,5},{7,6},{8,11},{9,8},{10,9... | collective-permute-start | bytes 12296 | tf_op jit(solution)/shard_map/columns_around/ppermute | solution.py:388
  13.7 4.5 %collective-permute-start.3 = (f32[8,128]{1,0:T(8,128)S(1)}, f32[8,128]{1,0:T(8,128)S(1)}, u32[]{:S(2)}, u32[]{:S(2)}) collective-permute-start(f32[8,128]{1,0:T(8,128)S(1)} %get-tuple-element.17), channel_id=1, source_target_pairs={{0,1},{1,2},{2,3},{3,0},{4,5},{5,6},{6,7},{7,4},{8,9},{9,10},{10,1... | collective-permute-start | bytes 12296 | tf_op jit(solution)/shard_map/columns_around/ppermute | solution.py:388
  18.2 10.3 %copy-start = (bf16[256,512]{1,0:T(8,128)(2,1)S(1)}, bf16[256,512]{1,0:T(8,128)(2,1)}, u32[]{:S(2)}) copy-start(bf16[256,512]{1,0:T(8,128)(2,1)} %constant.18.clone.refs_6_.refs_11_) | copy-start | bytes 786436
  18.2 10.3 %copy-start.1 = (bf16[256,512]{1,0:T(8,128)(2,1)S(1)}, bf16[256,512]{1,0:T(8,128)(2,1)}, u32[]{:S(2)}) copy-start(bf16[256,512]{1,0:T(8,128)(2,1)} %constant.17.clone.refs_5_.refs_10_) | copy-start | bytes 786436
  18.2 10.3 %copy-start.4 = (f32[4,8,256]{2,1,0:T(8,128)S(1)}, f32[4,8,256]{2,1,0:T(8,128)}, u32[]{:S(2)}) copy-start(f32[4,8,256]{2,1,0:T(8,128)} %constant.21.clone.refs_4_) | copy-start | bytes 98308
  18.2 18.6 %copy-start.2 = (bf16[512,256]{1,0:T(8,128)(2,1)S(1)}, bf16[512,256]{1,0:T(8,128)(2,1)}, u32[]{:S(2)}) copy-start(bf16[512,256]{1,0:T(8,128)(2,1)} %constant.20.clone.refs_9_) | copy-start | bytes 786436
  18.2 18.6 %copy-start.3 = (bf16[512,256]{1,0:T(8,128)(2,1)S(1)}, bf16[512,256]{1,0:T(8,128)(2,1)}, u32[]{:S(2)}) copy-start(bf16[512,256]{1,0:T(8,128)(2,1)} %constant.19.clone.refs_8_) | copy-start | bytes 786436
  22.7 23.3 %copy-start.5 = (f32[4,8,256]{2,1,0:T(8,128)S(1)}, f32[4,8,256]{2,1,0:T(8,128)}, u32[]{:S(2)}) copy-start(f32[4,8,256]{2,1,0:T(8,128)} %constant.22.clone.refs_4_) | copy-start | bytes 98308
  22.7 5.2 %collective-permute-start.6 = (f32[64,256]{1,0:T(8,128)S(1)}, f32[64,256]{1,0:T(8,128)S(1)}, u32[]{:S(2)}, u32[]{:S(2)}) collective-permute-start(f32[64,256]{1,0:T(8,128)S(1)} %advance.1.refs_0_.refs_5_), channel_id=1, source_target_pairs={{0,3},{1,2},{2,1},{3,0},{4,7},{5,6},{6,5},{7,4},{8,11},{9,10},{10,... | collective-permute-start | bytes 196616 | tf_op jit(solution)/shard_map/ppermute | solution.py:365
  22.8 5.1 %collective-permute-start.5 = (f32[64,256]{1,0:T(8,128)S(1)}, f32[64,256]{1,0:T(8,128)S(1)}, u32[]{:S(2)}, u32[]{:S(2)}) collective-permute-start(f32[64,256]{1,0:T(8,128)S(1)} %advance.1.refs_0_.refs_5_), channel_id=1, source_target_pairs={{0,2},{1,3},{2,0},{3,1},{4,6},{5,7},{6,4},{7,5},{8,10},{9,11},{10,... | collective-permute-start | bytes 196616 | tf_op jit(solution)/shard_map/ppermute | solution.py:365
  23.3 5.1 %collective-permute-start.4 = (f32[64,256]{1,0:T(8,128)S(1)}, f32[64,256]{1,0:T(8,128)S(1)}, u32[]{:S(2)}, u32[]{:S(2)}) collective-permute-start(f32[64,256]{1,0:T(8,128)S(1)} %advance.1.refs_0_.refs_5_), channel_id=1, source_target_pairs={{0,1},{1,0},{2,3},{3,2},{4,5},{5,4},{6,7},{7,6},{8,9},{9,8},{10,11... | collective-permute-start | bytes 196616 | tf_op jit(solution)/shard_map/ppermute | solution.py:365
  28.7 6.1 %collective-permute-start.12 = (f32[64,256]{1,0:T(8,128)S(1)}, f32[64,256]{1,0:T(8,128)S(1)}, u32[]{:S(2)}, u32[]{:S(2)}) collective-permute-start(f32[64,256]{1,0:T(8,128)S(1)} %shard_map.149.refs_0_), channel_id=1, source_target_pairs={{0,24},{4,28},{8,16},{12,20},{16,8},{20,12},{24,0},{28,4},{1,25},{... | collective-permute-start | bytes 196616 | tf_op jit(solution)/shard_map/ppermute | solution.py:365
  28.8 6.1 %collective-permute-start.10 = (f32[64,256]{1,0:T(8,128)S(1)}, f32[64,256]{1,0:T(8,128)S(1)}, u32[]{:S(2)}, u32[]{:S(2)}) collective-permute-start(f32[64,256]{1,0:T(8,128)S(1)} %shard_map.149.refs_0_), channel_id=1, source_target_pairs={{0,16},{4,20},{8,24},{12,28},{16,0},{20,4},{24,8},{28,12},{1,17},{... | collective-permute-start | bytes 196616 | tf_op jit(solution)/shard_map/ppermute | solution.py:365
  28.9 6.7 %collective-permute-start.8 = (f32[64,256]{1,0:T(8,128)S(1)}, f32[64,256]{1,0:T(8,128)S(1)}, u32[]{:S(2)}, u32[]{:S(2)}) collective-permute-start(f32[64,256]{1,0:T(8,128)S(1)} %shard_map.149.refs_0_), channel_id=1, source_target_pairs={{0,8},{4,12},{8,0},{12,4},{16,24},{20,28},{24,16},{28,20},{1,9},{5... | collective-permute-start | bytes 196616 | tf_op jit(solution)/shard_map/ppermute | solution.py:365
  33.2 2.4 %collective-permute-start.7 = (f32[64,256]{1,0:T(8,128)S(1)}, f32[64,256]{1,0:T(8,128)S(1)}, u32[]{:S(2)}, u32[]{:S(2)}) collective-permute-start(f32[64,256]{1,0:T(8,128)S(1)} %shard_map.149.refs_0_), channel_id=1, source_target_pairs={{0,4},{4,0},{8,12},{12,8},{16,20},{20,16},{24,28},{28,24},{1,5},{5... | collective-permute-start | bytes 196616 | tf_op jit(solution)/shard_map/ppermute | solution.py:365
  34.8 1.3 %collective-permute-start.13 = (f32[64,256]{1,0:T(8,128)S(1)}, f32[64,256]{1,0:T(8,128)S(1)}, u32[]{:S(2)}, u32[]{:S(2)}) collective-permute-start(f32[64,256]{1,0:T(8,128)S(1)} %collective-permute-done.12.refs_6_), channel_id=1, source_target_pairs={{0,4},{4,0},{8,12},{12,8},{16,20},{20,16},{24,28},{28,24},{1,5},{5... | collective-permute-start | bytes 196616 | tf_op jit(solution)/shard_map/ppermute | solution.py:365
  34.9 1.4 %collective-permute-start.11 = (f32[64,256]{1,0:T(8,128)S(1)}, f32[64,256]{1,0:T(8,128)S(1)}, u32[]{:S(2)}, u32[]{:S(2)}) collective-permute-start(f32[64,256]{1,0:T(8,128)S(1)} %collective-permute-done.10.refs_4_), channel_id=1, source_target_pairs={{0,4},{4,0},{8,12},{12,8},{16,20},{20,16},{24,28},{28,24},{1,5},{5... | collective-permute-start | bytes 196616 | tf_op jit(solution)/shard_map/ppermute | solution.py:365
  35.5 1.3 %collective-permute-start.9 = (f32[64,256]{1,0:T(8,128)S(1)}, f32[64,256]{1,0:T(8,128)S(1)}, u32[]{:S(2)}, u32[]{:S(2)}) collective-permute-start(f32[64,256]{1,0:T(8,128)S(1)} %collective-permute-done.8.refs_2_), channel_id=1, source_target_pairs={{0,4},{4,0},{8,12},{12,8},{16,20},{20,16},{24,28},{28,24},{1,5},{5... | collective-permute-start | bytes 196616 | tf_op jit(solution)/shard_map/ppermute | solution.py:365
  38.2 5.3 %collective-permute-start.16 = (f32[64,256]{1,0:T(8,128)S(1)}, f32[64,256]{1,0:T(8,128)S(1)}, u32[]{:S(2)}, u32[]{:S(2)}) collective-permute-start(f32[64,256]{1,0:T(8,128)S(1)} %shard_map.150.refs_0_), channel_id=1, source_target_pairs={{0,3},{1,2},{2,1},{3,0},{4,7},{5,6},{6,5},{7,4},{8,11},{9,10},{10,... | collective-permute-start | bytes 196616 | tf_op jit(solution)/shard_map/ppermute | solution.py:365
  40.2 4.6 %collective-permute-start.15 = (f32[64,256]{1,0:T(8,128)S(1)}, f32[64,256]{1,0:T(8,128)S(1)}, u32[]{:S(2)}, u32[]{:S(2)}) collective-permute-start(f32[64,256]{1,0:T(8,128)S(1)} %shard_map.150.refs_0_), channel_id=1, source_target_pairs={{0,2},{1,3},{2,0},{3,1},{4,6},{5,7},{6,4},{7,5},{8,10},{9,11},{10,... | collective-permute-start | bytes 196616 | tf_op jit(solution)/shard_map/ppermute | solution.py:365
  41.7 4.3 %collective-permute-start.14 = (f32[64,256]{1,0:T(8,128)S(1)}, f32[64,256]{1,0:T(8,128)S(1)}, u32[]{:S(2)}, u32[]{:S(2)}) collective-permute-start(f32[64,256]{1,0:T(8,128)S(1)} %shard_map.150.refs_0_), channel_id=1, source_target_pairs={{0,1},{1,0},{2,3},{3,2},{4,5},{5,4},{6,7},{7,6},{8,9},{9,8},{10,11... | collective-permute-start | bytes 196616 | tf_op jit(solution)/shard_map/ppermute | solution.py:365

commit v2 on v1

--- a/solution.py
+++ b/solution.py
@@ -265,16 +265,22 @@
     out_ref[...] = spectra[:, :breadth] + sign * swap(spectra[:, breadth:])
 
 
-def row_kernel(*refs, scale):
-    *blocks, table_ref, table_low_ref, high_ref, low_ref, out_ref, gathered = refs
+def join_kernel(*refs):
+    *blocks, out_ref = refs
+    for k, ref in enumerate(blocks):
+        out_ref[k] = ref[...]
+
+
+def row_kernel(own_ref, other_ref, table_ref, table_low_ref, high_ref, low_ref, out_ref, gathered, *, scale):
     rows, breadth = out_ref.shape
     height = rows // 2
-    length = len(blocks) * height
+    length = 2 * own_ref.shape[0] * height
     own_index = lax.axis_index("gx")
-    for k, ref in enumerate(blocks):
-        start = pl.multiple_of((own_index ^ k) * height, height)
-        gathered[pl.ds(start, height), :breadth] = ref[:height, :]
-        gathered[pl.ds(start, height), breadth:] = ref[height:, :]
+    for core, ref in enumerate((own_ref, other_ref)):
+        for k in range(own_ref.shape[0]):
+            start = pl.multiple_of((own_index ^ (2 * k + core)) * height, height)
+            gathered[pl.ds(start, height), :breadth] = ref[k, :height, :]
+            gathered[pl.ds(start, height), breadth:] = ref[k, height:, :]
     data = gathered[...]
     data, data_low = split(data)
     spectra = dot(table_ref[...], data) + dot(table_ref[...], data_low) + dot(table_low_ref[...], data)
@@ -370,8 +376,9 @@
 
 
 def gather_x(block):
-    own = [block] + [partner(block, "gx", k) for k in range(2, lax.axis_size("gx"), 2)]
-    return [other for held in own for other in (held, partner(held, "gx", 1))]
+    blocks = [block] + [partner(block, "gx", k) for k in range(2, lax.axis_size("gx"), 2)]
+    own = call(join_kernel, jax.ShapeDtypeStruct((len(blocks), *block.shape), f32))(*blocks)
+    return own, partner(own, "gx", 1)
 
 
 def on_device(u_field, v_field, w_first, b_first, w_second, b_second, w_third, b_third):

time: 46.9 us -> 47.3 us (level)
  waiting for transfers between devices: 15.2 us -> 16 us
    ppermute x13 -> x10, waiting for transfers between devices: 9.61 us -> 10.4 us  [partner(): lax.ppermute(block, axis, [(i, i ^ k) for i in range(lax.axis_size(axis))])]
    ppermute x13 -> x10, starting transfers between devices: 12.1 us -> 11.6 us  [partner(): lax.ppermute(block, axis, [(i, i ^ k) for i in range(lax.axis_size(axis))])]
  transfers between devices with their start and end apart: 17 -> 14, of which waited for: 12 -> 10; matrix products, arithmetic and copies ran while one was open for 6% -> 6% of each run, Pallas kernels for 2% -> 2%
where the time goes in v2:
time: 47.3 us; the launch traced here: 47 us
  starting transfers between devices  18.7 us (40%)
  waiting for transfers between devices  16 us (34%)
  Pallas kernels  7.59 us (16%)
  other arithmetic  3.2 us (7%)
  local copies, waits for them, and re-layouts  0.86 us (2%)
  between operations  0.77 us (2%)
    ppermute x10, starting transfers between devices, partner(): lax.ppermute(block, axis, [(i, i ^ k) for i in range(lax.axis_size(axis))])  11.6 us
    ppermute x10, waiting for transfers between devices, partner(): lax.ppermute(block, axis, [(i, i ^ k) for i in range(lax.axis_size(axis))])  10.4 us
    ppermute x4, starting transfers between devices, shifted(): lax.ppermute(value, axis, [(i, (i + distance) % peers) for i in range(pee...  7.05 us
    ppermute x4, waiting for transfers between devices, shifted(): lax.ppermute(value, axis, [(i, (i + distance) % peers) for i in range(pee...  5.55 us
    pallas_call x1, Pallas kernels, on_device(): call(advance_kernel, block, (pltpu.VMEM((2, rows + 16, breadth + 128), f3...  4.45 us
    pallas_call x1, Pallas kernels, on_device(): call(functools.partial(row_kernel, scale=1.0 / (grid_x * grid_y)), block,...  1.37 us
    concatenate x1, other arithmetic, on_device(): jnp.concatenate([w_second.reshape(576, 64), w_third.reshape(144, 64)], ax...  0.97 us
  transfers between devices with their start and end apart: 14, of which 10 were waited for; matrix products, arithmetic and copies ran while one was open for 6% of the time, Pallas kernels for 2%

profile of v2, /device:TPU:0, one launch (start us, length us, event | category | flops | bytes accessed | tf_op | source)
XLA Modules:
  0.0 47.0 jit_solution(8580595146553135048)
XLA Ops:
  0.8 0.8 %bitcast_select_fusion.both_ref = f32[64,256]{1,0:T(8,128)S(1)} fusion(f32[32,256]{1,0:T(8,128)} %param.15, f32[32,256]{1,0:T(8,128)} %param.14, pred[64]{0:T(512)(128)(4,1)S(1)} %iota.12), kind=kLoop, calls=%fused_computation.1 | loop fusion | flops 16384 | bytes 131136 | tf_op jit(solution)/shard_map/rows_around/jit(_where)/select_n | solution.py:399
  1.7 4.5 %collective-permute-start = (f32[8,256]{1,0:T(8,128)S(1)}, f32[8,256]{1,0:T(8,128)S(1)}, u32[]{:S(2)}, u32[]{:S(2)}) collective-permute-start(f32[8,256]{1,0:T(8,128)S(1)} %get-tuple-element.13), channel_id=1, source_target_pairs={{0,28},{4,0},{8,4},{12,8},{16,12},{20,16},{24,20},{28,24},{1,29},{... | collective-permute-start | bytes 24584 | tf_op jit(solution)/shard_map/rows_around/ppermute | solution.py:395
  6.2 0.7 %pad_bitcast_fusion = f32[1,64]{1,0:T(1,128)S(1)} fusion(f32[16]{0:T(128)} %param.21), kind=kLoop, calls=%fused_computation.4 | loop fusion | bytes 320 | tf_op jit(solution)/shard_map/weights/stack | solution.py:405
  6.9 0.7 %convert_bitcast_fusion = f32[9,2,64]{2,1,0:T(2,128)S(1)} fusion(bf16[9,64,2]{1,2,0:T(2,128)(2,1)} %param.16), kind=kLoop, calls=%fused_computation.3 | loop fusion | flops 1152 | bytes 6912 | tf_op jit(solution)/shard_map/weights/convert_element_type | solution.py:406
  7.6 0.7 %pad_maximum_fusion.1.packed_ref = f32[21,64]{1,0:T(8,128)S(1)} fusion(f32[1,64]{1,0:T(1,128)S(1)} %pad_bitcast_fusion, f32[1,64]{1,0:T(1,128)} %bitcast.14, f32[1,64]{1,0:T(1,128)} %bitcast.15, f32[18,64]{1,0:T(8,128)S(1)} %reshape.21), kind=kLoop, calls=%fused_computation.2 | loop fusion | flops 4032 | bytes 10752 | tf_op jit(solution)/shard_map/weights/concatenate | solution.py:406
  8.6 2.5 %collective-permute-done.1.top_ref = f32[8,256]{1,0:T(8,128)S(1)} collective-permute-done((f32[8,256]{1,0:T(8,128)S(1)}, f32[8,256]{1,0:T(8,128)S(1)}, u32[]{:S(2)}, u32[]{:S(2)}) %collective-permute-start.1) | collective-permute-done | bytes 8224 | tf_op jit(solution)/shard_map/rows_around/ppermute | solution.py:395
  11.2 2.5 %collective-permute-start.2 = (f32[8,128]{1,0:T(8,128)S(1)}, f32[8,128]{1,0:T(8,128)S(1)}, u32[]{:S(2)}, u32[]{:S(2)}) collective-permute-start(f32[8,128]{1,0:T(8,128)S(1)} %get-tuple-element.16), channel_id=1, source_target_pairs={{0,3},{1,0},{2,1},{3,2},{4,7},{5,4},{6,5},{7,6},{8,11},{9,8},{10,9... | collective-permute-start | bytes 12296 | tf_op jit(solution)/shard_map/columns_around/ppermute | solution.py:395
  13.7 1.0 %pad_maximum_fusion.packed_ref = bf16[720,64]{1,0:T(8,128)(2,1)S(1)} fusion(bf16[144,64]{1,0:T(8,128)(2,1)} %bitcast.13, bf16[576,64]{1,0:T(8,128)(2,1)} %bitcast.12), kind=kLoop, calls=%fused_computation | loop fusion | flops 184320 | bytes 184320 | tf_op jit(solution)/shard_map/weights/concatenate | solution.py:425
  15.1 3.1 %collective-permute-done.3.left_ref = f32[8,128]{1,0:T(8,128)S(1)} collective-permute-done((f32[8,128]{1,0:T(8,128)S(1)}, f32[8,128]{1,0:T(8,128)S(1)}, u32[]{:S(2)}, u32[]{:S(2)}) %collective-permute-start.3) | collective-permute-done | bytes 4128 | tf_op jit(solution)/shard_map/columns_around/ppermute | solution.py:395
  18.2 4.5 %advance.1.refs_0_.refs_5_ = f32[64,256]{1,0:T(8,128)S(1)} custom-call(f32[64,256]{1,0:T(8,128)S(1)} %bitcast_select_fusion.both_ref, f32[8,256]{1,0:T(8,128)S(1)} %collective-permute-done.bot_ref, f32[8,256]{1,0:T(8,128)S(1)} %collective-permute-done.1.top_ref, f32[8,128]{1,0:T(8,128)S(1)} %collective-permute-done.2.right_ref, ...), custom_call_target="tpu_custom_call" | custom-call | flops 1000000000 | bytes 1048576 | tf_op jit(solution)/shard_map/advance/pallas_call | solution.py:432
  22.8 0.6 %collective-permute-start.5 = (f32[64,256]{1,0:T(8,128)S(1)}, f32[64,256]{1,0:T(8,128)S(1)}, u32[]{:S(2)}, u32[]{:S(2)}) collective-permute-start(f32[64,256]{1,0:T(8,128)S(1)} %advance.1.refs_0_.refs_5_), channel_id=1, source_target_pairs={{0,2},{1,3},{2,0},{3,1},{4,6},{5,7},{6,4},{7,5},{8,10},{9,11},{10,... | collective-permute-start | bytes 196616 | tf_op jit(solution)/shard_map/ppermute | solution.py:371
  23.3 2.9 %collective-permute-start.4 = (f32[64,256]{1,0:T(8,128)S(1)}, f32[64,256]{1,0:T(8,128)S(1)}, u32[]{:S(2)}, u32[]{:S(2)}) collective-permute-start(f32[64,256]{1,0:T(8,128)S(1)} %advance.1.refs_0_.refs_5_), channel_id=1, source_target_pairs={{0,1},{1,0},{2,3},{3,2},{4,5},{5,4},{6,7},{7,6},{8,9},{9,8},{10,11... | collective-permute-start | bytes 196616 | tf_op jit(solution)/shard_map/ppermute | solution.py:371
  26.2 1.7 %collective-permute-done.6.refs_3_ = f32[64,256]{1,0:T(8,128)S(1)} collective-permute-done((f32[64,256]{1,0:T(8,128)S(1)}, f32[64,256]{1,0:T(8,128)S(1)}, u32[]{:S(2)}, u32[]{:S(2)}) %collective-permute-start.6) | collective-permute-done | bytes 65568 | tf_op jit(solution)/shard_map/ppermute | solution.py:371
  28.9 4.3 %collective-permute-start.7 = (f32[64,256]{1,0:T(8,128)S(1)}, f32[64,256]{1,0:T(8,128)S(1)}, u32[]{:S(2)}, u32[]{:S(2)}) collective-permute-start(f32[64,256]{1,0:T(8,128)S(1)} %shard_map.149.refs_0_), channel_id=1, source_target_pairs={{0,8},{4,12},{8,0},{12,4},{16,24},{20,28},{24,16},{28,20},{1,9},{5... | collective-permute-start | bytes 196616 | tf_op jit(solution)/shard_map/ppermute | solution.py:371
  33.2 1.7 %collective-permute-done.9.refs_3_ = f32[64,256]{1,0:T(8,128)S(1)} collective-permute-done((f32[64,256]{1,0:T(8,128)S(1)}, f32[64,256]{1,0:T(8,128)S(1)}, u32[]{:S(2)}, u32[]{:S(2)}) %collective-permute-start.9) | collective-permute-done | bytes 65568 | tf_op jit(solution)/shard_map/ppermute | solution.py:371
  34.9 0.7 %collective-permute-done.7.refs_1_ = f32[64,256]{1,0:T(8,128)S(1)} collective-permute-done((f32[64,256]{1,0:T(8,128)S(1)}, f32[64,256]{1,0:T(8,128)S(1)}, u32[]{:S(2)}, u32[]{:S(2)}) %collective-permute-start.7) | collective-permute-done | bytes 65568 | tf_op jit(solution)/shard_map/ppermute | solution.py:371
  35.6 1.5 %collective-permute-done.10.other_ref = f32[4,64,256]{2,1,0:T(8,128)S(1)} collective-permute-done((f32[4,64,256]{2,1,0:T(8,128)S(1)}, f32[4,64,256]{2,1,0:T(8,128)S(1)}, u32[]{:S(2)}, u32[]{:S(2)}) %collective-permute-start.10) | collective-permute-done | bytes 262176 | tf_op jit(solution)/shard_map/ppermute | solution.py:371
  37.2 1.4 %shard_map.151.refs_0_ = f32[64,256]{1,0:T(8,128)S(1)} custom-call(f32[4,64,256]{2,1,0:T(8,128)S(1)} %shard_map.150.own_ref, f32[4,64,256]{2,1,0:T(8,128)S(1)} %collective-permute-done.10.other_ref, bf16[512,256]{1,0:T(8,128)(2,1)S(1)} %copy-done.3, bf16[512,256]{1,0:T(8,128)(2,1)S(1)} %copy-done.2, bf16[256,512]{1,0:T(8,128)(2,1)S(1)} %copy-done.1, ...), custom_call_target="tpu_custom_call" | custom-call | flops 10000000 | bytes 1048576 | tf_op jit(solution)/shard_map/pallas_call | solution.py:448
  38.5 2.0 %collective-permute-start.13 = (f32[64,256]{1,0:T(8,128)S(1)}, f32[64,256]{1,0:T(8,128)S(1)}, u32[]{:S(2)}, u32[]{:S(2)}) collective-permute-start(f32[64,256]{1,0:T(8,128)S(1)} %shard_map.151.refs_0_), channel_id=1, source_target_pairs={{0,3},{1,2},{2,1},{3,0},{4,7},{5,6},{6,5},{7,4},{8,11},{9,10},{10,... | collective-permute-start | bytes 196616 | tf_op jit(solution)/shard_map/ppermute | solution.py:371
  40.6 1.5 %collective-permute-start.12 = (f32[64,256]{1,0:T(8,128)S(1)}, f32[64,256]{1,0:T(8,128)S(1)}, u32[]{:S(2)}, u32[]{:S(2)}) collective-permute-start(f32[64,256]{1,0:T(8,128)S(1)} %shard_map.151.refs_0_), channel_id=1, source_target_pairs={{0,2},{1,3},{2,0},{3,1},{4,6},{5,7},{6,4},{7,5},{8,10},{9,11},{10,... | collective-permute-start | bytes 196616 | tf_op jit(solution)/shard_map/ppermute | solution.py:371
  42.1 1.8 %collective-permute-done.13.refs_3_ = f32[64,256]{1,0:T(8,128)S(1)} collective-permute-done((f32[64,256]{1,0:T(8,128)S(1)}, f32[64,256]{1,0:T(8,128)S(1)}, u32[]{:S(2)}, u32[]{:S(2)}) %collective-permute-start.13) | collective-permute-done | bytes 65568 | tf_op jit(solution)/shard_map/ppermute | solution.py:371
  43.9 1.2 %collective-permute-done.12.refs_2_ = f32[64,256]{1,0:T(8,128)S(1)} collective-permute-done((f32[64,256]{1,0:T(8,128)S(1)}, f32[64,256]{1,0:T(8,128)S(1)}, u32[]{:S(2)}, u32[]{:S(2)}) %collective-permute-start.12) | collective-permute-done | bytes 65568 | tf_op jit(solution)/shard_map/ppermute | solution.py:371
  45.1 1.2 %collective-permute-done.11.refs_1_ = f32[64,256]{1,0:T(8,128)S(1)} collective-permute-done((f32[64,256]{1,0:T(8,128)S(1)}, f32[64,256]{1,0:T(8,128)S(1)}, u32[]{:S(2)}, u32[]{:S(2)}) %collective-permute-start.11) | collective-permute-done | bytes 65568 | tf_op jit(solution)/shard_map/ppermute | solution.py:371
  46.4 0.7 %shard_map.152 = (f32[32,256]{1,0:T(8,128)}, f32[32,256]{1,0:T(8,128)}) custom-call(f32[64,256]{1,0:T(8,128)S(1)} %shard_map.151.refs_0_, f32[64,256]{1,0:T(8,128)S(1)} %collective-permute-done.11.refs_1_, f32[64,256]{1,0:T(8,128)S(1)} %collective-permute-done.12.refs_2_, f32[64,256]{1,0:T(8,128)S(1)} %collective-permute-done.13.refs_3_, ...), custom_call_target="tpu_custom_call" | custom-call | flops 10000000 | bytes 1048576 | tf_op jit(solution)/shard_map/pallas_call | solution.py:454
  (34 shorter events, 2.2 us)
Async XLA Ops:
  1.7 6.9 %collective-permute-start = (f32[8,256]{1,0:T(8,128)S(1)}, f32[8,256]{1,0:T(8,128)S(1)}, u32[]{:S(2)}, u32[]{:S(2)}) collective-permute-start(f32[8,256]{1,0:T(8,128)S(1)} %get-tuple-element.13), channel_id=1, source_target_pairs={{0,28},{4,0},{8,4},{12,8},{16,12},{20,16},{24,20},{28,24},{1,29},{... | collective-permute-start | bytes 24584 | tf_op jit(solution)/shard_map/rows_around/ppermute | solution.py:395
  6.2 4.9 %collective-permute-start.1 = (f32[8,256]{1,0:T(8,128)S(1)}, f32[8,256]{1,0:T(8,128)S(1)}, u32[]{:S(2)}, u32[]{:S(2)}) collective-permute-start(f32[8,256]{1,0:T(8,128)S(1)} %get-tuple-element.14), channel_id=1, source_target_pairs={{0,4},{4,8},{8,12},{12,16},{16,20},{20,24},{24,28},{28,0},{1,5},{5... | collective-permute-start | bytes 24584 | tf_op jit(solution)/shard_map/rows_around/ppermute | solution.py:395
  11.2 3.9 %collective-permute-start.2 = (f32[8,128]{1,0:T(8,128)S(1)}, f32[8,128]{1,0:T(8,128)S(1)}, u32[]{:S(2)}, u32[]{:S(2)}) collective-permute-start(f32[8,128]{1,0:T(8,128)S(1)} %get-tuple-element.16), channel_id=1, source_target_pairs={{0,3},{1,0},{2,1},{3,2},{4,7},{5,4},{6,5},{7,6},{8,11},{9,8},{10,9... | collective-permute-start | bytes 12296 | tf_op jit(solution)/shard_map/columns_around/ppermute | solution.py:395
  13.7 4.5 %collective-permute-start.3 = (f32[8,128]{1,0:T(8,128)S(1)}, f32[8,128]{1,0:T(8,128)S(1)}, u32[]{:S(2)}, u32[]{:S(2)}) collective-permute-start(f32[8,128]{1,0:T(8,128)S(1)} %get-tuple-element.17), channel_id=1, source_target_pairs={{0,1},{1,2},{2,3},{3,0},{4,5},{5,6},{6,7},{7,4},{8,9},{9,10},{10,1... | collective-permute-start | bytes 12296 | tf_op jit(solution)/shard_map/columns_around/ppermute | solution.py:395
  18.2 10.3 %copy-start = (bf16[256,512]{1,0:T(8,128)(2,1)S(1)}, bf16[256,512]{1,0:T(8,128)(2,1)}, u32[]{:S(2)}) copy-start(bf16[256,512]{1,0:T(8,128)(2,1)} %constant.18.clone.refs_6_.low_ref) | copy-start | bytes 786436
  18.2 10.3 %copy-start.1 = (bf16[256,512]{1,0:T(8,128)(2,1)S(1)}, bf16[256,512]{1,0:T(8,128)(2,1)}, u32[]{:S(2)}) copy-start(bf16[256,512]{1,0:T(8,128)(2,1)} %constant.17.clone.refs_5_.high_ref) | copy-start | bytes 786436
  18.2 10.3 %copy-start.4 = (f32[4,8,256]{2,1,0:T(8,128)S(1)}, f32[4,8,256]{2,1,0:T(8,128)}, u32[]{:S(2)}) copy-start(f32[4,8,256]{2,1,0:T(8,128)} %constant.21.clone.refs_4_) | copy-start | bytes 98308
  22.6 14.5 %copy-start.2 = (bf16[512,256]{1,0:T(8,128)(2,1)S(1)}, bf16[512,256]{1,0:T(8,128)(2,1)}, u32[]{:S(2)}) copy-start(bf16[512,256]{1,0:T(8,128)(2,1)} %constant.20.clone.table_low_ref) | copy-start | bytes 786436
  22.6 14.5 %copy-start.3 = (bf16[512,256]{1,0:T(8,128)(2,1)S(1)}, bf16[512,256]{1,0:T(8,128)(2,1)}, u32[]{:S(2)}) copy-start(bf16[512,256]{1,0:T(8,128)(2,1)} %constant.19.clone.table_ref) | copy-start | bytes 786436
  22.7 23.7 %copy-start.5 = (f32[4,8,256]{2,1,0:T(8,128)S(1)}, f32[4,8,256]{2,1,0:T(8,128)}, u32[]{:S(2)}) copy-start(f32[4,8,256]{2,1,0:T(8,128)} %constant.22.clone.refs_4_) | copy-start | bytes 98308
  22.7 5.2 %collective-permute-start.6 = (f32[64,256]{1,0:T(8,128)S(1)}, f32[64,256]{1,0:T(8,128)S(1)}, u32[]{:S(2)}, u32[]{:S(2)}) collective-permute-start(f32[64,256]{1,0:T(8,128)S(1)} %advance.1.refs_0_.refs_5_), channel_id=1, source_target_pairs={{0,3},{1,2},{2,1},{3,0},{4,7},{5,6},{6,5},{7,4},{8,11},{9,10},{10,... | collective-permute-start | bytes 196616 | tf_op jit(solution)/shard_map/ppermute | solution.py:371
  22.8 5.2 %collective-permute-start.5 = (f32[64,256]{1,0:T(8,128)S(1)}, f32[64,256]{1,0:T(8,128)S(1)}, u32[]{:S(2)}, u32[]{:S(2)}) collective-permute-start(f32[64,256]{1,0:T(8,128)S(1)} %advance.1.refs_0_.refs_5_), channel_id=1, source_target_pairs={{0,2},{1,3},{2,0},{3,1},{4,6},{5,7},{6,4},{7,5},{8,10},{9,11},{10,... | collective-permute-start | bytes 196616 | tf_op jit(solution)/shard_map/ppermute | solution.py:371
  23.3 5.1 %collective-permute-start.4 = (f32[64,256]{1,0:T(8,128)S(1)}, f32[64,256]{1,0:T(8,128)S(1)}, u32[]{:S(2)}, u32[]{:S(2)}) collective-permute-start(f32[64,256]{1,0:T(8,128)S(1)} %advance.1.refs_0_.refs_5_), channel_id=1, source_target_pairs={{0,1},{1,0},{2,3},{3,2},{4,5},{5,4},{6,7},{7,6},{8,9},{9,8},{10,11... | collective-permute-start | bytes 196616 | tf_op jit(solution)/shard_map/ppermute | solution.py:371
  28.7 6.1 %collective-permute-start.9 = (f32[64,256]{1,0:T(8,128)S(1)}, f32[64,256]{1,0:T(8,128)S(1)}, u32[]{:S(2)}, u32[]{:S(2)}) collective-permute-start(f32[64,256]{1,0:T(8,128)S(1)} %shard_map.149.refs_0_), channel_id=1, source_target_pairs={{0,24},{4,28},{8,16},{12,20},{16,8},{20,12},{24,0},{28,4},{1,25},{... | collective-permute-start | bytes 196616 | tf_op jit(solution)/shard_map/ppermute | solution.py:371
  28.8 6.1 %collective-permute-start.8 = (f32[64,256]{1,0:T(8,128)S(1)}, f32[64,256]{1,0:T(8,128)S(1)}, u32[]{:S(2)}, u32[]{:S(2)}) collective-permute-start(f32[64,256]{1,0:T(8,128)S(1)} %shard_map.149.refs_0_), channel_id=1, source_target_pairs={{0,16},{4,20},{8,24},{12,28},{16,0},{20,4},{24,8},{28,12},{1,17},{... | collective-permute-start | bytes 196616 | tf_op jit(solution)/shard_map/ppermute | solution.py:371
  28.9 6.7 %collective-permute-start.7 = (f32[64,256]{1,0:T(8,128)S(1)}, f32[64,256]{1,0:T(8,128)S(1)}, u32[]{:S(2)}, u32[]{:S(2)}) collective-permute-start(f32[64,256]{1,0:T(8,128)S(1)} %shard_map.149.refs_0_), channel_id=1, source_target_pairs={{0,8},{4,12},{8,0},{12,4},{16,24},{20,28},{24,16},{28,20},{1,9},{5... | collective-permute-start | bytes 196616 | tf_op jit(solution)/shard_map/ppermute | solution.py:371
  35.6 1.6 %collective-permute-start.10 = (f32[4,64,256]{2,1,0:T(8,128)S(1)}, f32[4,64,256]{2,1,0:T(8,128)S(1)}, u32[]{:S(2)}, u32[]{:S(2)}) collective-permute-start(f32[4,64,256]{2,1,0:T(8,128)S(1)} %shard_map.150.own_ref), channel_id=1, source_target_pairs={{0,4},{4,0},{8,12},{12,8},{16,20},{20,16},{24,28},{28,24},{1,5},{5... | collective-permute-start | bytes 786440 | tf_op jit(solution)/shard_map/ppermute | solution.py:371
  38.5 5.3 %collective-permute-start.13 = (f32[64,256]{1,0:T(8,128)S(1)}, f32[64,256]{1,0:T(8,128)S(1)}, u32[]{:S(2)}, u32[]{:S(2)}) collective-permute-start(f32[64,256]{1,0:T(8,128)S(1)} %shard_map.151.refs_0_), channel_id=1, source_target_pairs={{0,3},{1,2},{2,1},{3,0},{4,7},{5,6},{6,5},{7,4},{8,11},{9,10},{10,... | collective-permute-start | bytes 196616 | tf_op jit(solution)/shard_map/ppermute | solution.py:371
  40.6 4.6 %collective-permute-start.12 = (f32[64,256]{1,0:T(8,128)S(1)}, f32[64,256]{1,0:T(8,128)S(1)}, u32[]{:S(2)}, u32[]{:S(2)}) collective-permute-start(f32[64,256]{1,0:T(8,128)S(1)} %shard_map.151.refs_0_), channel_id=1, source_target_pairs={{0,2},{1,3},{2,0},{3,1},{4,6},{5,7},{6,4},{7,5},{8,10},{9,11},{10,... | collective-permute-start | bytes 196616 | tf_op jit(solution)/shard_map/ppermute | solution.py:371
  42.1 4.3 %collective-permute-start.11 = (f32[64,256]{1,0:T(8,128)S(1)}, f32[64,256]{1,0:T(8,128)S(1)}, u32[]{:S(2)}, u32[]{:S(2)}) collective-permute-start(f32[64,256]{1,0:T(8,128)S(1)} %shard_map.151.refs_0_), channel_id=1, source_target_pairs={{0,1},{1,0},{2,3},{3,2},{4,5},{5,4},{6,7},{7,6},{8,9},{9,8},{10,11... | collective-permute-start | bytes 196616 | tf_op jit(solution)/shard_map/ppermute | solution.py:371

commit v3 on v1

--- a/solution.py
+++ b/solution.py
@@ -50,25 +50,27 @@
     return jnp.concatenate([value[half:], value[:half]], axis=0)
 
 
-def rows_kernel(both_ref, last_ref, first_ref):
-    height = both_ref.shape[0] // 2
-    for q in range(2):
-        last_ref[4 * q : 4 * q + 4, :] = both_ref[height * (q + 1) - 4 : height * (q + 1), :]
-        first_ref[4 * q : 4 * q + 4, :] = both_ref[height * q : height * q + 4, :]
-
-
-def columns_kernel(both_ref, bot_ref, top_ref, order_ref, last_ref, first_ref, strip):
-    height, breadth = both_ref.shape[0] // 2, both_ref.shape[1]
-    rows = height + 8
+def columns_kernel(both_ref, last_ref, first_ref, strip):
+    cells, breadth = both_ref.shape
+    strip[cells:, :] = jnp.zeros((128 - cells, 128), f32)
     for side, out in ((0, first_ref), (breadth - 128, last_ref)):
-        strip[...] = jnp.zeros_like(strip)
-        for q in range(2):
-            start = rows * q
-            strip[start : start + height, :] = both_ref[height * q : height * (q + 1), side : side + 128]
-            strip[start + height : start + height + 4, :] = bot_ref[4 * q : 4 * q + 4, side : side + 128]
-            strip[start + height + 4 : start + rows, :] = top_ref[4 * q : 4 * q + 4, side : side + 128]
+        strip[:cells, :] = both_ref[:, side : side + 128]
         turned = strip[...].T
         out[...] = turned[0:8] if side == 0 else turned[120:128]
+
+
+def rows_kernel(both_ref, right_ref, left_ref, order_ref, order_too_ref, last_ref, first_ref, beside_ref, strip):
+    height, breadth = both_ref.shape[0] // 2, both_ref.shape[1]
+    strip[...] = jnp.zeros_like(strip)
+    strip[0:4, :] = right_ref[0:4, :]
+    strip[124:128, :] = left_ref[4:8, :]
+    beside_ref[...] = strip[...].T[: 2 * height]
+    for q in range(2):
+        start, end, own = height * q, height * (q + 1), slice(4 * q, 4 * q + 4)
+        last_ref[own, :breadth] = both_ref[end - 4 : end, :]
+        last_ref[own, breadth:] = beside_ref[end - 4 : end, :]
+        first_ref[own, :breadth] = both_ref[start : start + 4, :]
+        first_ref[own, breadth:] = beside_ref[start : start + 4, :]
 
 
 def first_weights_kernel(packed_ref, k1_ref, c1_ref, c2_ref, c3_ref, *, rows):
@@ -99,7 +101,8 @@
         k1_ref[r] = block.astype(bf16)
 
 
-def other_weights_kernel(packed_ref, k2_ref, even_ref, odd_ref):
+def other_weights_kernel(packed_ref, k2_ref, even_ref, odd_ref, order_ref):
+    order_ref[...] = jnp.zeros(order_ref.shape, f32)
     k2_ref[...] = jnp.zeros(k2_ref.shape, bf16)
     slots = {-1: 5, 0: 0, 1: 1, 2: 2, 3: 3, 4: 6}
     blank = jnp.zeros((64, 64), f32)
@@ -139,69 +142,118 @@
     odd_ref[...] = dot(raw, jnp.where(source == column_odd, 1.0, 0.0).astype(bf16)).astype(bf16)
 
 
+def fill(field, both_ref, beside_ref, height, breadth):
+    for q in range(2):
+        field[q, 8 : 8 + height, :breadth] = both_ref[height * q : height * (q + 1), :]
+        field[q, 8 : 8 + height, breadth:] = beside_ref[height * q : height * (q + 1), :]
+
+
+def patches_of(field, rows, depth):
+    lanes = field.shape[2]
+    whole = jnp.concatenate([field[0, 8 : 8 + rows], field[1, 8 : 8 + rows]], axis=0)
+    pieces = [pltpu.roll(whole, 1, 1), whole, pltpu.roll(whole, lanes - 1, 1)]
+    pieces.append(jnp.zeros((depth - 6 * rows, lanes), f32))
+    turned = jnp.concatenate(pieces, axis=0).T
+    return jnp.concatenate([turned[: lanes - 120], turned[lanes - 8 :]], axis=0).astype(bf16)
+
+
+def layer_1(patches, weights_ref, bias_ref, r):
+    return jnp.maximum(dot(patches, weights_ref[r]) + bias_ref[...], 0.0).astype(bf16)
+
+
+def with_neighbours(before, own, after, weights_ref):
+    beside = jnp.concatenate([before[:, 128:], after[:, :128]], axis=1)
+    return dot(own[...], weights_ref[:256]) + dot(beside, weights_ref[256:])
+
+
+def layer_2(before, own, after, weights_ref, bias_ref):
+    total = with_neighbours(before, own, after, weights_ref)
+    span = total.shape[0]
+    total = pltpu.roll(total[:, :256], 1, 0) + total[:, 256:512] + pltpu.roll(total[:, 512:], span - 1, 0)
+    return jnp.maximum(total + bias_ref[...], 0.0).astype(bf16)
+
+
+def layer_3(second, groups, r, weights_ref):
+    total = with_neighbours(second((r - 1) % groups), second(r), second((r + 1) % groups), weights_ref)
+    left_part = total[:, :128]
+    return (
+        pltpu.roll(left_part, 1, 0)
+        + pltpu.roll(left_part, 64, 1)
+        + pltpu.roll(total[:, 128:], total.shape[0] - 1, 0)
+    )
+
+
+def coefficients(second, groups, even, odd, even_ref, odd_ref):
+    block = layer_3(second, groups, even, even_ref)
+    if odd is not None:
+        lower = lax.broadcasted_iota(jnp.int32, block.shape, 1) < 64
+        block = jnp.where(lower, block, layer_3(second, groups, odd, odd_ref))
+    span = block.shape[0]
+    filler = jnp.zeros((112, 128), f32)
+    return jnp.concatenate([block[: span - 8], filler, block[span - 8 :]], axis=0).T
+
+
+def inner_kernel(
+    both_ref, beside_ref, w1_ref, w2_ref, even_ref, odd_ref, b1_ref, b2_ref, first_ref, second_ref, coeff_ref, field
+):
+    height, breadth = both_ref.shape[0] // 2, both_ref.shape[1]
+    rows = height + 8
+    groups = rows // 4
+    field[...] = jnp.zeros_like(field)
+    fill(field, both_ref, beside_ref, height, breadth)
+    patches = patches_of(field, rows, w1_ref.shape[1])
+    for r in range(1, groups - 3):
+        first_ref[r - 1] = layer_1(patches, w1_ref, b1_ref, r)
+        if r >= 3:
+            second_ref[r - 3] = layer_2(
+                first_ref.at[r - 3], first_ref.at[r - 2], first_ref.at[r - 1], w2_ref, b2_ref
+            )
+    block = coefficients(lambda r: second_ref.at[r - 2], groups, 3, 4, even_ref, odd_ref)
+    coeff_ref[0] = block[:64]
+    coeff_ref[1] = block[64:]
+
+
 def advance_kernel(
-    both_ref, bot_ref, top_ref, right_ref, left_ref, w1_ref, w2_ref, w3e_ref, w3o_ref,
-    b1_ref, b2_ref, b3_ref, star_ref, field, first, second, coeff, strip,
+    both_ref, beside_ref, bot_ref, top_ref, w1_ref, w2_ref, even_ref, odd_ref, b1_ref, b2_ref, b3_ref,
+    first_ref, second_ref, coeff_ref, star_ref, field, outer_first, outer_second, outer_coeff,
 ):
     height, breadth = both_ref.shape[0] // 2, both_ref.shape[1]
     rows = height + 8
     groups = rows // 4
     lanes = breadth + 128
-    strip[...] = jnp.zeros_like(strip)
-    strip[0:4, :] = right_ref[0:4, :]
-    strip[124:128, :] = left_ref[4:8, :]
-    beside = strip[...].T
+    fill(field, both_ref, beside_ref, height, breadth)
     for q in range(2):
-        field[q, 8 : 8 + height, :breadth] = both_ref[height * q : height * (q + 1), :]
-        field[q, 8 + height : 12 + height, :breadth] = bot_ref[4 * q : 4 * q + 4, :]
-        field[q, 12 + height : 16 + height, :breadth] = top_ref[4 * q : 4 * q + 4, :]
-        field[q, 8 : 8 + rows, breadth:] = beside[rows * q : rows * q + rows]
+        field[q, 8 + height : 12 + height, :] = bot_ref[4 * q : 4 * q + 4, :]
+        field[q, 12 + height : 16 + height, :] = top_ref[4 * q : 4 * q + 4, :]
         field[q, 0:8, :] = field[q, rows : rows + 8, :]
         field[q, 8 + rows : 16 + rows, :] = field[q, 8:16, :]
-    whole = jnp.concatenate([field[0, 8 : 8 + rows], field[1, 8 : 8 + rows]], axis=0)
-    pieces = [pltpu.roll(whole, 1, 1), whole, pltpu.roll(whole, lanes - 1, 1)]
-    depth = w1_ref.shape[1]
-    pieces.append(jnp.zeros((depth - 6 * rows, lanes), f32))
-    turned = jnp.concatenate(pieces, axis=0).T
-    patches = jnp.concatenate([turned[: breadth + 8], turned[lanes - 8 :]], axis=0).astype(bf16)
-    span = breadth + 16
-    for r in range(groups):
-        first[r] = jnp.maximum(dot(patches, w1_ref[r]) + b1_ref[...], 0.0).astype(bf16)
-
-    def gathered(source, r):
-        before, after = (r - 1) % groups, (r + 1) % groups
-        beside = jnp.concatenate([source[before, :, 128:], source[after, :, :128]], axis=1)
-        return source[r], beside
-
-    for r in range(groups):
-        own, beside = gathered(first, r)
-        total = dot(own, w2_ref[:256]) + dot(beside, w2_ref[256:])
-        total = pltpu.roll(total[:, :256], 1, 0) + total[:, 256:512] + pltpu.roll(total[:, 512:], span - 1, 0)
-        second[r] = jnp.maximum(total + b2_ref[...], 0.0).astype(bf16)
-
-    def last(r, ref):
-        own, beside = gathered(second, r)
-        total = dot(own, ref[:256]) + dot(beside, ref[256:])
-        left_part = total[:, :128]
-        return pltpu.roll(left_part, 1, 0) + pltpu.roll(left_part, 64, 1) + pltpu.roll(total[:, 128:], span - 1, 0)
-
-    def keep(r, block):
-        coeff[r, :, :breadth] = block[:, :breadth]
-        coeff[r, :, breadth:] = block[:, breadth:]
-
-    pairs = [(i, i + 1) for i in range(0, groups - 2, 2)] + [(groups - 1, None)]
-    for even, odd in pairs:
-        block = last(even, w3e_ref)
-        if odd is not None:
-            other = last(odd, w3o_ref)
-            lower = lax.broadcasted_iota(jnp.int32, block.shape, 1) < 64
-            block = jnp.where(lower, block, other)
-        block = jnp.concatenate(
-            [block[: breadth + 8], jnp.zeros((lanes - span, 128), f32), block[breadth + 8 :]], axis=0
-        ).T
-        keep(even, block[:64])
-        if odd is not None:
-            keep(odd, block[64:])
+    patches = patches_of(field, rows, w1_ref.shape[1])
+
+    ends = (groups - 3, groups - 2, groups - 1, 0, 1, groups - 4)
+
+    def first(r):
+        return outer_first.at[ends.index(r)] if r in ends[:4] else first_ref.at[r - 1]
+
+    def second(r):
+        return outer_second.at[ends.index(r)] if r in ends else second_ref.at[r - 2]
+
+    held = {3: coeff_ref.at[0], 4: coeff_ref.at[1]}
+
+    def do_first(r):
+        outer_first[ends.index(r)] = layer_1(patches, w1_ref, b1_ref, r)
+
+    def do_second(r):
+        outer_second[ends.index(r)] = layer_2(
+            first((r - 1) % groups), first(r), first((r + 1) % groups), w2_ref, b2_ref
+        )
+
+    def do_coefficients(even, odd):
+        block = coefficients(second, groups, even, odd, even_ref, odd_ref)
+        for r, part in ((even, block[:64]), (odd, block[64:])):
+            if r is not None:
+                place = len(held)
+                outer_coeff[place - 2] = part
+                held[r] = outer_coeff.at[place - 2]
 
     offsets = b3_ref[...]
     sub = lax.broadcasted_iota(jnp.int32, (8, breadth), 0) % 4
@@ -210,9 +262,8 @@
         start = 8 + 4 * r + shift
         return jnp.concatenate([field[q, start : start + 4, :] for q in qs], axis=0)
 
-    previous = None
-    for r in [groups - 1] + list(range(groups - 2)):
-        weights = coeff[r] + offsets
+    def flows(r, previous):
+        weights = held[r][...] + offsets
         weights = [weights[8 * i : 8 * i + 8] for i in range(8)]
         centre = stacked(r, 0)
 
@@ -242,7 +293,26 @@
             star = centre[:, :breadth] - step_ratio * (flow_x - above + change_y)
             star_ref[4 * r : 4 * r + 4, :] = star[:4]
             star_ref[height + 4 * r : height + 4 * r + 4, :] = star[4:]
-        previous = flow_x
+        return flow_x
+
+    for r in ends[:4]:
+        do_first(r)
+    for r in ends[1:5]:
+        do_second(r)
+    do_coefficients(groups - 1, None)
+    do_coefficients(0, 1)
+    do_second(groups - 4)
+    previous = flows(groups - 1, None)
+    previous = flows(0, previous)
+    previous = flows(1, previous)
+    inner = list(range(5, groups - 4))
+    do_coefficients(2, inner[0])
+    do_second(groups - 3)
+    for r in range(2, 5):
+        previous = flows(r, previous)
+    do_coefficients(groups - 4, groups - 3)
+    for r in range(5, groups - 2):
+        previous = flows(r, previous)
 
 
 def own_twiddle(ref):
@@ -387,12 +457,12 @@
         peers = lax.axis_size(axis)
         return lax.ppermute(value, axis, [(i, (i + distance) % peers) for i in range(peers)])
 
-    with jax.named_scope("rows_around"):
+    with jax.named_scope("columns_around"):
         component = lax.broadcasted_iota(jnp.int32, (2, height, breadth), 0)
         both = jnp.where(component == 0, u_field[None], v_field[None]).reshape(2 * height, breadth)
-        edge = shape((8, breadth), f32)
-        last, first = call(rows_kernel, (edge, edge))(both)
-        top, bottom = shifted(last, "gx", 1), shifted(first, "gx", -1)
+        edge = shape((8, 128), f32)
+        last, first = call(columns_kernel, (edge, edge), (pltpu.VMEM((128, 128), f32),))(both)
+        left, right = shifted(last, "gy", 1), shifted(first, "gy", -1)
 
     with jax.named_scope("weights"):
         biases = jnp.stack([b_first, b_second, jnp.pad(b_third, (0, 64 - b_third.shape[0]))])
@@ -406,34 +476,43 @@
                 shape((64, 1), f32),
             ),
         )(packed)
-
-    with jax.named_scope("columns_around"):
-        edge = shape((8, 128), f32)
-        last, first = call(columns_kernel, (edge, edge), (pltpu.VMEM((128, 128), f32),))(
-            both, bottom, top, biases[2]
-        )
-        left, right = shifted(last, "gy", 1), shifted(first, "gy", -1)
-
-    with jax.named_scope("weights"):
         packed = jnp.concatenate([w_second.reshape(576, 64), w_third.reshape(144, 64)], axis=0)
-        others = call(
-            other_weights_kernel, (shape((512, 768), bf16), shape((512, 256), bf16), shape((512, 256), bf16))
+        *others, order = call(
+            other_weights_kernel,
+            (shape((512, 768), bf16), shape((512, 256), bf16), shape((512, 256), bf16), shape((8, 128), f32)),
         )(packed)
 
+    with jax.named_scope("rows_around"):
+        edge = shape((8, breadth + 128), f32)
+        last, first, beside = call(
+            rows_kernel, (edge, edge, shape((2 * height, 128), f32)), (pltpu.VMEM((128, 128), f32),)
+        )(both, right, left, biases[2], order)
+        top, bottom = shifted(last, "gx", 1), shifted(first, "gx", -1)
+
     block = shape((2 * height, breadth), f32)
+    padded = pltpu.VMEM((2, rows + 16, breadth + 128), f32)
     with jax.named_scope("advance"):
+        inner = call(
+            inner_kernel,
+            (
+                shape((groups - 4, span, 256), bf16),
+                shape((groups - 6, span, 256), bf16),
+                shape((2, 64, breadth + 128), f32),
+            ),
+            (padded,),
+            flops=5 * 10**8,
+        )(both, beside, kernel_1, *others, *biases[:2])
         star = call(
             advance_kernel,
             block,
             (
-                pltpu.VMEM((2, rows + 16, breadth + 128), f32),
-                pltpu.VMEM((groups, span, 256), bf16),
-                pltpu.VMEM((groups, span, 256), bf16),
-                pltpu.VMEM((groups, 64, breadth + 128), f32),
-                pltpu.VMEM((128, 128), f32),
+                padded,
+                pltpu.VMEM((4, span, 256), bf16),
+                pltpu.VMEM((6, span, 256), bf16),
+                pltpu.VMEM((groups - 3, 64, breadth + 128), f32),
             ),
             flops=10**9,
-        )(both, bottom, top, right, left, kernel_1, *others, *biases)
+        )(both, beside, bottom, top, kernel_1, *others, *biases, *inner)
 
     column, row, twiddle_out, twiddle_home = tables(height, breadth, members_x, members_y)
     column, row = [[jnp.asarray(t) for t in pair] for pair in (column, row)]

time: 46.9 us -> 45 us (0.959)
  waiting for transfers between devices: 15.2 us -> 13.5 us
  starting transfers between devices: 19.1 us -> 18.1 us
  Pallas kernels: 7.58 us -> 8.26 us
    ppermute x4, waiting for transfers between devices: 5.55 us -> 3.47 us  [shifted(): lax.ppermute(value, axis, [(i, (i + distance) % peers) for i in range(pee...]
    ppermute x4, starting transfers between devices: 7.05 us -> 6.1 us  [shifted(): lax.ppermute(value, axis, [(i, (i + distance) % peers) for i in range(pee...]
    pallas_call x3 -> x4, Pallas kernels: 4.54 us -> 5.21 us  [the longest x1 2.94 us: on_device(): call(advance_kernel, block, (padded, pltpu.VMEM((4, span, 256), bf16), pl...]
  transfers between devices with their start and end apart: 17 -> 17, of which waited for: 12 -> 13; matrix products, arithmetic and copies ran while one was open for 6% -> 7% of each run, Pallas kernels for 2% -> 6%
where the time goes in v3:
time: 45 us; the launch traced here: 44.7 us
  starting transfers between devices  18.1 us (40%)
  waiting for transfers between devices  13.5 us (30%)
  Pallas kernels  8.26 us (18%)
  other arithmetic  3.2 us (7%)
  local copies, waits for them, and re-layouts  0.86 us (2%)
  between operations  0.75 us (2%)
    ppermute x13, starting transfers between devices, partner(): lax.ppermute(block, axis, [(i, i ^ k) for i in range(lax.axis_size(axis))])  12 us
    ppermute x13, waiting for transfers between devices, partner(): lax.ppermute(block, axis, [(i, i ^ k) for i in range(lax.axis_size(axis))])  10.1 us
    ppermute x4, starting transfers between devices, shifted(): lax.ppermute(value, axis, [(i, (i + distance) % peers) for i in range(pee...  6.1 us
    ppermute x4, waiting for transfers between devices, shifted(): lax.ppermute(value, axis, [(i, (i + distance) % peers) for i in range(pee...  3.47 us
    pallas_call x1, Pallas kernels, on_device(): call(advance_kernel, block, (padded, pltpu.VMEM((4, span, 256), bf16), pl...  2.94 us
    pallas_call x1, Pallas kernels, on_device(): call(inner_kernel, (shape((groups - 4, span, 256), bf16), shape((groups -...  2.12 us
    pallas_call x1, Pallas kernels, on_device(): call(functools.partial(row_kernel, scale=1.0 / (grid_x * grid_y)), block,...  1.38 us
    concatenate x1, other arithmetic, on_device(): jnp.concatenate([w_second.reshape(576, 64), w_third.reshape(144, 64)], ax...  0.97 us
  transfers between devices with their start and end apart: 17, of which 13 were waited for; matrix products, arithmetic and copies ran while one was open for 7% of the time, Pallas kernels for 6%

profile of v3, /device:TPU:0, one launch (start us, length us, event | category | flops | bytes accessed | tf_op | source)
XLA Modules:
  0.0 44.7 jit_solution(7343329806207784850)
XLA Ops:
  0.8 0.8 %bitcast_select_fusion.both_ref = f32[64,256]{1,0:T(8,128)S(1)} fusion(f32[32,256]{1,0:T(8,128)} %param.15, f32[32,256]{1,0:T(8,128)} %param.14, pred[64]{0:T(512)(128)(4,1)S(1)} %iota.12), kind=kLoop, calls=%fused_computation.1 | loop fusion | flops 16384 | bytes 131136 | tf_op jit(solution)/shard_map/columns_around/jit(_where)/select_n | solution.py:462
  1.7 3.9 %collective-permute-start = (f32[8,128]{1,0:T(8,128)S(1)}, f32[8,128]{1,0:T(8,128)S(1)}, u32[]{:S(2)}, u32[]{:S(2)}) collective-permute-start(f32[8,128]{1,0:T(8,128)S(1)} %get-tuple-element.18), channel_id=1, source_target_pairs={{0,3},{1,0},{2,1},{3,2},{4,7},{5,4},{6,5},{7,6},{8,11},{9,8},{10,9... | collective-permute-start | bytes 12296 | tf_op jit(solution)/shard_map/columns_around/ppermute | solution.py:458
  5.7 0.7 %pad_bitcast_fusion = f32[1,64]{1,0:T(1,128)S(1)} fusion(f32[16]{0:T(128)} %param.21), kind=kLoop, calls=%fused_computation.4 | loop fusion | bytes 320 | tf_op jit(solution)/shard_map/weights/stack | solution.py:468
  6.3 0.7 %convert_bitcast_fusion = f32[9,2,64]{2,1,0:T(2,128)S(1)} fusion(bf16[9,64,2]{1,2,0:T(2,128)(2,1)} %param.16), kind=kLoop, calls=%fused_computation.3 | loop fusion | flops 1152 | bytes 6912 | tf_op jit(solution)/shard_map/weights/convert_element_type | solution.py:469
  7.0 1.0 %pad_maximum_fusion.packed_ref = bf16[720,64]{1,0:T(8,128)(2,1)S(1)} fusion(bf16[144,64]{1,0:T(8,128)(2,1)} %bitcast.13, bf16[576,64]{1,0:T(8,128)(2,1)} %bitcast.12), kind=kLoop, calls=%fused_computation | loop fusion | flops 184320 | bytes 184320 | tf_op jit(solution)/shard_map/weights/concatenate | solution.py:479
  8.0 0.7 %pad_maximum_fusion.1.packed_ref = f32[21,64]{1,0:T(8,128)S(1)} fusion(f32[1,64]{1,0:T(1,128)S(1)} %pad_bitcast_fusion, f32[1,64]{1,0:T(1,128)} %bitcast.14, f32[1,64]{1,0:T(1,128)} %bitcast.15, f32[18,64]{1,0:T(8,128)S(1)} %reshape.21), kind=kLoop, calls=%fused_computation.2 | loop fusion | flops 4032 | bytes 10752 | tf_op jit(solution)/shard_map/weights/concatenate | solution.py:469
  9.5 0.7 %collective-permute-done.1.left_ref = f32[8,128]{1,0:T(8,128)S(1)} collective-permute-done((f32[8,128]{1,0:T(8,128)S(1)}, f32[8,128]{1,0:T(8,128)S(1)}, u32[]{:S(2)}, u32[]{:S(2)}) %collective-permute-start.1) | collective-permute-done | bytes 4128 | tf_op jit(solution)/shard_map/columns_around/ppermute | solution.py:458
  10.3 2.1 %collective-permute-start.2 = (f32[8,384]{1,0:T(8,128)S(1)}, f32[8,384]{1,0:T(8,128)S(1)}, u32[]{:S(2)}, u32[]{:S(2)}) collective-permute-start(f32[8,384]{1,0:T(8,128)S(1)} %get-tuple-element.23), channel_id=1, source_target_pairs={{0,28},{4,0},{8,4},{12,8},{16,12},{20,16},{24,20},{28,24},{1,29},{... | collective-permute-start | bytes 36872 | tf_op jit(solution)/shard_map/rows_around/ppermute | solution.py:458
  12.4 2.1 %advance.2 = (bf16[6,272,256]{2,1,0:T(8,128)(2,1)S(1)}, bf16[4,272,256]{2,1,0:T(8,128)(2,1)S(1)}, f32[2,64,384]{2,1,0:T(8,128)S(1)}) custom-call(f32[64,256]{1,0:T(8,128)S(1)} %bitcast_select_fusion.both_ref, f32[64,128]{1,0:T(8,128)S(1)} %get-tuple-element.22.beside_ref, bf16[10,256,256]{2,1,0:T(8,128)(2,1)S(1)} %get-tuple-element.25.w1_ref, ...), custom_call_target="tpu_custom_call" | custom-call | flops 500000000 | bytes 1048576 | tf_op jit(solution)/shard_map/advance/pallas_call | solution.py:495
  14.6 2.8 %collective-permute-done.3.top_ref = f32[8,384]{1,0:T(8,128)S(1)} collective-permute-done((f32[8,384]{1,0:T(8,128)S(1)}, f32[8,384]{1,0:T(8,128)S(1)}, u32[]{:S(2)}, u32[]{:S(2)}) %collective-permute-start.3) | collective-permute-done | bytes 12320 | tf_op jit(solution)/shard_map/rows_around/ppermute | solution.py:458
  17.4 2.9 %advance.3.refs_0_.refs_5_ = f32[64,256]{1,0:T(8,128)S(1)} custom-call(f32[64,256]{1,0:T(8,128)S(1)} %bitcast_select_fusion.both_ref, f32[64,128]{1,0:T(8,128)S(1)} %get-tuple-element.22.beside_ref, f32[8,384]{1,0:T(8,128)S(1)} %collective-permute-done.2.bot_ref, f32[8,384]{1,0:T(8,128)S(1)} %collective-permute-done.3.top_ref, ...), custom_call_target="tpu_custom_call" | custom-call | flops 1000000000 | bytes 1048576 | tf_op jit(solution)/shard_map/advance/pallas_call | solution.py:505
  20.3 2.7 %collective-permute-start.6 = (f32[64,256]{1,0:T(8,128)S(1)}, f32[64,256]{1,0:T(8,128)S(1)}, u32[]{:S(2)}, u32[]{:S(2)}) collective-permute-start(f32[64,256]{1,0:T(8,128)S(1)} %advance.3.refs_0_.refs_5_), channel_id=1, source_target_pairs={{0,3},{1,2},{2,1},{3,0},{4,7},{5,6},{6,5},{7,4},{8,11},{9,10},{10,... | collective-permute-start | bytes 196616 | tf_op jit(solution)/shard_map/ppermute | solution.py:435
  23.8 1.7 %collective-permute-done.6.refs_3_ = f32[64,256]{1,0:T(8,128)S(1)} collective-permute-done((f32[64,256]{1,0:T(8,128)S(1)}, f32[64,256]{1,0:T(8,128)S(1)}, u32[]{:S(2)}, u32[]{:S(2)}) %collective-permute-start.6) | collective-permute-done | bytes 65568 | tf_op jit(solution)/shard_map/ppermute | solution.py:435
  25.5 1.7 %collective-permute-done.5.refs_2_ = f32[64,256]{1,0:T(8,128)S(1)} collective-permute-done((f32[64,256]{1,0:T(8,128)S(1)}, f32[64,256]{1,0:T(8,128)S(1)}, u32[]{:S(2)}, u32[]{:S(2)}) %collective-permute-start.5) | collective-permute-done | bytes 65568 | tf_op jit(solution)/shard_map/ppermute | solution.py:435
  28.2 4.3 %collective-permute-start.8 = (f32[64,256]{1,0:T(8,128)S(1)}, f32[64,256]{1,0:T(8,128)S(1)}, u32[]{:S(2)}, u32[]{:S(2)}) collective-permute-start(f32[64,256]{1,0:T(8,128)S(1)} %shard_map.149.refs_0_), channel_id=1, source_target_pairs={{0,8},{4,12},{8,0},{12,4},{16,24},{20,28},{24,16},{28,20},{1,9},{5... | collective-permute-start | bytes 196616 | tf_op jit(solution)/shard_map/ppermute | solution.py:435
  32.5 1.7 %collective-permute-done.12.refs_6_ = f32[64,256]{1,0:T(8,128)S(1)} collective-permute-done((f32[64,256]{1,0:T(8,128)S(1)}, f32[64,256]{1,0:T(8,128)S(1)}, u32[]{:S(2)}, u32[]{:S(2)}) %collective-permute-start.12) | collective-permute-done | bytes 65568 | tf_op jit(solution)/shard_map/ppermute | solution.py:435
  34.9 0.6 %collective-permute-done.13.refs_7_ = f32[64,256]{1,0:T(8,128)S(1)} collective-permute-done((f32[64,256]{1,0:T(8,128)S(1)}, f32[64,256]{1,0:T(8,128)S(1)}, u32[]{:S(2)}, u32[]{:S(2)}) %collective-permute-start.13) | collective-permute-done | bytes 65568 | tf_op jit(solution)/shard_map/ppermute | solution.py:435
  36.1 1.4 %shard_map.150.refs_0_ = f32[64,256]{1,0:T(8,128)S(1)} custom-call(f32[64,256]{1,0:T(8,128)S(1)} %shard_map.149.refs_0_, f32[64,256]{1,0:T(8,128)S(1)} %collective-permute-done.7.refs_1_, f32[64,256]{1,0:T(8,128)S(1)} %collective-permute-done.8.refs_2_, f32[64,256]{1,0:T(8,128)S(1)} %collective-permute-done.9.refs_3_, ...), custom_call_target="tpu_custom_call" | custom-call | flops 10000000 | bytes 1048576 | tf_op jit(solution)/shard_map/pallas_call | solution.py:520
  37.5 1.3 %collective-permute-start.16 = (f32[64,256]{1,0:T(8,128)S(1)}, f32[64,256]{1,0:T(8,128)S(1)}, u32[]{:S(2)}, u32[]{:S(2)}) collective-permute-start(f32[64,256]{1,0:T(8,128)S(1)} %shard_map.150.refs_0_), channel_id=1, source_target_pairs={{0,3},{1,2},{2,1},{3,0},{4,7},{5,6},{6,5},{7,4},{8,11},{9,10},{10,... | collective-permute-start | bytes 196616 | tf_op jit(solution)/shard_map/ppermute | solution.py:435
  38.8 0.8 %collective-permute-start.15 = (f32[64,256]{1,0:T(8,128)S(1)}, f32[64,256]{1,0:T(8,128)S(1)}, u32[]{:S(2)}, u32[]{:S(2)}) collective-permute-start(f32[64,256]{1,0:T(8,128)S(1)} %shard_map.150.refs_0_), channel_id=1, source_target_pairs={{0,2},{1,3},{2,0},{3,1},{4,6},{5,7},{6,4},{7,5},{8,10},{9,11},{10,... | collective-permute-start | bytes 196616 | tf_op jit(solution)/shard_map/ppermute | solution.py:435
  39.6 1.4 %collective-permute-start.14 = (f32[64,256]{1,0:T(8,128)S(1)}, f32[64,256]{1,0:T(8,128)S(1)}, u32[]{:S(2)}, u32[]{:S(2)}) collective-permute-start(f32[64,256]{1,0:T(8,128)S(1)} %shard_map.150.refs_0_), channel_id=1, source_target_pairs={{0,1},{1,0},{2,3},{3,2},{4,5},{5,4},{6,7},{7,6},{8,9},{9,8},{10,11... | collective-permute-start | bytes 196616 | tf_op jit(solution)/shard_map/ppermute | solution.py:435
  41.1 2.0 %collective-permute-done.16.refs_3_ = f32[64,256]{1,0:T(8,128)S(1)} collective-permute-done((f32[64,256]{1,0:T(8,128)S(1)}, f32[64,256]{1,0:T(8,128)S(1)}, u32[]{:S(2)}, u32[]{:S(2)}) %collective-permute-start.16) | collective-permute-done | bytes 65568 | tf_op jit(solution)/shard_map/ppermute | solution.py:435
  43.1 0.9 %collective-permute-done.15.refs_2_ = f32[64,256]{1,0:T(8,128)S(1)} collective-permute-done((f32[64,256]{1,0:T(8,128)S(1)}, f32[64,256]{1,0:T(8,128)S(1)}, u32[]{:S(2)}, u32[]{:S(2)}) %collective-permute-start.15) | collective-permute-done | bytes 65568 | tf_op jit(solution)/shard_map/ppermute | solution.py:435
  44.1 0.7 %shard_map.151 = (f32[32,256]{1,0:T(8,128)}, f32[32,256]{1,0:T(8,128)}) custom-call(f32[64,256]{1,0:T(8,128)S(1)} %shard_map.150.refs_0_, f32[64,256]{1,0:T(8,128)S(1)} %collective-permute-done.14.refs_1_, f32[64,256]{1,0:T(8,128)S(1)} %collective-permute-done.15.refs_2_, f32[64,256]{1,0:T(8,128)S(1)} %collective-permute-done.16.refs_3_, ...), custom_call_target="tpu_custom_call" | custom-call | flops 10000000 | bytes 1048576 | tf_op jit(solution)/shard_map/pallas_call | solution.py:526
  (40 shorter events, 4.3 us)
Async XLA Ops:
  1.7 7.8 %collective-permute-start = (f32[8,128]{1,0:T(8,128)S(1)}, f32[8,128]{1,0:T(8,128)S(1)}, u32[]{:S(2)}, u32[]{:S(2)}) collective-permute-start(f32[8,128]{1,0:T(8,128)S(1)} %get-tuple-element.18), channel_id=1, source_target_pairs={{0,3},{1,0},{2,1},{3,2},{4,7},{5,4},{6,5},{7,6},{8,11},{9,8},{10,9... | collective-permute-start | bytes 12296 | tf_op jit(solution)/shard_map/columns_around/ppermute | solution.py:458
  5.7 4.5 %collective-permute-start.1 = (f32[8,128]{1,0:T(8,128)S(1)}, f32[8,128]{1,0:T(8,128)S(1)}, u32[]{:S(2)}, u32[]{:S(2)}) collective-permute-start(f32[8,128]{1,0:T(8,128)S(1)} %get-tuple-element.19), channel_id=1, source_target_pairs={{0,1},{1,2},{2,3},{3,0},{4,5},{5,6},{6,7},{7,4},{8,9},{9,10},{10,1... | collective-permute-start | bytes 12296 | tf_op jit(solution)/shard_map/columns_around/ppermute | solution.py:458
  10.3 4.3 %collective-permute-start.2 = (f32[8,384]{1,0:T(8,128)S(1)}, f32[8,384]{1,0:T(8,128)S(1)}, u32[]{:S(2)}, u32[]{:S(2)}) collective-permute-start(f32[8,384]{1,0:T(8,128)S(1)} %get-tuple-element.23), channel_id=1, source_target_pairs={{0,28},{4,0},{8,4},{12,8},{16,12},{20,16},{24,20},{28,24},{1,29},{... | collective-permute-start | bytes 36872 | tf_op jit(solution)/shard_map/rows_around/ppermute | solution.py:458
  12.4 4.9 %collective-permute-start.3 = (f32[8,384]{1,0:T(8,128)S(1)}, f32[8,384]{1,0:T(8,128)S(1)}, u32[]{:S(2)}, u32[]{:S(2)}) collective-permute-start(f32[8,384]{1,0:T(8,128)S(1)} %get-tuple-element.24), channel_id=1, source_target_pairs={{0,4},{4,8},{8,12},{12,16},{16,20},{20,24},{24,28},{28,0},{1,5},{5... | collective-permute-start | bytes 36872 | tf_op jit(solution)/shard_map/rows_around/ppermute | solution.py:458
  17.3 10.4 %copy-start = (bf16[256,512]{1,0:T(8,128)(2,1)S(1)}, bf16[256,512]{1,0:T(8,128)(2,1)}, u32[]{:S(2)}) copy-start(bf16[256,512]{1,0:T(8,128)(2,1)} %constant.18.clone.refs_6_.refs_11_) | copy-start | bytes 786436
  17.3 10.4 %copy-start.1 = (bf16[256,512]{1,0:T(8,128)(2,1)S(1)}, bf16[256,512]{1,0:T(8,128)(2,1)}, u32[]{:S(2)}) copy-start(bf16[256,512]{1,0:T(8,128)(2,1)} %constant.17.clone.refs_5_.refs_10_) | copy-start | bytes 786436
  17.3 10.4 %copy-start.4 = (f32[4,8,256]{2,1,0:T(8,128)S(1)}, f32[4,8,256]{2,1,0:T(8,128)}, u32[]{:S(2)}) copy-start(f32[4,8,256]{2,1,0:T(8,128)} %constant.21.clone.refs_4_) | copy-start | bytes 98308
  17.3 18.8 %copy-start.2 = (bf16[512,256]{1,0:T(8,128)(2,1)S(1)}, bf16[512,256]{1,0:T(8,128)(2,1)}, u32[]{:S(2)}) copy-start(bf16[512,256]{1,0:T(8,128)(2,1)} %constant.20.clone.refs_9_) | copy-start | bytes 786436
  17.3 18.8 %copy-start.3 = (bf16[512,256]{1,0:T(8,128)(2,1)S(1)}, bf16[512,256]{1,0:T(8,128)(2,1)}, u32[]{:S(2)}) copy-start(bf16[512,256]{1,0:T(8,128)(2,1)} %constant.19.clone.refs_8_) | copy-start | bytes 786436
  20.3 23.8 %copy-start.5 = (f32[4,8,256]{2,1,0:T(8,128)S(1)}, f32[4,8,256]{2,1,0:T(8,128)}, u32[]{:S(2)}) copy-start(f32[4,8,256]{2,1,0:T(8,128)} %constant.22.clone.refs_4_) | copy-start | bytes 98308
  20.3 5.2 %collective-permute-start.6 = (f32[64,256]{1,0:T(8,128)S(1)}, f32[64,256]{1,0:T(8,128)S(1)}, u32[]{:S(2)}, u32[]{:S(2)}) collective-permute-start(f32[64,256]{1,0:T(8,128)S(1)} %advance.3.refs_0_.refs_5_), channel_id=1, source_target_pairs={{0,3},{1,2},{2,1},{3,0},{4,7},{5,6},{6,5},{7,4},{8,11},{9,10},{10,... | collective-permute-start | bytes 196616 | tf_op jit(solution)/shard_map/ppermute | solution.py:435
  23.0 4.3 %collective-permute-start.5 = (f32[64,256]{1,0:T(8,128)S(1)}, f32[64,256]{1,0:T(8,128)S(1)}, u32[]{:S(2)}, u32[]{:S(2)}) collective-permute-start(f32[64,256]{1,0:T(8,128)S(1)} %advance.3.refs_0_.refs_5_), channel_id=1, source_target_pairs={{0,2},{1,3},{2,0},{3,1},{4,6},{5,7},{6,4},{7,5},{8,10},{9,11},{10,... | collective-permute-start | bytes 196616 | tf_op jit(solution)/shard_map/ppermute | solution.py:435
  23.5 4.3 %collective-permute-start.4 = (f32[64,256]{1,0:T(8,128)S(1)}, f32[64,256]{1,0:T(8,128)S(1)}, u32[]{:S(2)}, u32[]{:S(2)}) collective-permute-start(f32[64,256]{1,0:T(8,128)S(1)} %advance.3.refs_0_.refs_5_), channel_id=1, source_target_pairs={{0,1},{1,0},{2,3},{3,2},{4,5},{5,4},{6,7},{7,6},{8,9},{9,8},{10,11... | collective-permute-start | bytes 196616 | tf_op jit(solution)/shard_map/ppermute | solution.py:435
  28.0 6.1 %collective-permute-start.12 = (f32[64,256]{1,0:T(8,128)S(1)}, f32[64,256]{1,0:T(8,128)S(1)}, u32[]{:S(2)}, u32[]{:S(2)}) collective-permute-start(f32[64,256]{1,0:T(8,128)S(1)} %shard_map.149.refs_0_), channel_id=1, source_target_pairs={{0,24},{4,28},{8,16},{12,20},{16,8},{20,12},{24,0},{28,4},{1,25},{... | collective-permute-start | bytes 196616 | tf_op jit(solution)/shard_map/ppermute | solution.py:435
  28.1 6.1 %collective-permute-start.10 = (f32[64,256]{1,0:T(8,128)S(1)}, f32[64,256]{1,0:T(8,128)S(1)}, u32[]{:S(2)}, u32[]{:S(2)}) collective-permute-start(f32[64,256]{1,0:T(8,128)S(1)} %shard_map.149.refs_0_), channel_id=1, source_target_pairs={{0,16},{4,20},{8,24},{12,28},{16,0},{20,4},{24,8},{28,12},{1,17},{... | collective-permute-start | bytes 196616 | tf_op jit(solution)/shard_map/ppermute | solution.py:435
  28.2 6.7 %collective-permute-start.8 = (f32[64,256]{1,0:T(8,128)S(1)}, f32[64,256]{1,0:T(8,128)S(1)}, u32[]{:S(2)}, u32[]{:S(2)}) collective-permute-start(f32[64,256]{1,0:T(8,128)S(1)} %shard_map.149.refs_0_), channel_id=1, source_target_pairs={{0,8},{4,12},{8,0},{12,4},{16,24},{20,28},{24,16},{28,20},{1,9},{5... | collective-permute-start | bytes 196616 | tf_op jit(solution)/shard_map/ppermute | solution.py:435
  32.5 2.4 %collective-permute-start.7 = (f32[64,256]{1,0:T(8,128)S(1)}, f32[64,256]{1,0:T(8,128)S(1)}, u32[]{:S(2)}, u32[]{:S(2)}) collective-permute-start(f32[64,256]{1,0:T(8,128)S(1)} %shard_map.149.refs_0_), channel_id=1, source_target_pairs={{0,4},{4,0},{8,12},{12,8},{16,20},{20,16},{24,28},{28,24},{1,5},{5... | collective-permute-start | bytes 196616 | tf_op jit(solution)/shard_map/ppermute | solution.py:435
  34.2 1.3 %collective-permute-start.13 = (f32[64,256]{1,0:T(8,128)S(1)}, f32[64,256]{1,0:T(8,128)S(1)}, u32[]{:S(2)}, u32[]{:S(2)}) collective-permute-start(f32[64,256]{1,0:T(8,128)S(1)} %collective-permute-done.12.refs_6_), channel_id=1, source_target_pairs={{0,4},{4,0},{8,12},{12,8},{16,20},{20,16},{24,28},{28,24},{1,5},{5... | collective-permute-start | bytes 196616 | tf_op jit(solution)/shard_map/ppermute | solution.py:435
  34.2 1.4 %collective-permute-start.11 = (f32[64,256]{1,0:T(8,128)S(1)}, f32[64,256]{1,0:T(8,128)S(1)}, u32[]{:S(2)}, u32[]{:S(2)}) collective-permute-start(f32[64,256]{1,0:T(8,128)S(1)} %collective-permute-done.10.refs_4_), channel_id=1, source_target_pairs={{0,4},{4,0},{8,12},{12,8},{16,20},{20,16},{24,28},{28,24},{1,5},{5... | collective-permute-start | bytes 196616 | tf_op jit(solution)/shard_map/ppermute | solution.py:435
  34.8 1.3 %collective-permute-start.9 = (f32[64,256]{1,0:T(8,128)S(1)}, f32[64,256]{1,0:T(8,128)S(1)}, u32[]{:S(2)}, u32[]{:S(2)}) collective-permute-start(f32[64,256]{1,0:T(8,128)S(1)} %collective-permute-done.8.refs_2_), channel_id=1, source_target_pairs={{0,4},{4,0},{8,12},{12,8},{16,20},{20,16},{24,28},{28,24},{1,5},{5... | collective-permute-start | bytes 196616 | tf_op jit(solution)/shard_map/ppermute | solution.py:435
  37.5 5.6 %collective-permute-start.16 = (f32[64,256]{1,0:T(8,128)S(1)}, f32[64,256]{1,0:T(8,128)S(1)}, u32[]{:S(2)}, u32[]{:S(2)}) collective-permute-start(f32[64,256]{1,0:T(8,128)S(1)} %shard_map.150.refs_0_), channel_id=1, source_target_pairs={{0,3},{1,2},{2,1},{3,0},{4,7},{5,6},{6,5},{7,4},{8,11},{9,10},{10,... | collective-permute-start | bytes 196616 | tf_op jit(solution)/shard_map/ppermute | solution.py:435
  38.8 5.2 %collective-permute-start.15 = (f32[64,256]{1,0:T(8,128)S(1)}, f32[64,256]{1,0:T(8,128)S(1)}, u32[]{:S(2)}, u32[]{:S(2)}) collective-permute-start(f32[64,256]{1,0:T(8,128)S(1)} %shard_map.150.refs_0_), channel_id=1, source_target_pairs={{0,2},{1,3},{2,0},{3,1},{4,6},{5,7},{6,4},{7,5},{8,10},{9,11},{10,... | collective-permute-start | bytes 196616 | tf_op jit(solution)/shard_map/ppermute | solution.py:435
  39.6 4.4 %collective-permute-start.14 = (f32[64,256]{1,0:T(8,128)S(1)}, f32[64,256]{1,0:T(8,128)S(1)}, u32[]{:S(2)}, u32[]{:S(2)}) collective-permute-start(f32[64,256]{1,0:T(8,128)S(1)} %shard_map.150.refs_0_), channel_id=1, source_target_pairs={{0,1},{1,0},{2,3},{3,2},{4,5},{5,4},{6,7},{7,6},{8,9},{9,8},{10,11... | collective-permute-start | bytes 196616 | tf_op jit(solution)/shard_map/ppermute | solution.py:435

commit v4 on v3

--- a/solution.py
+++ b/solution.py
@@ -73,20 +73,19 @@
         first_ref[own, breadth:] = beside_ref[start : start + 4, :]
 
 
-def first_weights_kernel(packed_ref, k1_ref, c1_ref, c2_ref, c3_ref, *, rows):
+def first_weights_kernel(taps_ref, biases_ref, k1_ref, c1_ref, c2_ref, c3_ref, *, rows):
     groups, depth, _ = k1_ref.shape
-    packed = packed_ref[...]
-    wide = jnp.concatenate([packed] * 4, axis=1)
-    c1_ref[...] = wide[18:19]
-    c2_ref[...] = wide[19:20]
-    place = lax.broadcasted_iota(jnp.int32, (64, 64), 0) // 4
+    wide = [jnp.concatenate([taps_ref[i]] * 4, axis=1) for i in range(9)]
+    c1_ref[...] = jnp.concatenate([biases_ref[:, :64]] * 4, axis=1)
+    c2_ref[...] = jnp.concatenate([biases_ref[:, 64:128]] * 4, axis=1)
+    place = lax.broadcasted_iota(jnp.int32, (64, 16), 0) // 4
     channel = 8 * (place // 8) + 4 * (place % 2) + (place // 2) % 4
-    hit = channel == lax.broadcasted_iota(jnp.int32, (64, 64), 1)
-    c3_ref[...] = jnp.sum(jnp.where(hit, packed[20:21], 0.0), axis=1, keepdims=True)
+    hit = channel == lax.broadcasted_iota(jnp.int32, (64, 16), 1)
+    c3_ref[...] = jnp.sum(jnp.where(hit, biases_ref[:, 128:144], 0.0), axis=1, keepdims=True)
     spread = []
     for d in range(3):
         parts = [
-            jnp.broadcast_to(wide[(3 * d + s) * 2 + q : (3 * d + s) * 2 + q + 1, :], (rows, 256))
+            jnp.broadcast_to(wide[3 * d + s][q : q + 1, :], (rows, 256))
             for s in range(3)
             for q in range(2)
         ]
@@ -335,8 +334,28 @@
     out_ref[...] = spectra[:, :breadth] + sign * swap(spectra[:, breadth:])
 
 
-def row_kernel(*refs, scale):
-    *blocks, table_ref, table_low_ref, high_ref, low_ref, out_ref, gathered = refs
+def factors_kernel(out_ref, *, scale):
+    _, length, breadth = out_ref.shape
+    index = lax.broadcasted_iota(jnp.int32, (length, breadth), 0)
+    wave_x = jnp.where(index >= length // 2, index - length, index).astype(f32) * (2.0 * math.pi / length)
+    members_y = lax.axis_size("gy")
+    grid_y = members_y * breadth
+    number_y = lax.axis_index("gy") + members_y * lax.broadcasted_iota(jnp.int32, (1, breadth), 1)
+    wave_y = jnp.where(number_y >= grid_y // 2, number_y - grid_y, number_y).astype(f32) * (2.0 * math.pi / grid_y)
+    edge_y = number_y == grid_y // 2
+    edge_x = index == length // 2
+    total = wave_x * wave_x + wave_y * wave_y
+    zero = total == 0.0
+    inverse = scale / jnp.where(zero, 1.0, total)
+    same = (0.5 * inverse) * (wave_y * wave_y - wave_x * wave_x)
+    cross = jnp.where(edge_x != edge_y, 0.0, -inverse * wave_x * wave_y)
+    out_ref[0] = jnp.where(zero, 0.5 * scale, same)
+    out_ref[1] = jnp.where(zero, -0.5 * scale, same)
+    out_ref[2] = cross
+
+
+def row_kernel(*refs):
+    *blocks, factors_ref, table_ref, table_low_ref, high_ref, low_ref, out_ref, gathered = refs
     rows, breadth = out_ref.shape
     height = rows // 2
     length = len(blocks) * height
@@ -350,21 +369,7 @@
     spectra = dot(table_ref[...], data) + dot(table_ref[...], data_low) + dot(table_low_ref[...], data)
     real_part = spectra[:length, :breadth] + spectra[length:, breadth:]
     imag_part = spectra[:length, breadth:] - spectra[length:, :breadth]
-    index = lax.broadcasted_iota(jnp.int32, (length, breadth), 0)
-    wave_x = jnp.where(index >= length // 2, index - length, index).astype(f32) * (2.0 * math.pi / length)
-    members_y = lax.axis_size("gy")
-    grid_y = members_y * breadth
-    number_y = lax.axis_index("gy") + members_y * lax.broadcasted_iota(jnp.int32, (1, breadth), 1)
-    wave_y = jnp.where(number_y >= grid_y // 2, number_y - grid_y, number_y).astype(f32) * (2.0 * math.pi / grid_y)
-    edge_y = number_y == grid_y // 2
-    edge_x = index == length // 2
-    total = wave_x * wave_x + wave_y * wave_y
-    zero = total == 0.0
-    inverse = scale / jnp.where(zero, 1.0, total)
-    same = (0.5 * inverse) * (wave_y * wave_y - wave_x * wave_x)
-    cross = jnp.where(edge_x != edge_y, 0.0, -inverse * wave_x * wave_y)
-    same_real = jnp.where(zero, 0.5 * scale, same)
-    same_imag = jnp.where(zero, -0.5 * scale, same)
+    same_real, same_imag, cross = factors_ref[0], factors_ref[1], factors_ref[2]
     kept_real = same_real * real_part - cross * imag_part
     kept_imag = same_imag * imag_part + cross * real_part
     kept, kept_low = split(jnp.concatenate([kept_real, kept_imag], axis=1))
@@ -458,15 +463,14 @@
         return lax.ppermute(value, axis, [(i, (i + distance) % peers) for i in range(peers)])
 
     with jax.named_scope("columns_around"):
-        component = lax.broadcasted_iota(jnp.int32, (2, height, breadth), 0)
-        both = jnp.where(component == 0, u_field[None], v_field[None]).reshape(2 * height, breadth)
+        both = jnp.stack([u_field, v_field]).reshape(2 * height, breadth)
         edge = shape((8, 128), f32)
         last, first = call(columns_kernel, (edge, edge), (pltpu.VMEM((128, 128), f32),))(both)
         left, right = shifted(last, "gy", 1), shifted(first, "gy", -1)
 
     with jax.named_scope("weights"):
-        biases = jnp.stack([b_first, b_second, jnp.pad(b_third, (0, 64 - b_third.shape[0]))])
-        packed = jnp.concatenate([w_first.transpose(0, 2, 1).reshape(18, 64).astype(f32), biases], axis=0)
+        taps = w_first.transpose(0, 2, 1).astype(f32)
+        biases = jnp.concatenate([b_first, b_second, b_third])[None]
         kernel_1, *biases = call(
             functools.partial(first_weights_kernel, rows=rows),
             (
@@ -475,7 +479,7 @@
                 shape((1, 256), f32),
                 shape((64, 1), f32),
             ),
-        )(packed)
+        )(taps, biases)
         packed = jnp.concatenate([w_second.reshape(576, 64), w_third.reshape(144, 64)], axis=0)
         *others, order = call(
             other_weights_kernel,
@@ -517,11 +521,12 @@
     column, row, twiddle_out, twiddle_home = tables(height, breadth, members_x, members_y)
     column, row = [[jnp.asarray(t) for t in pair] for pair in (column, row)]
     spectra = call(column_kernel, block)(*gather_y(star), jnp.asarray(twiddle_out), *column)
-    columns = call(
-        functools.partial(row_kernel, scale=1.0 / (grid_x * grid_y)),
-        block,
-        (pltpu.VMEM((grid_x, 2 * breadth), f32),),
-    )(*gather_x(spectra), *row, *column)
+    factors = call(
+        functools.partial(factors_kernel, scale=1.0 / (grid_x * grid_y)), shape((3, grid_x, breadth), f32)
+    )()
+    columns = call(row_kernel, block, (pltpu.VMEM((grid_x, 2 * breadth), f32),))(
+        *gather_x(spectra), factors, *row, *column
+    )
     part = shape((height, breadth), f32)
     return tuple(call(home_kernel, (part, part))(*gather_y(columns), jnp.asarray(twiddle_home), star))
 

time: 45 us -> 44.5 us (0.989)
  waiting for transfers between devices: 13.5 us -> 15.3 us
  starting transfers between devices: 18.1 us -> 16.5 us
  local copies, waits for them, and re-layouts: 0.86 us -> 0.03 us
    ppermute x13, waiting for transfers between devices: 10.1 us -> 11.3 us  [partner(): lax.ppermute(block, axis, [(i, i ^ k) for i in range(lax.axis_size(axis))])]
    ppermute x13, starting transfers between devices: 12 us -> 10.9 us  [partner(): lax.ppermute(block, axis, [(i, i ^ k) for i in range(lax.axis_size(axis))])]
    select_n x1 -> x0, other arithmetic: 0.85 us -> none  [on_device(): jnp.where(component == 0, u_field[None], v_field[None])]
    another operation x0 -> x1, other arithmetic: none -> 0.78 us  [on_device(): both = jnp.stack([u_field, v_field]).reshape(2 * height, breadth)]
    another operation x1 -> x0, local copies, waits for them, and re-layouts: 0.66 us -> none  [on_device(): jnp.stack([b_first, b_second, jnp.pad(b_third, (0, 64 - b_third.shape[0]))])]
    ppermute x4, waiting for transfers between devices: 3.47 us -> 4.05 us  [shifted(): lax.ppermute(value, axis, [(i, (i + distance) % peers) for i in range(pee...]
    ppermute x4, starting transfers between devices: 6.1 us -> 5.62 us  [shifted(): lax.ppermute(value, axis, [(i, (i + distance) % peers) for i in range(pee...]
    pallas_call x1 -> x2, Pallas kernels: 1.38 us -> 1.53 us  [the longest x1 1.36 us: on_device(): call(row_kernel, block, (pltpu.VMEM((grid_x, 2 * breadth), f32),))]
  transfers between devices with their start and end apart: 17 -> 17, of which waited for: 13 -> 13; matrix products, arithmetic and copies ran while one was open for 7% -> 5% of each run, Pallas kernels for 6% -> 7%
where the time goes in v4:
time: 44.5 us; the launch traced here: 44.3 us
  starting transfers between devices  16.5 us (37%)
  waiting for transfers between devices  15.3 us (34%)
  Pallas kernels  8.45 us (19%)
  other arithmetic  3.21 us (7%)
  between operations  0.75 us (2%)
    ppermute x13, waiting for transfers between devices, partner(): lax.ppermute(block, axis, [(i, i ^ k) for i in range(lax.axis_size(axis))])  11.3 us
    ppermute x13, starting transfers between devices, partner(): lax.ppermute(block, axis, [(i, i ^ k) for i in range(lax.axis_size(axis))])  10.9 us
    ppermute x4, starting transfers between devices, shifted(): lax.ppermute(value, axis, [(i, (i + distance) % peers) for i in range(pee...  5.62 us
    ppermute x4, waiting for transfers between devices, shifted(): lax.ppermute(value, axis, [(i, (i + distance) % peers) for i in range(pee...  4.05 us
    pallas_call x1, Pallas kernels, on_device(): call(advance_kernel, block, (padded, pltpu.VMEM((4, span, 256), bf16), pl...  2.96 us
    pallas_call x1, Pallas kernels, on_device(): call(inner_kernel, (shape((groups - 4, span, 256), bf16), shape((groups -...  2.13 us
    pallas_call x1, Pallas kernels, on_device(): call(row_kernel, block, (pltpu.VMEM((grid_x, 2 * breadth), f32),))  1.36 us
    concatenate x1, other arithmetic, on_device(): jnp.concatenate([w_second.reshape(576, 64), w_third.reshape(144, 64)], ax...  0.97 us
  transfers between devices with their start and end apart: 17, of which 13 were waited for; matrix products, arithmetic and copies ran while one was open for 5% of the time, Pallas kernels for 7%

profile of v4, /device:TPU:0, one launch (start us, length us, event | category | flops | bytes accessed | tf_op | source)
XLA Modules:
  0.0 44.3 jit_solution(16821432919635458816)
XLA Ops:
  0.6 0.8 %pad_maximum_fusion.1 = f32[2,32,256]{2,1,0:T(8,128)S(1)} fusion(f32[1,32,256]{2,1,0:T(8,128)} %bitcast.15, f32[1,32,256]{2,1,0:T(8,128)} %bitcast.16), kind=kLoop, calls=%fused_computation.1 | loop fusion | flops 16384 | bytes 131072 | tf_op jit(solution)/shard_map/columns_around/stack | solution.py:466
  1.5 3.9 %collective-permute-start = (f32[8,128]{1,0:T(8,128)S(1)}, f32[8,128]{1,0:T(8,128)S(1)}, u32[]{:S(2)}, u32[]{:S(2)}) collective-permute-start(f32[8,128]{1,0:T(8,128)S(1)} %get-tuple-element.18), channel_id=1, source_target_pairs={{0,3},{1,0},{2,1},{3,2},{4,7},{5,4},{6,5},{7,6},{8,11},{9,8},{10,9... | collective-permute-start | bytes 12296 | tf_op jit(solution)/shard_map/columns_around/ppermute | solution.py:463
  5.4 0.7 %convert_bitcast_fusion.taps_ref = f32[9,2,64]{2,1,0:T(2,128)S(1)} fusion(bf16[9,64,2]{1,2,0:T(2,128)(2,1)} %param.16), kind=kLoop, calls=%fused_computation.2 | loop fusion | flops 1152 | bytes 6912 | tf_op jit(solution)/shard_map/weights/convert_element_type | solution.py:472
  6.1 1.0 %pad_maximum_fusion.packed_ref = bf16[720,64]{1,0:T(8,128)(2,1)S(1)} fusion(bf16[144,64]{1,0:T(8,128)(2,1)} %bitcast.14, bf16[576,64]{1,0:T(8,128)(2,1)} %bitcast.13), kind=kLoop, calls=%fused_computation | loop fusion | flops 184320 | bytes 184320 | tf_op jit(solution)/shard_map/weights/concatenate | solution.py:483
  7.1 0.8 %pad_maximum_fusion.2 = f32[144]{0:T(256)S(1)} fusion(f32[16]{0:T(128)} %param.21, f32[64]{0:T(128)} %param.19, f32[64]{0:T(128)} %param.17), kind=kLoop, calls=%fused_computation.3 | loop fusion | flops 288 | bytes 1152 | tf_op jit(solution)/shard_map/weights/concatenate | solution.py:473
  8.7 1.3 %collective-permute-done.1.left_ref = f32[8,128]{1,0:T(8,128)S(1)} collective-permute-done((f32[8,128]{1,0:T(8,128)S(1)}, f32[8,128]{1,0:T(8,128)S(1)}, u32[]{:S(2)}, u32[]{:S(2)}) %collective-permute-start.1) | collective-permute-done | bytes 4128 | tf_op jit(solution)/shard_map/columns_around/ppermute | solution.py:463
  10.0 1.7 %collective-permute-start.2 = (f32[8,384]{1,0:T(8,128)S(1)}, f32[8,384]{1,0:T(8,128)S(1)}, u32[]{:S(2)}, u32[]{:S(2)}) collective-permute-start(f32[8,384]{1,0:T(8,128)S(1)} %get-tuple-element.23), channel_id=1, source_target_pairs={{0,28},{4,0},{8,4},{12,8},{16,12},{20,16},{24,20},{28,24},{1,29},{... | collective-permute-start | bytes 36872 | tf_op jit(solution)/shard_map/rows_around/ppermute | solution.py:463
  11.7 2.1 %advance.2 = (bf16[6,272,256]{2,1,0:T(8,128)(2,1)S(1)}, bf16[4,272,256]{2,1,0:T(8,128)(2,1)S(1)}, f32[2,64,384]{2,1,0:T(8,128)S(1)}) custom-call(f32[64,256]{1,0:T(8,128)S(1)} %bitcast.10, f32[64,128]{1,0:T(8,128)S(1)} %get-tuple-element.22.beside_ref, bf16[10,256,256]{2,1,0:T(8,128)(2,1)S(1)} %get-tuple-element.25.w1_ref, ...), custom_call_target="tpu_custom_call" | custom-call | flops 500000000 | bytes 1048576 | tf_op jit(solution)/shard_map/advance/pallas_call | solution.py:499
  13.8 2.8 %collective-permute-done.3.top_ref = f32[8,384]{1,0:T(8,128)S(1)} collective-permute-done((f32[8,384]{1,0:T(8,128)S(1)}, f32[8,384]{1,0:T(8,128)S(1)}, u32[]{:S(2)}, u32[]{:S(2)}) %collective-permute-start.3) | collective-permute-done | bytes 12320 | tf_op jit(solution)/shard_map/rows_around/ppermute | solution.py:463
  16.6 3.0 %advance.3.refs_0_.refs_5_ = f32[64,256]{1,0:T(8,128)S(1)} custom-call(f32[64,256]{1,0:T(8,128)S(1)} %bitcast.11, f32[64,128]{1,0:T(8,128)S(1)} %get-tuple-element.22.beside_ref, f32[8,384]{1,0:T(8,128)S(1)} %collective-permute-done.2.bot_ref, f32[8,384]{1,0:T(8,128)S(1)} %collective-permute-done.3.top_ref, ...), custom_call_target="tpu_custom_call" | custom-call | flops 1000000000 | bytes 1048576 | tf_op jit(solution)/shard_map/advance/pallas_call | solution.py:509
  19.6 1.6 %collective-permute-start.4 = (f32[64,256]{1,0:T(8,128)S(1)}, f32[64,256]{1,0:T(8,128)S(1)}, u32[]{:S(2)}, u32[]{:S(2)}) collective-permute-start(f32[64,256]{1,0:T(8,128)S(1)} %advance.3.refs_0_.refs_5_), channel_id=1, source_target_pairs={{0,1},{1,0},{2,3},{3,2},{4,5},{5,4},{6,7},{7,6},{8,9},{9,8},{10,11... | collective-permute-start | bytes 196616 | tf_op jit(solution)/shard_map/ppermute | solution.py:440
  21.2 1.5 %collective-permute-start.5 = (f32[64,256]{1,0:T(8,128)S(1)}, f32[64,256]{1,0:T(8,128)S(1)}, u32[]{:S(2)}, u32[]{:S(2)}) collective-permute-start(f32[64,256]{1,0:T(8,128)S(1)} %advance.3.refs_0_.refs_5_), channel_id=1, source_target_pairs={{0,2},{1,3},{2,0},{3,1},{4,6},{5,7},{6,4},{7,5},{8,10},{9,11},{10,... | collective-permute-start | bytes 196616 | tf_op jit(solution)/shard_map/ppermute | solution.py:440
  23.1 0.8 %collective-permute-done.4.refs_1_ = f32[64,256]{1,0:T(8,128)S(1)} collective-permute-done((f32[64,256]{1,0:T(8,128)S(1)}, f32[64,256]{1,0:T(8,128)S(1)}, u32[]{:S(2)}, u32[]{:S(2)}) %collective-permute-start.4) | collective-permute-done | bytes 65568 | tf_op jit(solution)/shard_map/ppermute | solution.py:440
  23.9 1.6 %collective-permute-done.5.refs_2_ = f32[64,256]{1,0:T(8,128)S(1)} collective-permute-done((f32[64,256]{1,0:T(8,128)S(1)}, f32[64,256]{1,0:T(8,128)S(1)}, u32[]{:S(2)}, u32[]{:S(2)}) %collective-permute-start.5) | collective-permute-done | bytes 65568 | tf_op jit(solution)/shard_map/ppermute | solution.py:440
  25.5 2.4 %collective-permute-done.6.refs_3_ = f32[64,256]{1,0:T(8,128)S(1)} collective-permute-done((f32[64,256]{1,0:T(8,128)S(1)}, f32[64,256]{1,0:T(8,128)S(1)}, u32[]{:S(2)}, u32[]{:S(2)}) %collective-permute-start.6) | collective-permute-done | bytes 65568 | tf_op jit(solution)/shard_map/ppermute | solution.py:440
  28.3 3.4 %collective-permute-start.8 = (f32[64,256]{1,0:T(8,128)S(1)}, f32[64,256]{1,0:T(8,128)S(1)}, u32[]{:S(2)}, u32[]{:S(2)}) collective-permute-start(f32[64,256]{1,0:T(8,128)S(1)} %shard_map.149.refs_0_), channel_id=1, source_target_pairs={{0,8},{4,12},{8,0},{12,4},{16,24},{20,28},{24,16},{28,20},{1,9},{5... | collective-permute-start | bytes 196616 | tf_op jit(solution)/shard_map/ppermute | solution.py:440
  31.7 1.7 %collective-permute-done.10.refs_4_ = f32[64,256]{1,0:T(8,128)S(1)} collective-permute-done((f32[64,256]{1,0:T(8,128)S(1)}, f32[64,256]{1,0:T(8,128)S(1)}, u32[]{:S(2)}, u32[]{:S(2)}) %collective-permute-start.10) | collective-permute-done | bytes 65568 | tf_op jit(solution)/shard_map/ppermute | solution.py:440
  33.4 1.1 %collective-permute-done.12.refs_6_ = f32[64,256]{1,0:T(8,128)S(1)} collective-permute-done((f32[64,256]{1,0:T(8,128)S(1)}, f32[64,256]{1,0:T(8,128)S(1)}, u32[]{:S(2)}, u32[]{:S(2)}) %collective-permute-start.12) | collective-permute-done | bytes 65568 | tf_op jit(solution)/shard_map/ppermute | solution.py:440
  36.0 1.4 %shard_map.151.refs_0_ = f32[64,256]{1,0:T(8,128)S(1)} custom-call(f32[64,256]{1,0:T(8,128)S(1)} %shard_map.149.refs_0_, f32[64,256]{1,0:T(8,128)S(1)} %collective-permute-done.7.refs_1_, f32[64,256]{1,0:T(8,128)S(1)} %collective-permute-done.8.refs_2_, f32[64,256]{1,0:T(8,128)S(1)} %collective-permute-done.9.refs_3_, ...), custom_call_target="tpu_custom_call" | custom-call | flops 10000000 | bytes 1048576 | tf_op jit(solution)/shard_map/pallas_call | solution.py:527
  37.6 0.9 %collective-permute-start.15 = (f32[64,256]{1,0:T(8,128)S(1)}, f32[64,256]{1,0:T(8,128)S(1)}, u32[]{:S(2)}, u32[]{:S(2)}) collective-permute-start(f32[64,256]{1,0:T(8,128)S(1)} %shard_map.151.refs_0_), channel_id=1, source_target_pairs={{0,2},{1,3},{2,0},{3,1},{4,6},{5,7},{6,4},{7,5},{8,10},{9,11},{10,... | collective-permute-start | bytes 196616 | tf_op jit(solution)/shard_map/ppermute | solution.py:440
  38.4 2.5 %collective-permute-start.16 = (f32[64,256]{1,0:T(8,128)S(1)}, f32[64,256]{1,0:T(8,128)S(1)}, u32[]{:S(2)}, u32[]{:S(2)}) collective-permute-start(f32[64,256]{1,0:T(8,128)S(1)} %shard_map.151.refs_0_), channel_id=1, source_target_pairs={{0,3},{1,2},{2,1},{3,0},{4,7},{5,6},{6,5},{7,4},{8,11},{9,10},{10,... | collective-permute-start | bytes 196616 | tf_op jit(solution)/shard_map/ppermute | solution.py:440
  41.0 1.0 %collective-permute-done.14.refs_1_ = f32[64,256]{1,0:T(8,128)S(1)} collective-permute-done((f32[64,256]{1,0:T(8,128)S(1)}, f32[64,256]{1,0:T(8,128)S(1)}, u32[]{:S(2)}, u32[]{:S(2)}) %collective-permute-start.14) | collective-permute-done | bytes 65568 | tf_op jit(solution)/shard_map/ppermute | solution.py:440
  42.5 1.1 %collective-permute-done.16.refs_3_ = f32[64,256]{1,0:T(8,128)S(1)} collective-permute-done((f32[64,256]{1,0:T(8,128)S(1)}, f32[64,256]{1,0:T(8,128)S(1)}, u32[]{:S(2)}, u32[]{:S(2)}) %collective-permute-start.16) | collective-permute-done | bytes 65568 | tf_op jit(solution)/shard_map/ppermute | solution.py:440
  43.6 0.7 %shard_map.152 = (f32[32,256]{1,0:T(8,128)}, f32[32,256]{1,0:T(8,128)}) custom-call(f32[64,256]{1,0:T(8,128)S(1)} %shard_map.151.refs_0_, f32[64,256]{1,0:T(8,128)S(1)} %collective-permute-done.14.refs_1_, f32[64,256]{1,0:T(8,128)S(1)} %collective-permute-done.15.refs_2_, f32[64,256]{1,0:T(8,128)S(1)} %collective-permute-done.16.refs_3_, ...), custom_call_target="tpu_custom_call" | custom-call | flops 10000000 | bytes 1048576 | tf_op jit(solution)/shard_map/pallas_call | solution.py:531
  (36 shorter events, 3.9 us)
Async XLA Ops:
  1.5 7.2 %collective-permute-start = (f32[8,128]{1,0:T(8,128)S(1)}, f32[8,128]{1,0:T(8,128)S(1)}, u32[]{:S(2)}, u32[]{:S(2)}) collective-permute-start(f32[8,128]{1,0:T(8,128)S(1)} %get-tuple-element.18), channel_id=1, source_target_pairs={{0,3},{1,0},{2,1},{3,2},{4,7},{5,4},{6,5},{7,6},{8,11},{9,8},{10,9... | collective-permute-start | bytes 12296 | tf_op jit(solution)/shard_map/columns_around/ppermute | solution.py:463
  5.4 4.5 %collective-permute-start.1 = (f32[8,128]{1,0:T(8,128)S(1)}, f32[8,128]{1,0:T(8,128)S(1)}, u32[]{:S(2)}, u32[]{:S(2)}) collective-permute-start(f32[8,128]{1,0:T(8,128)S(1)} %get-tuple-element.19), channel_id=1, source_target_pairs={{0,1},{1,2},{2,3},{3,0},{4,5},{5,6},{6,7},{7,4},{8,9},{9,10},{10,1... | collective-permute-start | bytes 12296 | tf_op jit(solution)/shard_map/columns_around/ppermute | solution.py:463
  10.0 3.8 %collective-permute-start.2 = (f32[8,384]{1,0:T(8,128)S(1)}, f32[8,384]{1,0:T(8,128)S(1)}, u32[]{:S(2)}, u32[]{:S(2)}) collective-permute-start(f32[8,384]{1,0:T(8,128)S(1)} %get-tuple-element.23), channel_id=1, source_target_pairs={{0,28},{4,0},{8,4},{12,8},{16,12},{20,16},{24,20},{28,24},{1,29},{... | collective-permute-start | bytes 36872 | tf_op jit(solution)/shard_map/rows_around/ppermute | solution.py:463
  11.7 4.9 %collective-permute-start.3 = (f32[8,384]{1,0:T(8,128)S(1)}, f32[8,384]{1,0:T(8,128)S(1)}, u32[]{:S(2)}, u32[]{:S(2)}) collective-permute-start(f32[8,384]{1,0:T(8,128)S(1)} %get-tuple-element.24), channel_id=1, source_target_pairs={{0,4},{4,8},{8,12},{12,16},{16,20},{20,24},{24,28},{28,0},{1,5},{5... | collective-permute-start | bytes 36872 | tf_op jit(solution)/shard_map/rows_around/ppermute | solution.py:463
  16.6 11.3 %copy-start = (bf16[256,512]{1,0:T(8,128)(2,1)S(1)}, bf16[256,512]{1,0:T(8,128)(2,1)}, u32[]{:S(2)}) copy-start(bf16[256,512]{1,0:T(8,128)(2,1)} %constant.12.clone.refs_5_.refs_11_) | copy-start | bytes 786436
  16.6 11.3 %copy-start.1 = (bf16[256,512]{1,0:T(8,128)(2,1)S(1)}, bf16[256,512]{1,0:T(8,128)(2,1)}, u32[]{:S(2)}) copy-start(bf16[256,512]{1,0:T(8,128)(2,1)} %constant.13.clone.refs_6_.refs_12_) | copy-start | bytes 786436
  16.6 11.3 %copy-start.4 = (f32[4,8,256]{2,1,0:T(8,128)S(1)}, f32[4,8,256]{2,1,0:T(8,128)}, u32[]{:S(2)}) copy-start(f32[4,8,256]{2,1,0:T(8,128)} %constant.16.clone.refs_4_) | copy-start | bytes 98308
  19.6 16.5 %copy-start.2 = (bf16[512,256]{1,0:T(8,128)(2,1)S(1)}, bf16[512,256]{1,0:T(8,128)(2,1)}, u32[]{:S(2)}) copy-start(bf16[512,256]{1,0:T(8,128)(2,1)} %constant.14.clone.refs_9_) | copy-start | bytes 786436
  19.6 16.5 %copy-start.3 = (bf16[512,256]{1,0:T(8,128)(2,1)S(1)}, bf16[512,256]{1,0:T(8,128)(2,1)}, u32[]{:S(2)}) copy-start(bf16[512,256]{1,0:T(8,128)(2,1)} %constant.15.clone.refs_10_) | copy-start | bytes 786436
  19.6 4.3 %collective-permute-start.4 = (f32[64,256]{1,0:T(8,128)S(1)}, f32[64,256]{1,0:T(8,128)S(1)}, u32[]{:S(2)}, u32[]{:S(2)}) collective-permute-start(f32[64,256]{1,0:T(8,128)S(1)} %advance.3.refs_0_.refs_5_), channel_id=1, source_target_pairs={{0,1},{1,0},{2,3},{3,2},{4,5},{5,4},{6,7},{7,6},{8,9},{9,8},{10,11... | collective-permute-start | bytes 196616 | tf_op jit(solution)/shard_map/ppermute | solution.py:440
  21.2 4.3 %collective-permute-start.5 = (f32[64,256]{1,0:T(8,128)S(1)}, f32[64,256]{1,0:T(8,128)S(1)}, u32[]{:S(2)}, u32[]{:S(2)}) collective-permute-start(f32[64,256]{1,0:T(8,128)S(1)} %advance.3.refs_0_.refs_5_), channel_id=1, source_target_pairs={{0,2},{1,3},{2,0},{3,1},{4,6},{5,7},{6,4},{7,5},{8,10},{9,11},{10,... | collective-permute-start | bytes 196616 | tf_op jit(solution)/shard_map/ppermute | solution.py:440
  22.7 5.2 %collective-permute-start.6 = (f32[64,256]{1,0:T(8,128)S(1)}, f32[64,256]{1,0:T(8,128)S(1)}, u32[]{:S(2)}, u32[]{:S(2)}) collective-permute-start(f32[64,256]{1,0:T(8,128)S(1)} %advance.3.refs_0_.refs_5_), channel_id=1, source_target_pairs={{0,3},{1,2},{2,1},{3,0},{4,7},{5,6},{6,5},{7,4},{8,11},{9,10},{10,... | collective-permute-start | bytes 196616 | tf_op jit(solution)/shard_map/ppermute | solution.py:440
  28.1 5.2 %collective-permute-start.10 = (f32[64,256]{1,0:T(8,128)S(1)}, f32[64,256]{1,0:T(8,128)S(1)}, u32[]{:S(2)}, u32[]{:S(2)}) collective-permute-start(f32[64,256]{1,0:T(8,128)S(1)} %shard_map.149.refs_0_), channel_id=1, source_target_pairs={{0,16},{4,20},{8,24},{12,28},{16,0},{20,4},{24,8},{28,12},{1,17},{... | collective-permute-start | bytes 196616 | tf_op jit(solution)/shard_map/ppermute | solution.py:440
  28.2 6.3 %collective-permute-start.12 = (f32[64,256]{1,0:T(8,128)S(1)}, f32[64,256]{1,0:T(8,128)S(1)}, u32[]{:S(2)}, u32[]{:S(2)}) collective-permute-start(f32[64,256]{1,0:T(8,128)S(1)} %shard_map.149.refs_0_), channel_id=1, source_target_pairs={{0,24},{4,28},{8,16},{12,20},{16,8},{20,12},{24,0},{28,4},{1,25},{... | collective-permute-start | bytes 196616 | tf_op jit(solution)/shard_map/ppermute | solution.py:440
  28.3 6.5 %collective-permute-start.8 = (f32[64,256]{1,0:T(8,128)S(1)}, f32[64,256]{1,0:T(8,128)S(1)}, u32[]{:S(2)}, u32[]{:S(2)}) collective-permute-start(f32[64,256]{1,0:T(8,128)S(1)} %shard_map.149.refs_0_), channel_id=1, source_target_pairs={{0,8},{4,12},{8,0},{12,4},{16,24},{20,28},{24,16},{28,20},{1,9},{5... | collective-permute-start | bytes 196616 | tf_op jit(solution)/shard_map/ppermute | solution.py:440
  31.7 3.5 %collective-permute-start.7 = (f32[64,256]{1,0:T(8,128)S(1)}, f32[64,256]{1,0:T(8,128)S(1)}, u32[]{:S(2)}, u32[]{:S(2)}) collective-permute-start(f32[64,256]{1,0:T(8,128)S(1)} %shard_map.149.refs_0_), channel_id=1, source_target_pairs={{0,4},{4,0},{8,12},{12,8},{16,20},{20,16},{24,28},{28,24},{1,5},{5... | collective-permute-start | bytes 196616 | tf_op jit(solution)/shard_map/ppermute | solution.py:440
  33.4 1.8 %collective-permute-start.11 = (f32[64,256]{1,0:T(8,128)S(1)}, f32[64,256]{1,0:T(8,128)S(1)}, u32[]{:S(2)}, u32[]{:S(2)}) collective-permute-start(f32[64,256]{1,0:T(8,128)S(1)} %collective-permute-done.10.refs_4_), channel_id=1, source_target_pairs={{0,4},{4,0},{8,12},{12,8},{16,20},{20,16},{24,28},{28,24},{1,5},{5... | collective-permute-start | bytes 196616 | tf_op jit(solution)/shard_map/ppermute | solution.py:440
  34.5 1.3 %collective-permute-start.13 = (f32[64,256]{1,0:T(8,128)S(1)}, f32[64,256]{1,0:T(8,128)S(1)}, u32[]{:S(2)}, u32[]{:S(2)}) collective-permute-start(f32[64,256]{1,0:T(8,128)S(1)} %collective-permute-done.12.refs_6_), channel_id=1, source_target_pairs={{0,4},{4,0},{8,12},{12,8},{16,20},{20,16},{24,28},{28,24},{1,5},{5... | collective-permute-start | bytes 196616 | tf_op jit(solution)/shard_map/ppermute | solution.py:440
  34.8 1.3 %collective-permute-start.9 = (f32[64,256]{1,0:T(8,128)S(1)}, f32[64,256]{1,0:T(8,128)S(1)}, u32[]{:S(2)}, u32[]{:S(2)}) collective-permute-start(f32[64,256]{1,0:T(8,128)S(1)} %collective-permute-done.8.refs_2_), channel_id=1, source_target_pairs={{0,4},{4,0},{8,12},{12,8},{16,20},{20,16},{24,28},{28,24},{1,5},{5... | collective-permute-start | bytes 196616 | tf_op jit(solution)/shard_map/ppermute | solution.py:440
  35.2 8.4 %copy-start.5 = (f32[4,8,256]{2,1,0:T(8,128)S(1)}, f32[4,8,256]{2,1,0:T(8,128)}, u32[]{:S(2)}) copy-start(f32[4,8,256]{2,1,0:T(8,128)} %constant.17.clone.refs_4_) | copy-start | bytes 98308
  37.4 4.6 %collective-permute-start.14 = (f32[64,256]{1,0:T(8,128)S(1)}, f32[64,256]{1,0:T(8,128)S(1)}, u32[]{:S(2)}, u32[]{:S(2)}) collective-permute-start(f32[64,256]{1,0:T(8,128)S(1)} %shard_map.151.refs_0_), channel_id=1, source_target_pairs={{0,1},{1,0},{2,3},{3,2},{4,5},{5,4},{6,7},{7,6},{8,9},{9,8},{10,11... | collective-permute-start | bytes 196616 | tf_op jit(solution)/shard_map/ppermute | solution.py:440
  37.6 5.0 %collective-permute-start.15 = (f32[64,256]{1,0:T(8,128)S(1)}, f32[64,256]{1,0:T(8,128)S(1)}, u32[]{:S(2)}, u32[]{:S(2)}) collective-permute-start(f32[64,256]{1,0:T(8,128)S(1)} %shard_map.151.refs_0_), channel_id=1, source_target_pairs={{0,2},{1,3},{2,0},{3,1},{4,6},{5,7},{6,4},{7,5},{8,10},{9,11},{10,... | collective-permute-start | bytes 196616 | tf_op jit(solution)/shard_map/ppermute | solution.py:440
  38.4 5.2 %collective-permute-start.16 = (f32[64,256]{1,0:T(8,128)S(1)}, f32[64,256]{1,0:T(8,128)S(1)}, u32[]{:S(2)}, u32[]{:S(2)}) collective-permute-start(f32[64,256]{1,0:T(8,128)S(1)} %shard_map.151.refs_0_), channel_id=1, source_target_pairs={{0,3},{1,2},{2,1},{3,0},{4,7},{5,6},{6,5},{7,4},{8,11},{9,10},{10,... | collective-permute-start | bytes 196616 | tf_op jit(solution)/shard_map/ppermute | solution.py:440

commit v5 on v4

--- a/solution.py
+++ b/solution.py
@@ -102,17 +102,14 @@
 
 def other_weights_kernel(packed_ref, k2_ref, even_ref, odd_ref, order_ref):
     order_ref[...] = jnp.zeros(order_ref.shape, f32)
-    k2_ref[...] = jnp.zeros(k2_ref.shape, bf16)
     slots = {-1: 5, 0: 0, 1: 1, 2: 2, 3: 3, 4: 6}
     blank = jnp.zeros((64, 64), f32)
     for c in range(3):
         taps = [packed_ref[64 * (3 * d + c) : 64 * (3 * d + c) + 64, :].astype(f32) for d in range(3)]
         two = [(taps[0], blank), (taps[1], taps[0]), (taps[2], taps[1]), (blank, taps[2])]
         two = [jnp.concatenate(pair, axis=0).T.astype(bf16) for pair in two]
-        for h in range(2):
-            for d in range(4):
-                slot = slots[d + 2 * h - 1]
-                k2_ref[64 * slot : 64 * slot + 64, 256 * c + 128 * h : 256 * c + 128 * h + 128] = two[d]
+        for slot, source in enumerate((1, 2, 3, 0)):
+            k2_ref[64 * slot : 64 * slot + 64, 128 * c : 128 * c + 128] = two[source]
 
     taps = [
         [packed_ref[576 + 16 * (3 * d + c) : 592 + 16 * (3 * d + c), :].astype(f32) for d in range(3)]
@@ -166,10 +163,15 @@
 
 
 def layer_2(before, own, after, weights_ref, bias_ref):
-    total = with_neighbours(before, own, after, weights_ref)
-    span = total.shape[0]
-    total = pltpu.roll(total[:, :256], 1, 0) + total[:, 256:512] + pltpu.roll(total[:, 512:], span - 1, 0)
-    return jnp.maximum(total + bias_ref[...], 0.0).astype(bf16)
+    span = own.shape[0]
+    lower = lax.broadcasted_iota(jnp.int32, (span, 128), 1) < 64
+    left, right = own[:, :128], own[:, 128:]
+    results = []
+    for pair, below, above in ((left, right, before[:, 128:]), (right, after[:, :128], left)):
+        total = dot(jnp.concatenate([pair, jnp.where(lower, below, above)], axis=1), weights_ref[...])
+        total = pltpu.roll(total[:, :128], 1, 0) + total[:, 128:256] + pltpu.roll(total[:, 256:], span - 1, 0)
+        results.append(jnp.maximum(total + bias_ref[:, :128], 0.0).astype(bf16))
+    return jnp.concatenate(results, axis=1)
 
 
 def layer_3(second, groups, r, weights_ref):
@@ -355,7 +357,7 @@
 
 
 def row_kernel(*refs):
-    *blocks, factors_ref, table_ref, table_low_ref, high_ref, low_ref, out_ref, gathered = refs
+    *blocks, factors_ref, table_ref, high_ref, low_ref, out_ref, gathered = refs
     rows, breadth = out_ref.shape
     height = rows // 2
     length = len(blocks) * height
@@ -366,7 +368,8 @@
         gathered[pl.ds(start, height), breadth:] = ref[height:, :]
     data = gathered[...]
     data, data_low = split(data)
-    spectra = dot(table_ref[...], data) + dot(table_ref[...], data_low) + dot(table_low_ref[...], data)
+    both = dot(table_ref[...], data)
+    spectra = both[: 2 * length] + both[2 * length :] + dot(table_ref[: 2 * length], data_low)
     real_part = spectra[:length, :breadth] + spectra[length:, breadth:]
     imag_part = spectra[:length, breadth:] - spectra[length:, :breadth]
     same_real, same_imag, cross = factors_ref[0], factors_ref[1], factors_ref[2]
@@ -375,12 +378,11 @@
     kept, kept_low = split(jnp.concatenate([kept_real, kept_imag], axis=1))
     start = pl.multiple_of(own_index * height, height)
 
-    def own(ref):
-        parts = [ref[pl.ds(start, height), :], ref[pl.ds(pl.multiple_of(length + start, height), height), :]]
-        return jnp.concatenate(parts, axis=0)
-
-    table, table_low = own(table_ref), own(table_low_ref)
-    home = dot(table, kept) + dot(table, kept_low) + dot(table_low, kept)
+    table = jnp.concatenate(
+        [table_ref[pl.ds(pl.multiple_of(part * length + start, height), height), :] for part in range(4)], axis=0
+    )
+    both = dot(table, kept)
+    home = both[: 2 * height] + both[2 * height :] + dot(table[: 2 * height], kept_low)
     home = jnp.concatenate(
         [
             home[:height, :breadth] - home[height:, breadth:],
@@ -424,7 +426,7 @@
     length = height * members_x
     k = np.arange(length)
     phase = turn * (np.outer(k, k) % length) / length
-    row = split_table(np.concatenate([np.cos(phase), np.sin(phase)], axis=0))
+    row = np.concatenate(split_table(np.concatenate([np.cos(phase), np.sin(phase)], axis=0)), axis=0)
     g = np.arange(members_y)[:, None, None]
     partner = g ^ np.arange(members_y)[None, :, None]
     whole = breadth * members_y
@@ -483,7 +485,7 @@
         packed = jnp.concatenate([w_second.reshape(576, 64), w_third.reshape(144, 64)], axis=0)
         *others, order = call(
             other_weights_kernel,
-            (shape((512, 768), bf16), shape((512, 256), bf16), shape((512, 256), bf16), shape((8, 128), f32)),
+            (shape((256, 384), bf16), shape((512, 256), bf16), shape((512, 256), bf16), shape((8, 128), f32)),
         )(packed)
 
     with jax.named_scope("rows_around"):
@@ -519,13 +521,13 @@
         )(both, beside, bottom, top, kernel_1, *others, *biases, *inner)
 
     column, row, twiddle_out, twiddle_home = tables(height, breadth, members_x, members_y)
-    column, row = [[jnp.asarray(t) for t in pair] for pair in (column, row)]
+    column, row = [jnp.asarray(t) for t in column], jnp.asarray(row)
     spectra = call(column_kernel, block)(*gather_y(star), jnp.asarray(twiddle_out), *column)
     factors = call(
         functools.partial(factors_kernel, scale=1.0 / (grid_x * grid_y)), shape((3, grid_x, breadth), f32)
     )()
     columns = call(row_kernel, block, (pltpu.VMEM((grid_x, 2 * breadth), f32),))(
-        *gather_x(spectra), factors, *row, *column
+        *gather_x(spectra), factors, row, *column
     )
     part = shape((height, breadth), f32)
     return tuple(call(home_kernel, (part, part))(*gather_y(columns), jnp.asarray(twiddle_home), star))

time: 44.5 us -> 44 us (0.989)
  Pallas kernels: 8.45 us -> 7.54 us
  transfers between devices with their start and end apart: 17 -> 17, of which waited for: 13 -> 13; matrix products, arithmetic and copies ran while one was open for 5% -> 6% of each run, Pallas kernels for 7% -> 6%
where the time goes in v5:
time: 44 us; the launch traced here: 43.7 us
  starting transfers between devices  16.5 us (38%)
  waiting for transfers between devices  15.7 us (36%)
  Pallas kernels  7.54 us (17%)
  other arithmetic  3.21 us (7%)
  between operations  0.74 us (2%)
    ppermute x13, waiting for transfers between devices, partner(): lax.ppermute(block, axis, [(i, i ^ k) for i in range(lax.axis_size(axis))])  11.3 us
    ppermute x13, starting transfers between devices, partner(): lax.ppermute(block, axis, [(i, i ^ k) for i in range(lax.axis_size(axis))])  10.9 us
    ppermute x4, starting transfers between devices, shifted(): lax.ppermute(value, axis, [(i, (i + distance) % peers) for i in range(pee...  5.62 us
    ppermute x4, waiting for transfers between devices, shifted(): lax.ppermute(value, axis, [(i, (i + distance) % peers) for i in range(pee...  4.43 us
    pallas_call x1, Pallas kernels, on_device(): call(advance_kernel, block, (padded, pltpu.VMEM((4, span, 256), bf16), pl...  2.57 us
    pallas_call x1, Pallas kernels, on_device(): call(inner_kernel, (shape((groups - 4, span, 256), bf16), shape((groups -...  1.79 us
    pallas_call x1, Pallas kernels, on_device(): call(row_kernel, block, (pltpu.VMEM((grid_x, 2 * breadth), f32),))  1.22 us
    concatenate x1, other arithmetic, on_device(): jnp.concatenate([w_second.reshape(576, 64), w_third.reshape(144, 64)], ax...  0.97 us
  transfers between devices with their start and end apart: 17, of which 13 were waited for; matrix products, arithmetic and copies ran while one was open for 6% of the time, Pallas kernels for 6%

profile of v5, /device:TPU:0, one launch (start us, length us, event | category | flops | bytes accessed | tf_op | source)
XLA Modules:
  0.0 43.7 jit_solution(9800636610341660993)
XLA Ops:
  0.6 0.8 %pad_maximum_fusion.1 = f32[2,32,256]{2,1,0:T(8,128)S(1)} fusion(f32[1,32,256]{2,1,0:T(8,128)} %bitcast.15, f32[1,32,256]{2,1,0:T(8,128)} %bitcast.16), kind=kLoop, calls=%fused_computation.1 | loop fusion | flops 16384 | bytes 131072 | tf_op jit(solution)/shard_map/columns_around/stack | solution.py:468
  1.5 3.9 %collective-permute-start = (f32[8,128]{1,0:T(8,128)S(1)}, f32[8,128]{1,0:T(8,128)S(1)}, u32[]{:S(2)}, u32[]{:S(2)}) collective-permute-start(f32[8,128]{1,0:T(8,128)S(1)} %get-tuple-element.18), channel_id=1, source_target_pairs={{0,3},{1,0},{2,1},{3,2},{4,7},{5,4},{6,5},{7,6},{8,11},{9,8},{10,9... | collective-permute-start | bytes 12296 | tf_op jit(solution)/shard_map/columns_around/ppermute | solution.py:465
  5.4 0.7 %convert_bitcast_fusion.taps_ref = f32[9,2,64]{2,1,0:T(2,128)S(1)} fusion(bf16[9,64,2]{1,2,0:T(2,128)(2,1)} %param.15), kind=kLoop, calls=%fused_computation.2 | loop fusion | flops 1152 | bytes 6912 | tf_op jit(solution)/shard_map/weights/convert_element_type | solution.py:474
  6.1 1.0 %pad_maximum_fusion.packed_ref = bf16[720,64]{1,0:T(8,128)(2,1)S(1)} fusion(bf16[144,64]{1,0:T(8,128)(2,1)} %bitcast.14, bf16[576,64]{1,0:T(8,128)(2,1)} %bitcast.13), kind=kLoop, calls=%fused_computation | loop fusion | flops 184320 | bytes 184320 | tf_op jit(solution)/shard_map/weights/concatenate | solution.py:485
  7.1 0.8 %pad_maximum_fusion.2 = f32[144]{0:T(256)S(1)} fusion(f32[16]{0:T(128)} %param.20, f32[64]{0:T(128)} %param.18, f32[64]{0:T(128)} %param.16), kind=kLoop, calls=%fused_computation.3 | loop fusion | flops 288 | bytes 1152 | tf_op jit(solution)/shard_map/weights/concatenate | solution.py:475
  8.6 1.3 %collective-permute-done.1.left_ref = f32[8,128]{1,0:T(8,128)S(1)} collective-permute-done((f32[8,128]{1,0:T(8,128)S(1)}, f32[8,128]{1,0:T(8,128)S(1)}, u32[]{:S(2)}, u32[]{:S(2)}) %collective-permute-start.1) | collective-permute-done | bytes 4128 | tf_op jit(solution)/shard_map/columns_around/ppermute | solution.py:465
  10.0 1.7 %collective-permute-start.2 = (f32[8,384]{1,0:T(8,128)S(1)}, f32[8,384]{1,0:T(8,128)S(1)}, u32[]{:S(2)}, u32[]{:S(2)}) collective-permute-start(f32[8,384]{1,0:T(8,128)S(1)} %get-tuple-element.23), channel_id=1, source_target_pairs={{0,28},{4,0},{8,4},{12,8},{16,12},{20,16},{24,20},{28,24},{1,29},{... | collective-permute-start | bytes 36872 | tf_op jit(solution)/shard_map/rows_around/ppermute | solution.py:465
  11.7 1.8 %advance.2 = (bf16[6,272,256]{2,1,0:T(8,128)(2,1)S(1)}, bf16[4,272,256]{2,1,0:T(8,128)(2,1)S(1)}, f32[2,64,384]{2,1,0:T(8,128)S(1)}) custom-call(f32[64,256]{1,0:T(8,128)S(1)} %bitcast.10, f32[64,128]{1,0:T(8,128)S(1)} %get-tuple-element.22.beside_ref, bf16[10,256,256]{2,1,0:T(8,128)(2,1)S(1)} %get-tuple-element.25.w1_ref, ...), custom_call_target="tpu_custom_call" | custom-call | flops 500000000 | bytes 1048576 | tf_op jit(solution)/shard_map/advance/pallas_call | solution.py:501
  13.5 3.1 %collective-permute-done.3.top_ref = f32[8,384]{1,0:T(8,128)S(1)} collective-permute-done((f32[8,384]{1,0:T(8,128)S(1)}, f32[8,384]{1,0:T(8,128)S(1)}, u32[]{:S(2)}, u32[]{:S(2)}) %collective-permute-start.3) | collective-permute-done | bytes 12320 | tf_op jit(solution)/shard_map/rows_around/ppermute | solution.py:465
  16.6 2.6 %advance.3.refs_0_.refs_5_ = f32[64,256]{1,0:T(8,128)S(1)} custom-call(f32[64,256]{1,0:T(8,128)S(1)} %bitcast.11, f32[64,128]{1,0:T(8,128)S(1)} %get-tuple-element.22.beside_ref, f32[8,384]{1,0:T(8,128)S(1)} %collective-permute-done.2.bot_ref, f32[8,384]{1,0:T(8,128)S(1)} %collective-permute-done.3.top_ref, ...), custom_call_target="tpu_custom_call" | custom-call | flops 1000000000 | bytes 1048576 | tf_op jit(solution)/shard_map/advance/pallas_call | solution.py:511
  19.2 1.6 %collective-permute-start.4 = (f32[64,256]{1,0:T(8,128)S(1)}, f32[64,256]{1,0:T(8,128)S(1)}, u32[]{:S(2)}, u32[]{:S(2)}) collective-permute-start(f32[64,256]{1,0:T(8,128)S(1)} %advance.3.refs_0_.refs_5_), channel_id=1, source_target_pairs={{0,1},{1,0},{2,3},{3,2},{4,5},{5,4},{6,7},{7,6},{8,9},{9,8},{10,11... | collective-permute-start | bytes 196616 | tf_op jit(solution)/shard_map/ppermute | solution.py:442
  20.8 1.5 %collective-permute-start.5 = (f32[64,256]{1,0:T(8,128)S(1)}, f32[64,256]{1,0:T(8,128)S(1)}, u32[]{:S(2)}, u32[]{:S(2)}) collective-permute-start(f32[64,256]{1,0:T(8,128)S(1)} %advance.3.refs_0_.refs_5_), channel_id=1, source_target_pairs={{0,2},{1,3},{2,0},{3,1},{4,6},{5,7},{6,4},{7,5},{8,10},{9,11},{10,... | collective-permute-start | bytes 196616 | tf_op jit(solution)/shard_map/ppermute | solution.py:442
  22.7 0.8 %collective-permute-done.4.refs_1_ = f32[64,256]{1,0:T(8,128)S(1)} collective-permute-done((f32[64,256]{1,0:T(8,128)S(1)}, f32[64,256]{1,0:T(8,128)S(1)}, u32[]{:S(2)}, u32[]{:S(2)}) %collective-permute-start.4) | collective-permute-done | bytes 65568 | tf_op jit(solution)/shard_map/ppermute | solution.py:442
  23.5 1.5 %collective-permute-done.5.refs_2_ = f32[64,256]{1,0:T(8,128)S(1)} collective-permute-done((f32[64,256]{1,0:T(8,128)S(1)}, f32[64,256]{1,0:T(8,128)S(1)}, u32[]{:S(2)}, u32[]{:S(2)}) %collective-permute-start.5) | collective-permute-done | bytes 65568 | tf_op jit(solution)/shard_map/ppermute | solution.py:442
  25.0 2.4 %collective-permute-done.6.refs_3_ = f32[64,256]{1,0:T(8,128)S(1)} collective-permute-done((f32[64,256]{1,0:T(8,128)S(1)}, f32[64,256]{1,0:T(8,128)S(1)}, u32[]{:S(2)}, u32[]{:S(2)}) %collective-permute-start.6) | collective-permute-done | bytes 65568 | tf_op jit(solution)/shard_map/ppermute | solution.py:442
  27.9 3.4 %collective-permute-start.8 = (f32[64,256]{1,0:T(8,128)S(1)}, f32[64,256]{1,0:T(8,128)S(1)}, u32[]{:S(2)}, u32[]{:S(2)}) collective-permute-start(f32[64,256]{1,0:T(8,128)S(1)} %shard_map.140.refs_0_), channel_id=1, source_target_pairs={{0,8},{4,12},{8,0},{12,4},{16,24},{20,28},{24,16},{28,20},{1,9},{5... | collective-permute-start | bytes 196616 | tf_op jit(solution)/shard_map/ppermute | solution.py:442
  31.3 1.7 %collective-permute-done.10.refs_4_ = f32[64,256]{1,0:T(8,128)S(1)} collective-permute-done((f32[64,256]{1,0:T(8,128)S(1)}, f32[64,256]{1,0:T(8,128)S(1)}, u32[]{:S(2)}, u32[]{:S(2)}) %collective-permute-start.10) | collective-permute-done | bytes 65568 | tf_op jit(solution)/shard_map/ppermute | solution.py:442
  33.0 1.1 %collective-permute-done.12.refs_6_ = f32[64,256]{1,0:T(8,128)S(1)} collective-permute-done((f32[64,256]{1,0:T(8,128)S(1)}, f32[64,256]{1,0:T(8,128)S(1)}, u32[]{:S(2)}, u32[]{:S(2)}) %collective-permute-start.12) | collective-permute-done | bytes 65568 | tf_op jit(solution)/shard_map/ppermute | solution.py:442
  35.6 1.2 %shard_map.142.refs_0_ = f32[64,256]{1,0:T(8,128)S(1)} custom-call(f32[64,256]{1,0:T(8,128)S(1)} %shard_map.140.refs_0_, f32[64,256]{1,0:T(8,128)S(1)} %collective-permute-done.7.refs_1_, f32[64,256]{1,0:T(8,128)S(1)} %collective-permute-done.8.refs_2_, f32[64,256]{1,0:T(8,128)S(1)} %collective-permute-done.9.refs_3_, ...), custom_call_target="tpu_custom_call" | custom-call | flops 10000000 | bytes 1048576 | tf_op jit(solution)/shard_map/pallas_call | solution.py:529
  37.0 0.9 %collective-permute-start.15 = (f32[64,256]{1,0:T(8,128)S(1)}, f32[64,256]{1,0:T(8,128)S(1)}, u32[]{:S(2)}, u32[]{:S(2)}) collective-permute-start(f32[64,256]{1,0:T(8,128)S(1)} %shard_map.142.refs_0_), channel_id=1, source_target_pairs={{0,2},{1,3},{2,0},{3,1},{4,6},{5,7},{6,4},{7,5},{8,10},{9,11},{10,... | collective-permute-start | bytes 196616 | tf_op jit(solution)/shard_map/ppermute | solution.py:442
  37.9 2.5 %collective-permute-start.16 = (f32[64,256]{1,0:T(8,128)S(1)}, f32[64,256]{1,0:T(8,128)S(1)}, u32[]{:S(2)}, u32[]{:S(2)}) collective-permute-start(f32[64,256]{1,0:T(8,128)S(1)} %shard_map.142.refs_0_), channel_id=1, source_target_pairs={{0,3},{1,2},{2,1},{3,0},{4,7},{5,6},{6,5},{7,4},{8,11},{9,10},{10,... | collective-permute-start | bytes 196616 | tf_op jit(solution)/shard_map/ppermute | solution.py:442
  40.4 1.0 %collective-permute-done.14.refs_1_ = f32[64,256]{1,0:T(8,128)S(1)} collective-permute-done((f32[64,256]{1,0:T(8,128)S(1)}, f32[64,256]{1,0:T(8,128)S(1)}, u32[]{:S(2)}, u32[]{:S(2)}) %collective-permute-start.14) | collective-permute-done | bytes 65568 | tf_op jit(solution)/shard_map/ppermute | solution.py:442
  41.9 1.1 %collective-permute-done.16.refs_3_ = f32[64,256]{1,0:T(8,128)S(1)} collective-permute-done((f32[64,256]{1,0:T(8,128)S(1)}, f32[64,256]{1,0:T(8,128)S(1)}, u32[]{:S(2)}, u32[]{:S(2)}) %collective-permute-start.16) | collective-permute-done | bytes 65568 | tf_op jit(solution)/shard_map/ppermute | solution.py:442
  43.1 0.7 %shard_map.143 = (f32[32,256]{1,0:T(8,128)}, f32[32,256]{1,0:T(8,128)}) custom-call(f32[64,256]{1,0:T(8,128)S(1)} %shard_map.142.refs_0_, f32[64,256]{1,0:T(8,128)S(1)} %collective-permute-done.14.refs_1_, f32[64,256]{1,0:T(8,128)S(1)} %collective-permute-done.15.refs_2_, f32[64,256]{1,0:T(8,128)S(1)} %collective-permute-done.16.refs_3_, ...), custom_call_target="tpu_custom_call" | custom-call | flops 10000000 | bytes 1048576 | tf_op jit(solution)/shard_map/pallas_call | solution.py:533
  (34 shorter events, 3.9 us)
Async XLA Ops:
  1.5 7.1 %collective-permute-start = (f32[8,128]{1,0:T(8,128)S(1)}, f32[8,128]{1,0:T(8,128)S(1)}, u32[]{:S(2)}, u32[]{:S(2)}) collective-permute-start(f32[8,128]{1,0:T(8,128)S(1)} %get-tuple-element.18), channel_id=1, source_target_pairs={{0,3},{1,0},{2,1},{3,2},{4,7},{5,4},{6,5},{7,6},{8,11},{9,8},{10,9... | collective-permute-start | bytes 12296 | tf_op jit(solution)/shard_map/columns_around/ppermute | solution.py:465
  5.4 4.5 %collective-permute-start.1 = (f32[8,128]{1,0:T(8,128)S(1)}, f32[8,128]{1,0:T(8,128)S(1)}, u32[]{:S(2)}, u32[]{:S(2)}) collective-permute-start(f32[8,128]{1,0:T(8,128)S(1)} %get-tuple-element.19), channel_id=1, source_target_pairs={{0,1},{1,2},{2,3},{3,0},{4,5},{5,6},{6,7},{7,4},{8,9},{9,10},{10,1... | collective-permute-start | bytes 12296 | tf_op jit(solution)/shard_map/columns_around/ppermute | solution.py:465
  10.0 3.5 %collective-permute-start.2 = (f32[8,384]{1,0:T(8,128)S(1)}, f32[8,384]{1,0:T(8,128)S(1)}, u32[]{:S(2)}, u32[]{:S(2)}) collective-permute-start(f32[8,384]{1,0:T(8,128)S(1)} %get-tuple-element.23), channel_id=1, source_target_pairs={{0,28},{4,0},{8,4},{12,8},{16,12},{20,16},{24,20},{28,24},{1,29},{... | collective-permute-start | bytes 36872 | tf_op jit(solution)/shard_map/rows_around/ppermute | solution.py:465
  11.7 4.9 %collective-permute-start.3 = (f32[8,384]{1,0:T(8,128)S(1)}, f32[8,384]{1,0:T(8,128)S(1)}, u32[]{:S(2)}, u32[]{:S(2)}) collective-permute-start(f32[8,384]{1,0:T(8,128)S(1)} %get-tuple-element.24), channel_id=1, source_target_pairs={{0,4},{4,8},{8,12},{12,16},{16,20},{20,24},{24,28},{28,0},{1,5},{5... | collective-permute-start | bytes 36872 | tf_op jit(solution)/shard_map/rows_around/ppermute | solution.py:465
  16.6 10.9 %copy-start = (bf16[256,512]{1,0:T(8,128)(2,1)S(1)}, bf16[256,512]{1,0:T(8,128)(2,1)}, u32[]{:S(2)}) copy-start(bf16[256,512]{1,0:T(8,128)(2,1)} %constant.10.clone.refs_5_.refs_10_) | copy-start | bytes 786436
  16.6 10.9 %copy-start.1 = (bf16[256,512]{1,0:T(8,128)(2,1)S(1)}, bf16[256,512]{1,0:T(8,128)(2,1)}, u32[]{:S(2)}) copy-start(bf16[256,512]{1,0:T(8,128)(2,1)} %constant.11.clone.refs_6_.refs_11_) | copy-start | bytes 786436
  16.6 10.9 %copy-start.3 = (f32[4,8,256]{2,1,0:T(8,128)S(1)}, f32[4,8,256]{2,1,0:T(8,128)}, u32[]{:S(2)}) copy-start(f32[4,8,256]{2,1,0:T(8,128)} %constant.13.clone.refs_4_) | copy-start | bytes 98308
  19.2 16.4 %copy-start.2 = (bf16[1024,256]{1,0:T(8,128)(2,1)S(1)}, bf16[1024,256]{1,0:T(8,128)(2,1)}, u32[]{:S(2)}) copy-start(bf16[1024,256]{1,0:T(8,128)(2,1)} %constant.12.clone.refs_9_) | copy-start | bytes 1572868
  19.2 4.3 %collective-permute-start.4 = (f32[64,256]{1,0:T(8,128)S(1)}, f32[64,256]{1,0:T(8,128)S(1)}, u32[]{:S(2)}, u32[]{:S(2)}) collective-permute-start(f32[64,256]{1,0:T(8,128)S(1)} %advance.3.refs_0_.refs_5_), channel_id=1, source_target_pairs={{0,1},{1,0},{2,3},{3,2},{4,5},{5,4},{6,7},{7,6},{8,9},{9,8},{10,11... | collective-permute-start | bytes 196616 | tf_op jit(solution)/shard_map/ppermute | solution.py:442
  20.8 4.3 %collective-permute-start.5 = (f32[64,256]{1,0:T(8,128)S(1)}, f32[64,256]{1,0:T(8,128)S(1)}, u32[]{:S(2)}, u32[]{:S(2)}) collective-permute-start(f32[64,256]{1,0:T(8,128)S(1)} %advance.3.refs_0_.refs_5_), channel_id=1, source_target_pairs={{0,2},{1,3},{2,0},{3,1},{4,6},{5,7},{6,4},{7,5},{8,10},{9,11},{10,... | collective-permute-start | bytes 196616 | tf_op jit(solution)/shard_map/ppermute | solution.py:442
  22.3 5.2 %collective-permute-start.6 = (f32[64,256]{1,0:T(8,128)S(1)}, f32[64,256]{1,0:T(8,128)S(1)}, u32[]{:S(2)}, u32[]{:S(2)}) collective-permute-start(f32[64,256]{1,0:T(8,128)S(1)} %advance.3.refs_0_.refs_5_), channel_id=1, source_target_pairs={{0,3},{1,2},{2,1},{3,0},{4,7},{5,6},{6,5},{7,4},{8,11},{9,10},{10,... | collective-permute-start | bytes 196616 | tf_op jit(solution)/shard_map/ppermute | solution.py:442
  27.7 5.2 %collective-permute-start.10 = (f32[64,256]{1,0:T(8,128)S(1)}, f32[64,256]{1,0:T(8,128)S(1)}, u32[]{:S(2)}, u32[]{:S(2)}) collective-permute-start(f32[64,256]{1,0:T(8,128)S(1)} %shard_map.140.refs_0_), channel_id=1, source_target_pairs={{0,16},{4,20},{8,24},{12,28},{16,0},{20,4},{24,8},{28,12},{1,17},{... | collective-permute-start | bytes 196616 | tf_op jit(solution)/shard_map/ppermute | solution.py:442
  27.8 6.3 %collective-permute-start.12 = (f32[64,256]{1,0:T(8,128)S(1)}, f32[64,256]{1,0:T(8,128)S(1)}, u32[]{:S(2)}, u32[]{:S(2)}) collective-permute-start(f32[64,256]{1,0:T(8,128)S(1)} %shard_map.140.refs_0_), channel_id=1, source_target_pairs={{0,24},{4,28},{8,16},{12,20},{16,8},{20,12},{24,0},{28,4},{1,25},{... | collective-permute-start | bytes 196616 | tf_op jit(solution)/shard_map/ppermute | solution.py:442
  27.9 6.5 %collective-permute-start.8 = (f32[64,256]{1,0:T(8,128)S(1)}, f32[64,256]{1,0:T(8,128)S(1)}, u32[]{:S(2)}, u32[]{:S(2)}) collective-permute-start(f32[64,256]{1,0:T(8,128)S(1)} %shard_map.140.refs_0_), channel_id=1, source_target_pairs={{0,8},{4,12},{8,0},{12,4},{16,24},{20,28},{24,16},{28,20},{1,9},{5... | collective-permute-start | bytes 196616 | tf_op jit(solution)/shard_map/ppermute | solution.py:442
  31.3 3.5 %collective-permute-start.7 = (f32[64,256]{1,0:T(8,128)S(1)}, f32[64,256]{1,0:T(8,128)S(1)}, u32[]{:S(2)}, u32[]{:S(2)}) collective-permute-start(f32[64,256]{1,0:T(8,128)S(1)} %shard_map.140.refs_0_), channel_id=1, source_target_pairs={{0,4},{4,0},{8,12},{12,8},{16,20},{20,16},{24,28},{28,24},{1,5},{5... | collective-permute-start | bytes 196616 | tf_op jit(solution)/shard_map/ppermute | solution.py:442
  33.0 1.8 %collective-permute-start.11 = (f32[64,256]{1,0:T(8,128)S(1)}, f32[64,256]{1,0:T(8,128)S(1)}, u32[]{:S(2)}, u32[]{:S(2)}) collective-permute-start(f32[64,256]{1,0:T(8,128)S(1)} %collective-permute-done.10.refs_4_), channel_id=1, source_target_pairs={{0,4},{4,0},{8,12},{12,8},{16,20},{20,16},{24,28},{28,24},{1,5},{5... | collective-permute-start | bytes 196616 | tf_op jit(solution)/shard_map/ppermute | solution.py:442
  34.1 1.3 %collective-permute-start.13 = (f32[64,256]{1,0:T(8,128)S(1)}, f32[64,256]{1,0:T(8,128)S(1)}, u32[]{:S(2)}, u32[]{:S(2)}) collective-permute-start(f32[64,256]{1,0:T(8,128)S(1)} %collective-permute-done.12.refs_6_), channel_id=1, source_target_pairs={{0,4},{4,0},{8,12},{12,8},{16,20},{20,16},{24,28},{28,24},{1,5},{5... | collective-permute-start | bytes 196616 | tf_op jit(solution)/shard_map/ppermute | solution.py:442
  34.3 1.3 %collective-permute-start.9 = (f32[64,256]{1,0:T(8,128)S(1)}, f32[64,256]{1,0:T(8,128)S(1)}, u32[]{:S(2)}, u32[]{:S(2)}) collective-permute-start(f32[64,256]{1,0:T(8,128)S(1)} %collective-permute-done.8.refs_2_), channel_id=1, source_target_pairs={{0,4},{4,0},{8,12},{12,8},{16,20},{20,16},{24,28},{28,24},{1,5},{5... | collective-permute-start | bytes 196616 | tf_op jit(solution)/shard_map/ppermute | solution.py:442
  34.8 8.3 %copy-start.4 = (f32[4,8,256]{2,1,0:T(8,128)S(1)}, f32[4,8,256]{2,1,0:T(8,128)}, u32[]{:S(2)}) copy-start(f32[4,8,256]{2,1,0:T(8,128)} %constant.14.clone.refs_4_) | copy-start | bytes 98308
  36.8 4.6 %collective-permute-start.14 = (f32[64,256]{1,0:T(8,128)S(1)}, f32[64,256]{1,0:T(8,128)S(1)}, u32[]{:S(2)}, u32[]{:S(2)}) collective-permute-start(f32[64,256]{1,0:T(8,128)S(1)} %shard_map.142.refs_0_), channel_id=1, source_target_pairs={{0,1},{1,0},{2,3},{3,2},{4,5},{5,4},{6,7},{7,6},{8,9},{9,8},{10,11... | collective-permute-start | bytes 196616 | tf_op jit(solution)/shard_map/ppermute | solution.py:442
  37.0 5.0 %collective-permute-start.15 = (f32[64,256]{1,0:T(8,128)S(1)}, f32[64,256]{1,0:T(8,128)S(1)}, u32[]{:S(2)}, u32[]{:S(2)}) collective-permute-start(f32[64,256]{1,0:T(8,128)S(1)} %shard_map.142.refs_0_), channel_id=1, source_target_pairs={{0,2},{1,3},{2,0},{3,1},{4,6},{5,7},{6,4},{7,5},{8,10},{9,11},{10,... | collective-permute-start | bytes 196616 | tf_op jit(solution)/shard_map/ppermute | solution.py:442
  37.9 5.2 %collective-permute-start.16 = (f32[64,256]{1,0:T(8,128)S(1)}, f32[64,256]{1,0:T(8,128)S(1)}, u32[]{:S(2)}, u32[]{:S(2)}) collective-permute-start(f32[64,256]{1,0:T(8,128)S(1)} %shard_map.142.refs_0_), channel_id=1, source_target_pairs={{0,3},{1,2},{2,1},{3,0},{4,7},{5,6},{6,5},{7,4},{8,11},{9,10},{10,... | collective-permute-start | bytes 196616 | tf_op jit(solution)/shard_map/ppermute | solution.py:442

commit v6 on v5

--- a/solution.py
+++ b/solution.py
@@ -50,27 +50,34 @@
     return jnp.concatenate([value[half:], value[:half]], axis=0)
 
 
-def columns_kernel(both_ref, last_ref, first_ref, strip):
+def by_parity(axis, for_even, for_odd):
+    return jnp.where(lax.axis_index(axis) % 2 == 0, for_even, for_odd)
+
+
+def columns_kernel(both_ref, near_ref, far_ref, strip):
     cells, breadth = both_ref.shape
     strip[cells:, :] = jnp.zeros((128 - cells, 128), f32)
-    for side, out in ((0, first_ref), (breadth - 128, last_ref)):
-        strip[:cells, :] = both_ref[:, side : side + 128]
-        turned = strip[...].T
-        out[...] = turned[0:8] if side == 0 else turned[120:128]
-
-
-def rows_kernel(both_ref, right_ref, left_ref, order_ref, order_too_ref, last_ref, first_ref, beside_ref, strip):
+    strip[:cells, :] = both_ref[:, :128]
+    first = strip[...].T[0:8]
+    strip[:cells, :] = both_ref[:, breadth - 128 :]
+    last = strip[...].T[120:128]
+    near_ref[...] = by_parity("gy", last, first)
+    far_ref[...] = by_parity("gy", first, last)
+
+
+def rows_kernel(both_ref, from_near_ref, from_far_ref, order_ref, order_too_ref, near_ref, far_ref, beside_ref, strip):
     height, breadth = both_ref.shape[0] // 2, both_ref.shape[1]
+    from_near, from_far = from_near_ref[...], from_far_ref[...]
     strip[...] = jnp.zeros_like(strip)
-    strip[0:4, :] = right_ref[0:4, :]
-    strip[124:128, :] = left_ref[4:8, :]
-    beside_ref[...] = strip[...].T[: 2 * height]
-    for q in range(2):
-        start, end, own = height * q, height * (q + 1), slice(4 * q, 4 * q + 4)
-        last_ref[own, :breadth] = both_ref[end - 4 : end, :]
-        last_ref[own, breadth:] = beside_ref[end - 4 : end, :]
-        first_ref[own, :breadth] = both_ref[start : start + 4, :]
-        first_ref[own, breadth:] = beside_ref[start : start + 4, :]
+    strip[0:4, :] = by_parity("gy", from_near, from_far)[0:4]
+    strip[124:128, :] = by_parity("gy", from_far, from_near)[4:8]
+    beside = strip[...].T[: 2 * height]
+    beside_ref[...] = beside
+    whole = jnp.concatenate([both_ref[...], beside], axis=1)
+    last = jnp.concatenate([whole[height - 4 : height], whole[2 * height - 4 :]], axis=0)
+    first = jnp.concatenate([whole[:4], whole[height : height + 4]], axis=0)
+    near_ref[...] = by_parity("gx", last, first)
+    far_ref[...] = by_parity("gx", first, last)
 
 
 def first_weights_kernel(taps_ref, biases_ref, k1_ref, c1_ref, c2_ref, c3_ref, *, rows):
@@ -215,7 +222,7 @@
 
 
 def advance_kernel(
-    both_ref, beside_ref, bot_ref, top_ref, w1_ref, w2_ref, even_ref, odd_ref, b1_ref, b2_ref, b3_ref,
+    both_ref, beside_ref, from_near_ref, from_far_ref, w1_ref, w2_ref, even_ref, odd_ref, b1_ref, b2_ref, b3_ref,
     first_ref, second_ref, coeff_ref, star_ref, field, outer_first, outer_second, outer_coeff,
 ):
     height, breadth = both_ref.shape[0] // 2, both_ref.shape[1]
@@ -223,9 +230,11 @@
     groups = rows // 4
     lanes = breadth + 128
     fill(field, both_ref, beside_ref, height, breadth)
+    from_near, from_far = from_near_ref[...], from_far_ref[...]
+    below, above = by_parity("gx", from_near, from_far), by_parity("gx", from_far, from_near)
     for q in range(2):
-        field[q, 8 + height : 12 + height, :] = bot_ref[4 * q : 4 * q + 4, :]
-        field[q, 12 + height : 16 + height, :] = top_ref[4 * q : 4 * q + 4, :]
+        field[q, 8 + height : 12 + height, :] = below[4 * q : 4 * q + 4]
+        field[q, 12 + height : 16 + height, :] = above[4 * q : 4 * q + 4]
         field[q, 0:8, :] = field[q, rows : rows + 8, :]
         field[q, 8 + rows : 16 + rows, :] = field[q, 8:16, :]
     patches = patches_of(field, rows, w1_ref.shape[1])
@@ -460,15 +469,18 @@
     span = breadth + 16
     shape = jax.ShapeDtypeStruct
 
-    def shifted(value, axis, distance):
+    def swapped(near, far, axis):
         peers = lax.axis_size(axis)
-        return lax.ppermute(value, axis, [(i, (i + distance) % peers) for i in range(peers)])
+        after, before = lambda i: (i + 1) % peers, lambda i: (i - 1) % peers
+        pairs = [(i, before(i) if i % 2 else after(i)) for i in range(peers)]
+        other_pairs = [(i, after(i) if i % 2 else before(i)) for i in range(peers)]
+        return lax.ppermute(near, axis, pairs), lax.ppermute(far, axis, other_pairs)
 
     with jax.named_scope("columns_around"):
         both = jnp.stack([u_field, v_field]).reshape(2 * height, breadth)
         edge = shape((8, 128), f32)
-        last, first = call(columns_kernel, (edge, edge), (pltpu.VMEM((128, 128), f32),))(both)
-        left, right = shifted(last, "gy", 1), shifted(first, "gy", -1)
+        near, far = call(columns_kernel, (edge, edge), (pltpu.VMEM((128, 128), f32),))(both)
+        near, far = swapped(near, far, "gy")
 
     with jax.named_scope("weights"):
         taps = w_first.transpose(0, 2, 1).astype(f32)
@@ -490,10 +502,10 @@
 
     with jax.named_scope("rows_around"):
         edge = shape((8, breadth + 128), f32)
-        last, first, beside = call(
+        near, far, beside = call(
             rows_kernel, (edge, edge, shape((2 * height, 128), f32)), (pltpu.VMEM((128, 128), f32),)
-        )(both, right, left, biases[2], order)
-        top, bottom = shifted(last, "gx", 1), shifted(first, "gx", -1)
+        )(both, near, far, biases[2], order)
+        near, far = swapped(near, far, "gx")
 
     block = shape((2 * height, breadth), f32)
     padded = pltpu.VMEM((2, rows + 16, breadth + 128), f32)
@@ -518,7 +530,7 @@
                 pltpu.VMEM((groups - 3, 64, breadth + 128), f32),
             ),
             flops=10**9,
-        )(both, beside, bottom, top, kernel_1, *others, *biases, *inner)
+        )(both, beside, near, far, kernel_1, *others, *biases, *inner)
 
     column, row, twiddle_out, twiddle_home = tables(height, breadth, members_x, members_y)
     column, row = [jnp.asarray(t) for t in column], jnp.asarray(row)

time: 44 us -> 43.2 us (0.982)
  waiting for transfers between devices: 15.7 us -> 12 us
  starting transfers between devices: 16.5 us -> 19.4 us
    ppermute x4, waiting for transfers between devices: 4.43 us -> 0.01 us  [the longest x2 0.01 us: swapped(): lax.ppermute(near, axis, pairs)]
    ppermute x4, starting transfers between devices: 5.62 us -> 8.27 us  [the longest x2 5.19 us: swapped(): lax.ppermute(far, axis, other_pairs)]
    ppermute x13, waiting for transfers between devices: 11.3 us -> 12 us  [partner(): lax.ppermute(block, axis, [(i, i ^ k) for i in range(lax.axis_size(axis))])]
  transfers between devices with their start and end apart: 17 -> 17, of which waited for: 13 -> 11; matrix products, arithmetic and copies ran while one was open for 6% -> 6% of each run, Pallas kernels for 6% -> 6%
where the time goes in v6:
time: 43.2 us; the launch traced here: 43 us
  starting transfers between devices  19.4 us (45%)
  waiting for transfers between devices  12 us (28%)
  Pallas kernels  7.54 us (17%)
  other arithmetic  3.21 us (7%)
  between operations  0.78 us (2%)
    ppermute x13, waiting for transfers between devices, partner(): lax.ppermute(block, axis, [(i, i ^ k) for i in range(lax.axis_size(axis))])  12 us
    ppermute x13, starting transfers between devices, partner(): lax.ppermute(block, axis, [(i, i ^ k) for i in range(lax.axis_size(axis))])  11.2 us
    ppermute x2, starting transfers between devices, swapped(): lax.ppermute(far, axis, other_pairs)  5.19 us
    ppermute x2, starting transfers between devices, swapped(): lax.ppermute(near, axis, pairs)  3.08 us
    pallas_call x1, Pallas kernels, on_device(): call(advance_kernel, block, (padded, pltpu.VMEM((4, span, 256), bf16), pl...  2.57 us
    pallas_call x1, Pallas kernels, on_device(): call(inner_kernel, (shape((groups - 4, span, 256), bf16), shape((groups -...  1.79 us
    pallas_call x1, Pallas kernels, on_device(): call(row_kernel, block, (pltpu.VMEM((grid_x, 2 * breadth), f32),))  1.22 us
    concatenate x1, other arithmetic, on_device(): jnp.concatenate([w_second.reshape(576, 64), w_third.reshape(144, 64)], ax...  0.97 us
  transfers between devices with their start and end apart: 17, of which 11 were waited for; matrix products, arithmetic and copies ran while one was open for 6% of the time, Pallas kernels for 6%

profile of v6, /device:TPU:0, one launch (start us, length us, event | category | flops | bytes accessed | tf_op | source)
XLA Modules:
  0.0 43.0 jit_solution(8899335171486871010)
XLA Ops:
  0.6 0.8 %pad_maximum_fusion.1 = f32[2,32,256]{2,1,0:T(8,128)S(1)} fusion(f32[1,32,256]{2,1,0:T(8,128)} %bitcast.15, f32[1,32,256]{2,1,0:T(8,128)} %bitcast.16), kind=kLoop, calls=%fused_computation.1 | loop fusion | flops 16384 | bytes 131072 | tf_op jit(solution)/shard_map/columns_around/stack | solution.py:480
  1.5 3.0 %collective-permute-start = (f32[8,128]{1,0:T(8,128)S(1)}, f32[8,128]{1,0:T(8,128)S(1)}, u32[]{:S(2)}, u32[]{:S(2)}) collective-permute-start(f32[8,128]{1,0:T(8,128)S(1)} %get-tuple-element.18), channel_id=1, source_target_pairs={{0,1},{1,0},{2,3},{3,2},{4,5},{5,4},{6,7},{7,6},{8,9},{9,8},{10,11... | collective-permute-start | bytes 12296 | tf_op jit(solution)/shard_map/columns_around/ppermute | solution.py:477
  4.5 1.5 %collective-permute-start.1 = (f32[8,128]{1,0:T(8,128)S(1)}, f32[8,128]{1,0:T(8,128)S(1)}, u32[]{:S(2)}, u32[]{:S(2)}) collective-permute-start(f32[8,128]{1,0:T(8,128)S(1)} %get-tuple-element.19), channel_id=1, source_target_pairs={{0,3},{1,2},{2,1},{3,0},{4,7},{5,6},{6,5},{7,4},{8,11},{9,10},{10,... | collective-permute-start | bytes 12296 | tf_op jit(solution)/shard_map/columns_around/ppermute | solution.py:477
  6.0 0.7 %convert_bitcast_fusion.taps_ref = f32[9,2,64]{2,1,0:T(2,128)S(1)} fusion(bf16[9,64,2]{1,2,0:T(2,128)(2,1)} %param.15), kind=kLoop, calls=%fused_computation.2 | loop fusion | flops 1152 | bytes 6912 | tf_op jit(solution)/shard_map/weights/convert_element_type | solution.py:486
  6.7 1.0 %pad_maximum_fusion.packed_ref = bf16[720,64]{1,0:T(8,128)(2,1)S(1)} fusion(bf16[144,64]{1,0:T(8,128)(2,1)} %bitcast.14, bf16[576,64]{1,0:T(8,128)(2,1)} %bitcast.13), kind=kLoop, calls=%fused_computation | loop fusion | flops 184320 | bytes 184320 | tf_op jit(solution)/shard_map/weights/concatenate | solution.py:497
  7.6 0.8 %pad_maximum_fusion.2 = f32[144]{0:T(256)S(1)} fusion(f32[16]{0:T(128)} %param.20, f32[64]{0:T(128)} %param.18, f32[64]{0:T(128)} %param.16), kind=kLoop, calls=%fused_computation.3 | loop fusion | flops 288 | bytes 1152 | tf_op jit(solution)/shard_map/weights/concatenate | solution.py:487
  9.4 3.7 %collective-permute-start.3 = (f32[8,384]{1,0:T(8,128)S(1)}, f32[8,384]{1,0:T(8,128)S(1)}, u32[]{:S(2)}, u32[]{:S(2)}) collective-permute-start(f32[8,384]{1,0:T(8,128)S(1)} %get-tuple-element.24), channel_id=1, source_target_pairs={{0,28},{4,8},{8,4},{12,16},{16,12},{20,24},{24,20},{28,0},{1,29},{... | collective-permute-start | bytes 36872 | tf_op jit(solution)/shard_map/rows_around/ppermute | solution.py:477
  13.1 1.8 %advance.2 = (bf16[6,272,256]{2,1,0:T(8,128)(2,1)S(1)}, bf16[4,272,256]{2,1,0:T(8,128)(2,1)S(1)}, f32[2,64,384]{2,1,0:T(8,128)S(1)}) custom-call(f32[64,256]{1,0:T(8,128)S(1)} %bitcast.10, f32[64,128]{1,0:T(8,128)S(1)} %get-tuple-element.22.beside_ref, bf16[10,256,256]{2,1,0:T(8,128)(2,1)S(1)} %get-tuple-element.25.w1_ref, ...), custom_call_target="tpu_custom_call" | custom-call | flops 500000000 | bytes 1048576 | tf_op jit(solution)/shard_map/advance/pallas_call | solution.py:513
  14.9 2.6 %advance.3.refs_0_.refs_5_ = f32[64,256]{1,0:T(8,128)S(1)} custom-call(f32[64,256]{1,0:T(8,128)S(1)} %bitcast.11, f32[64,128]{1,0:T(8,128)S(1)} %get-tuple-element.22.beside_ref, f32[8,384]{1,0:T(8,128)S(1)} %collective-permute-done.2.from_near_ref, f32[8,384]{1,0:T(8,128)S(1)} %collective-permute-done.3.from_far_ref, ...), custom_call_target="tpu_custom_call" | custom-call | flops 1000000000 | bytes 1048576 | tf_op jit(solution)/shard_map/advance/pallas_call | solution.py:523
  17.5 1.5 %collective-permute-start.4 = (f32[64,256]{1,0:T(8,128)S(1)}, f32[64,256]{1,0:T(8,128)S(1)}, u32[]{:S(2)}, u32[]{:S(2)}) collective-permute-start(f32[64,256]{1,0:T(8,128)S(1)} %advance.3.refs_0_.refs_5_), channel_id=1, source_target_pairs={{0,1},{1,0},{2,3},{3,2},{4,5},{5,4},{6,7},{7,6},{8,9},{9,8},{10,11... | collective-permute-start | bytes 196616 | tf_op jit(solution)/shard_map/ppermute | solution.py:451
  19.5 1.5 %collective-permute-start.6 = (f32[64,256]{1,0:T(8,128)S(1)}, f32[64,256]{1,0:T(8,128)S(1)}, u32[]{:S(2)}, u32[]{:S(2)}) collective-permute-start(f32[64,256]{1,0:T(8,128)S(1)} %advance.3.refs_0_.refs_5_), channel_id=1, source_target_pairs={{0,3},{1,2},{2,1},{3,0},{4,7},{5,6},{6,5},{7,4},{8,11},{9,10},{10,... | collective-permute-start | bytes 196616 | tf_op jit(solution)/shard_map/ppermute | solution.py:451
  21.0 1.0 %collective-permute-done.4.refs_1_ = f32[64,256]{1,0:T(8,128)S(1)} collective-permute-done((f32[64,256]{1,0:T(8,128)S(1)}, f32[64,256]{1,0:T(8,128)S(1)}, u32[]{:S(2)}, u32[]{:S(2)}) %collective-permute-start.4) | collective-permute-done | bytes 65568 | tf_op jit(solution)/shard_map/ppermute | solution.py:451
  22.0 1.3 %collective-permute-done.5.refs_2_ = f32[64,256]{1,0:T(8,128)S(1)} collective-permute-done((f32[64,256]{1,0:T(8,128)S(1)}, f32[64,256]{1,0:T(8,128)S(1)}, u32[]{:S(2)}, u32[]{:S(2)}) %collective-permute-start.5) | collective-permute-done | bytes 65568 | tf_op jit(solution)/shard_map/ppermute | solution.py:451
  23.3 1.4 %collective-permute-done.6.refs_3_ = f32[64,256]{1,0:T(8,128)S(1)} collective-permute-done((f32[64,256]{1,0:T(8,128)S(1)}, f32[64,256]{1,0:T(8,128)S(1)}, u32[]{:S(2)}, u32[]{:S(2)}) %collective-permute-start.6) | collective-permute-done | bytes 65568 | tf_op jit(solution)/shard_map/ppermute | solution.py:451
  25.2 1.4 %collective-permute-start.12 = (f32[64,256]{1,0:T(8,128)S(1)}, f32[64,256]{1,0:T(8,128)S(1)}, u32[]{:S(2)}, u32[]{:S(2)}) collective-permute-start(f32[64,256]{1,0:T(8,128)S(1)} %shard_map.140.refs_0_), channel_id=1, source_target_pairs={{0,24},{4,28},{8,16},{12,20},{16,8},{20,12},{24,0},{28,4},{1,25},{... | collective-permute-start | bytes 196616 | tf_op jit(solution)/shard_map/ppermute | solution.py:451
  26.6 1.9 %collective-permute-start.8 = (f32[64,256]{1,0:T(8,128)S(1)}, f32[64,256]{1,0:T(8,128)S(1)}, u32[]{:S(2)}, u32[]{:S(2)}) collective-permute-start(f32[64,256]{1,0:T(8,128)S(1)} %shard_map.140.refs_0_), channel_id=1, source_target_pairs={{0,8},{4,12},{8,0},{12,4},{16,24},{20,28},{24,16},{28,20},{1,9},{5... | collective-permute-start | bytes 196616 | tf_op jit(solution)/shard_map/ppermute | solution.py:451
  28.5 3.6 %collective-permute-done.10.refs_4_ = f32[64,256]{1,0:T(8,128)S(1)} collective-permute-done((f32[64,256]{1,0:T(8,128)S(1)}, f32[64,256]{1,0:T(8,128)S(1)}, u32[]{:S(2)}, u32[]{:S(2)}) %collective-permute-start.10) | collective-permute-done | bytes 65568 | tf_op jit(solution)/shard_map/ppermute | solution.py:451
  34.1 1.2 %shard_map.142.refs_0_ = f32[64,256]{1,0:T(8,128)S(1)} custom-call(f32[64,256]{1,0:T(8,128)S(1)} %shard_map.140.refs_0_, f32[64,256]{1,0:T(8,128)S(1)} %collective-permute-done.7.refs_1_, f32[64,256]{1,0:T(8,128)S(1)} %collective-permute-done.8.refs_2_, f32[64,256]{1,0:T(8,128)S(1)} %collective-permute-done.9.refs_3_, ...), custom_call_target="tpu_custom_call" | custom-call | flops 10000000 | bytes 1048576 | tf_op jit(solution)/shard_map/pallas_call | solution.py:541
  35.3 1.0 %collective-permute-start.14 = (f32[64,256]{1,0:T(8,128)S(1)}, f32[64,256]{1,0:T(8,128)S(1)}, u32[]{:S(2)}, u32[]{:S(2)}) collective-permute-start(f32[64,256]{1,0:T(8,128)S(1)} %shard_map.142.refs_0_), channel_id=1, source_target_pairs={{0,1},{1,0},{2,3},{3,2},{4,5},{5,4},{6,7},{7,6},{8,9},{9,8},{10,11... | collective-permute-start | bytes 196616 | tf_op jit(solution)/shard_map/ppermute | solution.py:451
  36.3 0.8 %collective-permute-start.15 = (f32[64,256]{1,0:T(8,128)S(1)}, f32[64,256]{1,0:T(8,128)S(1)}, u32[]{:S(2)}, u32[]{:S(2)}) collective-permute-start(f32[64,256]{1,0:T(8,128)S(1)} %shard_map.142.refs_0_), channel_id=1, source_target_pairs={{0,2},{1,3},{2,0},{3,1},{4,6},{5,7},{6,4},{7,5},{8,10},{9,11},{10,... | collective-permute-start | bytes 196616 | tf_op jit(solution)/shard_map/ppermute | solution.py:451
  37.1 1.7 %collective-permute-start.16 = (f32[64,256]{1,0:T(8,128)S(1)}, f32[64,256]{1,0:T(8,128)S(1)}, u32[]{:S(2)}, u32[]{:S(2)}) collective-permute-start(f32[64,256]{1,0:T(8,128)S(1)} %shard_map.142.refs_0_), channel_id=1, source_target_pairs={{0,3},{1,2},{2,1},{3,0},{4,7},{5,6},{6,5},{7,4},{8,11},{9,10},{10,... | collective-permute-start | bytes 196616 | tf_op jit(solution)/shard_map/ppermute | solution.py:451
  38.8 0.8 %collective-permute-done.14.refs_1_ = f32[64,256]{1,0:T(8,128)S(1)} collective-permute-done((f32[64,256]{1,0:T(8,128)S(1)}, f32[64,256]{1,0:T(8,128)S(1)}, u32[]{:S(2)}, u32[]{:S(2)}) %collective-permute-start.14) | collective-permute-done | bytes 65568 | tf_op jit(solution)/shard_map/ppermute | solution.py:451
  39.6 1.6 %collective-permute-done.15.refs_2_ = f32[64,256]{1,0:T(8,128)S(1)} collective-permute-done((f32[64,256]{1,0:T(8,128)S(1)}, f32[64,256]{1,0:T(8,128)S(1)}, u32[]{:S(2)}, u32[]{:S(2)}) %collective-permute-start.15) | collective-permute-done | bytes 65568 | tf_op jit(solution)/shard_map/ppermute | solution.py:451
  41.3 1.0 %collective-permute-done.16.refs_3_ = f32[64,256]{1,0:T(8,128)S(1)} collective-permute-done((f32[64,256]{1,0:T(8,128)S(1)}, f32[64,256]{1,0:T(8,128)S(1)}, u32[]{:S(2)}, u32[]{:S(2)}) %collective-permute-start.16) | collective-permute-done | bytes 65568 | tf_op jit(solution)/shard_map/ppermute | solution.py:451
  (34 shorter events, 4.6 us)
Async XLA Ops:
  1.5 7.7 %collective-permute-start = (f32[8,128]{1,0:T(8,128)S(1)}, f32[8,128]{1,0:T(8,128)S(1)}, u32[]{:S(2)}, u32[]{:S(2)}) collective-permute-start(f32[8,128]{1,0:T(8,128)S(1)} %get-tuple-element.18), channel_id=1, source_target_pairs={{0,1},{1,0},{2,3},{3,2},{4,5},{5,4},{6,7},{7,6},{8,9},{9,8},{10,11... | collective-permute-start | bytes 12296 | tf_op jit(solution)/shard_map/columns_around/ppermute | solution.py:477
  4.5 4.7 %collective-permute-start.1 = (f32[8,128]{1,0:T(8,128)S(1)}, f32[8,128]{1,0:T(8,128)S(1)}, u32[]{:S(2)}, u32[]{:S(2)}) collective-permute-start(f32[8,128]{1,0:T(8,128)S(1)} %get-tuple-element.19), channel_id=1, source_target_pairs={{0,3},{1,2},{2,1},{3,0},{4,7},{5,6},{6,5},{7,4},{8,11},{9,10},{10,... | collective-permute-start | bytes 12296 | tf_op jit(solution)/shard_map/columns_around/ppermute | solution.py:477
  9.3 5.6 %collective-permute-start.2 = (f32[8,384]{1,0:T(8,128)S(1)}, f32[8,384]{1,0:T(8,128)S(1)}, u32[]{:S(2)}, u32[]{:S(2)}) collective-permute-start(f32[8,384]{1,0:T(8,128)S(1)} %get-tuple-element.23), channel_id=1, source_target_pairs={{0,4},{4,0},{8,12},{12,8},{16,20},{20,16},{24,28},{28,24},{1,5},{5... | collective-permute-start | bytes 36872 | tf_op jit(solution)/shard_map/rows_around/ppermute | solution.py:477
  9.4 5.5 %collective-permute-start.3 = (f32[8,384]{1,0:T(8,128)S(1)}, f32[8,384]{1,0:T(8,128)S(1)}, u32[]{:S(2)}, u32[]{:S(2)}) collective-permute-start(f32[8,384]{1,0:T(8,128)S(1)} %get-tuple-element.24), channel_id=1, source_target_pairs={{0,28},{4,8},{8,4},{12,16},{16,12},{20,24},{24,20},{28,0},{1,29},{... | collective-permute-start | bytes 36872 | tf_op jit(solution)/shard_map/rows_around/ppermute | solution.py:477
  14.9 9.8 %copy-start = (bf16[256,512]{1,0:T(8,128)(2,1)S(1)}, bf16[256,512]{1,0:T(8,128)(2,1)}, u32[]{:S(2)}) copy-start(bf16[256,512]{1,0:T(8,128)(2,1)} %constant.10.clone.refs_5_.refs_10_) | copy-start | bytes 786436
  14.9 9.8 %copy-start.1 = (bf16[256,512]{1,0:T(8,128)(2,1)S(1)}, bf16[256,512]{1,0:T(8,128)(2,1)}, u32[]{:S(2)}) copy-start(bf16[256,512]{1,0:T(8,128)(2,1)} %constant.11.clone.refs_6_.refs_11_) | copy-start | bytes 786436
  14.9 9.8 %copy-start.3 = (f32[4,8,256]{2,1,0:T(8,128)S(1)}, f32[4,8,256]{2,1,0:T(8,128)}, u32[]{:S(2)}) copy-start(f32[4,8,256]{2,1,0:T(8,128)} %constant.13.clone.refs_4_) | copy-start | bytes 98308
  17.5 16.6 %copy-start.2 = (bf16[1024,256]{1,0:T(8,128)(2,1)S(1)}, bf16[1024,256]{1,0:T(8,128)(2,1)}, u32[]{:S(2)}) copy-start(bf16[1024,256]{1,0:T(8,128)(2,1)} %constant.12.clone.refs_9_) | copy-start | bytes 1572868
  17.5 4.5 %collective-permute-start.4 = (f32[64,256]{1,0:T(8,128)S(1)}, f32[64,256]{1,0:T(8,128)S(1)}, u32[]{:S(2)}, u32[]{:S(2)}) collective-permute-start(f32[64,256]{1,0:T(8,128)S(1)} %advance.3.refs_0_.refs_5_), channel_id=1, source_target_pairs={{0,1},{1,0},{2,3},{3,2},{4,5},{5,4},{6,7},{7,6},{8,9},{9,8},{10,11... | collective-permute-start | bytes 196616 | tf_op jit(solution)/shard_map/ppermute | solution.py:451
  19.0 4.3 %collective-permute-start.5 = (f32[64,256]{1,0:T(8,128)S(1)}, f32[64,256]{1,0:T(8,128)S(1)}, u32[]{:S(2)}, u32[]{:S(2)}) collective-permute-start(f32[64,256]{1,0:T(8,128)S(1)} %advance.3.refs_0_.refs_5_), channel_id=1, source_target_pairs={{0,2},{1,3},{2,0},{3,1},{4,6},{5,7},{6,4},{7,5},{8,10},{9,11},{10,... | collective-permute-start | bytes 196616 | tf_op jit(solution)/shard_map/ppermute | solution.py:451
  19.5 5.2 %collective-permute-start.6 = (f32[64,256]{1,0:T(8,128)S(1)}, f32[64,256]{1,0:T(8,128)S(1)}, u32[]{:S(2)}, u32[]{:S(2)}) collective-permute-start(f32[64,256]{1,0:T(8,128)S(1)} %advance.3.refs_0_.refs_5_), channel_id=1, source_target_pairs={{0,3},{1,2},{2,1},{3,0},{4,7},{5,6},{6,5},{7,4},{8,11},{9,10},{10,... | collective-permute-start | bytes 196616 | tf_op jit(solution)/shard_map/ppermute | solution.py:451
  25.0 7.2 %collective-permute-start.10 = (f32[64,256]{1,0:T(8,128)S(1)}, f32[64,256]{1,0:T(8,128)S(1)}, u32[]{:S(2)}, u32[]{:S(2)}) collective-permute-start(f32[64,256]{1,0:T(8,128)S(1)} %shard_map.140.refs_0_), channel_id=1, source_target_pairs={{0,16},{4,20},{8,24},{12,28},{16,0},{20,4},{24,8},{28,12},{1,17},{... | collective-permute-start | bytes 196616 | tf_op jit(solution)/shard_map/ppermute | solution.py:451
  25.2 6.9 %collective-permute-start.12 = (f32[64,256]{1,0:T(8,128)S(1)}, f32[64,256]{1,0:T(8,128)S(1)}, u32[]{:S(2)}, u32[]{:S(2)}) collective-permute-start(f32[64,256]{1,0:T(8,128)S(1)} %shard_map.140.refs_0_), channel_id=1, source_target_pairs={{0,24},{4,28},{8,16},{12,20},{16,8},{20,12},{24,0},{28,4},{1,25},{... | collective-permute-start | bytes 196616 | tf_op jit(solution)/shard_map/ppermute | solution.py:451
  26.6 6.2 %collective-permute-start.8 = (f32[64,256]{1,0:T(8,128)S(1)}, f32[64,256]{1,0:T(8,128)S(1)}, u32[]{:S(2)}, u32[]{:S(2)}) collective-permute-start(f32[64,256]{1,0:T(8,128)S(1)} %shard_map.140.refs_0_), channel_id=1, source_target_pairs={{0,8},{4,12},{8,0},{12,4},{16,24},{20,28},{24,16},{28,20},{1,9},{5... | collective-permute-start | bytes 196616 | tf_op jit(solution)/shard_map/ppermute | solution.py:451
  28.5 4.5 %collective-permute-start.7 = (f32[64,256]{1,0:T(8,128)S(1)}, f32[64,256]{1,0:T(8,128)S(1)}, u32[]{:S(2)}, u32[]{:S(2)}) collective-permute-start(f32[64,256]{1,0:T(8,128)S(1)} %shard_map.140.refs_0_), channel_id=1, source_target_pairs={{0,4},{4,0},{8,12},{12,8},{16,20},{20,16},{24,28},{28,24},{1,5},{5... | collective-permute-start | bytes 196616 | tf_op jit(solution)/shard_map/ppermute | solution.py:451
  32.1 1.3 %collective-permute-start.11 = (f32[64,256]{1,0:T(8,128)S(1)}, f32[64,256]{1,0:T(8,128)S(1)}, u32[]{:S(2)}, u32[]{:S(2)}) collective-permute-start(f32[64,256]{1,0:T(8,128)S(1)} %collective-permute-done.10.refs_4_), channel_id=1, source_target_pairs={{0,4},{4,0},{8,12},{12,8},{16,20},{20,16},{24,28},{28,24},{1,5},{5... | collective-permute-start | bytes 196616 | tf_op jit(solution)/shard_map/ppermute | solution.py:451
  32.1 1.4 %collective-permute-start.13 = (f32[64,256]{1,0:T(8,128)S(1)}, f32[64,256]{1,0:T(8,128)S(1)}, u32[]{:S(2)}, u32[]{:S(2)}) collective-permute-start(f32[64,256]{1,0:T(8,128)S(1)} %collective-permute-done.12.refs_6_), channel_id=1, source_target_pairs={{0,4},{4,0},{8,12},{12,8},{16,20},{20,16},{24,28},{28,24},{1,5},{5... | collective-permute-start | bytes 196616 | tf_op jit(solution)/shard_map/ppermute | solution.py:451
  32.8 1.3 %collective-permute-start.9 = (f32[64,256]{1,0:T(8,128)S(1)}, f32[64,256]{1,0:T(8,128)S(1)}, u32[]{:S(2)}, u32[]{:S(2)}) collective-permute-start(f32[64,256]{1,0:T(8,128)S(1)} %collective-permute-done.8.refs_2_), channel_id=1, source_target_pairs={{0,4},{4,0},{8,12},{12,8},{16,20},{20,16},{24,28},{28,24},{1,5},{5... | collective-permute-start | bytes 196616 | tf_op jit(solution)/shard_map/ppermute | solution.py:451
  33.0 9.3 %copy-start.4 = (f32[4,8,256]{2,1,0:T(8,128)S(1)}, f32[4,8,256]{2,1,0:T(8,128)}, u32[]{:S(2)}) copy-start(f32[4,8,256]{2,1,0:T(8,128)} %constant.14.clone.refs_4_) | copy-start | bytes 98308
  35.3 4.3 %collective-permute-start.14 = (f32[64,256]{1,0:T(8,128)S(1)}, f32[64,256]{1,0:T(8,128)S(1)}, u32[]{:S(2)}, u32[]{:S(2)}) collective-permute-start(f32[64,256]{1,0:T(8,128)S(1)} %shard_map.142.refs_0_), channel_id=1, source_target_pairs={{0,1},{1,0},{2,3},{3,2},{4,5},{5,4},{6,7},{7,6},{8,9},{9,8},{10,11... | collective-permute-start | bytes 196616 | tf_op jit(solution)/shard_map/ppermute | solution.py:451
  36.3 5.0 %collective-permute-start.15 = (f32[64,256]{1,0:T(8,128)S(1)}, f32[64,256]{1,0:T(8,128)S(1)}, u32[]{:S(2)}, u32[]{:S(2)}) collective-permute-start(f32[64,256]{1,0:T(8,128)S(1)} %shard_map.142.refs_0_), channel_id=1, source_target_pairs={{0,2},{1,3},{2,0},{3,1},{4,6},{5,7},{6,4},{7,5},{8,10},{9,11},{10,... | collective-permute-start | bytes 196616 | tf_op jit(solution)/shard_map/ppermute | solution.py:451
  37.1 5.2 %collective-permute-start.16 = (f32[64,256]{1,0:T(8,128)S(1)}, f32[64,256]{1,0:T(8,128)S(1)}, u32[]{:S(2)}, u32[]{:S(2)}) collective-permute-start(f32[64,256]{1,0:T(8,128)S(1)} %shard_map.142.refs_0_), channel_id=1, source_target_pairs={{0,3},{1,2},{2,1},{3,0},{4,7},{5,6},{6,5},{7,4},{8,11},{9,10},{10,... | collective-permute-start | bytes 196616 | tf_op jit(solution)/shard_map/ppermute | solution.py:451

commit v7 on v6

--- a/solution.py
+++ b/solution.py
@@ -107,8 +107,7 @@
         k1_ref[r] = block.astype(bf16)
 
 
-def other_weights_kernel(packed_ref, k2_ref, even_ref, odd_ref, order_ref):
-    order_ref[...] = jnp.zeros(order_ref.shape, f32)
+def other_weights_kernel(packed_ref, k2_ref, even_ref, odd_ref):
     slots = {-1: 5, 0: 0, 1: 1, 2: 2, 3: 3, 4: 6}
     blank = jnp.zeros((64, 64), f32)
     for c in range(3):
@@ -495,16 +494,16 @@
             ),
         )(taps, biases)
         packed = jnp.concatenate([w_second.reshape(576, 64), w_third.reshape(144, 64)], axis=0)
-        *others, order = call(
+        others = call(
             other_weights_kernel,
-            (shape((256, 384), bf16), shape((512, 256), bf16), shape((512, 256), bf16), shape((8, 128), f32)),
+            (shape((256, 384), bf16), shape((512, 256), bf16), shape((512, 256), bf16)),
         )(packed)
 
     with jax.named_scope("rows_around"):
         edge = shape((8, breadth + 128), f32)
         near, far, beside = call(
             rows_kernel, (edge, edge, shape((2 * height, 128), f32)), (pltpu.VMEM((128, 128), f32),)
-        )(both, near, far, biases[2], order)
+        )(both, near, far, biases[2], packed)
         near, far = swapped(near, far, "gx")
 
     block = shape((2 * height, breadth), f32)

time: 43.2 us -> 43.2 us (level)
  no operation moved by 1% of the time
where the time goes in v7:
time: 43.2 us; the launch traced here: 43 us
  starting transfers between devices  19.4 us (45%)
  waiting for transfers between devices  12 us (28%)
  Pallas kernels  7.57 us (18%)
  other arithmetic  3.21 us (7%)
  between operations  0.78 us (2%)
    ppermute x13, waiting for transfers between devices, partner(): lax.ppermute(block, axis, [(i, i ^ k) for i in range(lax.axis_size(axis))])  12 us
    ppermute x13, starting transfers between devices, partner(): lax.ppermute(block, axis, [(i, i ^ k) for i in range(lax.axis_size(axis))])  11.2 us
    ppermute x2, starting transfers between devices, swapped(): lax.ppermute(far, axis, other_pairs)  5.19 us
    ppermute x2, starting transfers between devices, swapped(): lax.ppermute(near, axis, pairs)  3.08 us
    pallas_call x1, Pallas kernels, on_device(): call(advance_kernel, block, (padded, pltpu.VMEM((4, span, 256), bf16), pl...  2.6 us
    pallas_call x1, Pallas kernels, on_device(): call(inner_kernel, (shape((groups - 4, span, 256), bf16), shape((groups -...  1.78 us
    pallas_call x1, Pallas kernels, on_device(): call(row_kernel, block, (pltpu.VMEM((grid_x, 2 * breadth), f32),))  1.22 us
    concatenate x1, other arithmetic, on_device(): jnp.concatenate([w_second.reshape(576, 64), w_third.reshape(144, 64)], ax...  0.97 us
  transfers between devices with their start and end apart: 17, of which 11 were waited for; matrix products, arithmetic and copies ran while one was open for 6% of the time, Pallas kernels for 6%

profile of v7, /device:TPU:0, one launch (start us, length us, event | category | flops | bytes accessed | tf_op | source)
XLA Modules:
  0.0 43.0 jit_solution(15674688894543730658)
XLA Ops:
  0.6 0.8 %pad_maximum_fusion.1 = f32[2,32,256]{2,1,0:T(8,128)S(1)} fusion(f32[1,32,256]{2,1,0:T(8,128)} %bitcast.15, f32[1,32,256]{2,1,0:T(8,128)} %bitcast.16), kind=kLoop, calls=%fused_computation.1 | loop fusion | flops 16384 | bytes 131072 | tf_op jit(solution)/shard_map/columns_around/stack | solution.py:479
  1.5 3.0 %collective-permute-start = (f32[8,128]{1,0:T(8,128)S(1)}, f32[8,128]{1,0:T(8,128)S(1)}, u32[]{:S(2)}, u32[]{:S(2)}) collective-permute-start(f32[8,128]{1,0:T(8,128)S(1)} %get-tuple-element.17), channel_id=1, source_target_pairs={{0,1},{1,0},{2,3},{3,2},{4,5},{5,4},{6,7},{7,6},{8,9},{9,8},{10,11... | collective-permute-start | bytes 12296 | tf_op jit(solution)/shard_map/columns_around/ppermute | solution.py:476
  4.5 1.5 %collective-permute-start.1 = (f32[8,128]{1,0:T(8,128)S(1)}, f32[8,128]{1,0:T(8,128)S(1)}, u32[]{:S(2)}, u32[]{:S(2)}) collective-permute-start(f32[8,128]{1,0:T(8,128)S(1)} %get-tuple-element.18), channel_id=1, source_target_pairs={{0,3},{1,2},{2,1},{3,0},{4,7},{5,6},{6,5},{7,4},{8,11},{9,10},{10,... | collective-permute-start | bytes 12296 | tf_op jit(solution)/shard_map/columns_around/ppermute | solution.py:476
  6.0 0.7 %convert_bitcast_fusion.taps_ref = f32[9,2,64]{2,1,0:T(2,128)S(1)} fusion(bf16[9,64,2]{1,2,0:T(2,128)(2,1)} %param.15), kind=kLoop, calls=%fused_computation.2 | loop fusion | flops 1152 | bytes 6912 | tf_op jit(solution)/shard_map/weights/convert_element_type | solution.py:485
  6.7 1.0 %pad_maximum_fusion.order_too_ref.packed_ref = bf16[720,64]{1,0:T(8,128)(2,1)S(1)} fusion(bf16[144,64]{1,0:T(8,128)(2,1)} %bitcast.14, bf16[576,64]{1,0:T(8,128)(2,1)} %bitcast.13), kind=kLoop, calls=%fused_computation | loop fusion | flops 184320 | bytes 184320 | tf_op jit(solution)/shard_map/weights/concatenate | solution.py:496
  7.6 0.8 %pad_maximum_fusion.2 = f32[144]{0:T(256)S(1)} fusion(f32[16]{0:T(128)} %param.20, f32[64]{0:T(128)} %param.18, f32[64]{0:T(128)} %param.16), kind=kLoop, calls=%fused_computation.3 | loop fusion | flops 288 | bytes 1152 | tf_op jit(solution)/shard_map/weights/concatenate | solution.py:486
  9.4 3.7 %collective-permute-start.3 = (f32[8,384]{1,0:T(8,128)S(1)}, f32[8,384]{1,0:T(8,128)S(1)}, u32[]{:S(2)}, u32[]{:S(2)}) collective-permute-start(f32[8,384]{1,0:T(8,128)S(1)} %get-tuple-element.22), channel_id=1, source_target_pairs={{0,28},{4,8},{8,4},{12,16},{16,12},{20,24},{24,20},{28,0},{1,29},{... | collective-permute-start | bytes 36872 | tf_op jit(solution)/shard_map/rows_around/ppermute | solution.py:476
  13.1 1.8 %advance.2 = (bf16[6,272,256]{2,1,0:T(8,128)(2,1)S(1)}, bf16[4,272,256]{2,1,0:T(8,128)(2,1)S(1)}, f32[2,64,384]{2,1,0:T(8,128)S(1)}) custom-call(f32[64,256]{1,0:T(8,128)S(1)} %bitcast.10, f32[64,128]{1,0:T(8,128)S(1)} %get-tuple-element.20.beside_ref, bf16[10,256,256]{2,1,0:T(8,128)(2,1)S(1)} %get-tuple-element.23.w1_ref, ...), custom_call_target="tpu_custom_call" | custom-call | flops 500000000 | bytes 1048576 | tf_op jit(solution)/shard_map/advance/pallas_call | solution.py:512
  14.9 2.6 %advance.3.refs_0_.refs_5_ = f32[64,256]{1,0:T(8,128)S(1)} custom-call(f32[64,256]{1,0:T(8,128)S(1)} %bitcast.11, f32[64,128]{1,0:T(8,128)S(1)} %get-tuple-element.20.beside_ref, f32[8,384]{1,0:T(8,128)S(1)} %collective-permute-done.2.from_near_ref, f32[8,384]{1,0:T(8,128)S(1)} %collective-permute-done.3.from_far_ref, ...), custom_call_target="tpu_custom_call" | custom-call | flops 1000000000 | bytes 1048576 | tf_op jit(solution)/shard_map/advance/pallas_call | solution.py:522
  17.5 1.5 %collective-permute-start.4 = (f32[64,256]{1,0:T(8,128)S(1)}, f32[64,256]{1,0:T(8,128)S(1)}, u32[]{:S(2)}, u32[]{:S(2)}) collective-permute-start(f32[64,256]{1,0:T(8,128)S(1)} %advance.3.refs_0_.refs_5_), channel_id=1, source_target_pairs={{0,1},{1,0},{2,3},{3,2},{4,5},{5,4},{6,7},{7,6},{8,9},{9,8},{10,11... | collective-permute-start | bytes 196616 | tf_op jit(solution)/shard_map/ppermute | solution.py:450
  19.6 1.5 %collective-permute-start.6 = (f32[64,256]{1,0:T(8,128)S(1)}, f32[64,256]{1,0:T(8,128)S(1)}, u32[]{:S(2)}, u32[]{:S(2)}) collective-permute-start(f32[64,256]{1,0:T(8,128)S(1)} %advance.3.refs_0_.refs_5_), channel_id=1, source_target_pairs={{0,3},{1,2},{2,1},{3,0},{4,7},{5,6},{6,5},{7,4},{8,11},{9,10},{10,... | collective-permute-start | bytes 196616 | tf_op jit(solution)/shard_map/ppermute | solution.py:450
  21.0 1.0 %collective-permute-done.4.refs_1_ = f32[64,256]{1,0:T(8,128)S(1)} collective-permute-done((f32[64,256]{1,0:T(8,128)S(1)}, f32[64,256]{1,0:T(8,128)S(1)}, u32[]{:S(2)}, u32[]{:S(2)}) %collective-permute-start.4) | collective-permute-done | bytes 65568 | tf_op jit(solution)/shard_map/ppermute | solution.py:450
  22.0 1.3 %collective-permute-done.5.refs_2_ = f32[64,256]{1,0:T(8,128)S(1)} collective-permute-done((f32[64,256]{1,0:T(8,128)S(1)}, f32[64,256]{1,0:T(8,128)S(1)}, u32[]{:S(2)}, u32[]{:S(2)}) %collective-permute-start.5) | collective-permute-done | bytes 65568 | tf_op jit(solution)/shard_map/ppermute | solution.py:450
  23.3 1.4 %collective-permute-done.6.refs_3_ = f32[64,256]{1,0:T(8,128)S(1)} collective-permute-done((f32[64,256]{1,0:T(8,128)S(1)}, f32[64,256]{1,0:T(8,128)S(1)}, u32[]{:S(2)}, u32[]{:S(2)}) %collective-permute-start.6) | collective-permute-done | bytes 65568 | tf_op jit(solution)/shard_map/ppermute | solution.py:450
  25.3 1.4 %collective-permute-start.12 = (f32[64,256]{1,0:T(8,128)S(1)}, f32[64,256]{1,0:T(8,128)S(1)}, u32[]{:S(2)}, u32[]{:S(2)}) collective-permute-start(f32[64,256]{1,0:T(8,128)S(1)} %shard_map.140.refs_0_), channel_id=1, source_target_pairs={{0,24},{4,28},{8,16},{12,20},{16,8},{20,12},{24,0},{28,4},{1,25},{... | collective-permute-start | bytes 196616 | tf_op jit(solution)/shard_map/ppermute | solution.py:450
  26.6 1.9 %collective-permute-start.8 = (f32[64,256]{1,0:T(8,128)S(1)}, f32[64,256]{1,0:T(8,128)S(1)}, u32[]{:S(2)}, u32[]{:S(2)}) collective-permute-start(f32[64,256]{1,0:T(8,128)S(1)} %shard_map.140.refs_0_), channel_id=1, source_target_pairs={{0,8},{4,12},{8,0},{12,4},{16,24},{20,28},{24,16},{28,20},{1,9},{5... | collective-permute-start | bytes 196616 | tf_op jit(solution)/shard_map/ppermute | solution.py:450
  28.5 3.6 %collective-permute-done.10.refs_4_ = f32[64,256]{1,0:T(8,128)S(1)} collective-permute-done((f32[64,256]{1,0:T(8,128)S(1)}, f32[64,256]{1,0:T(8,128)S(1)}, u32[]{:S(2)}, u32[]{:S(2)}) %collective-permute-start.10) | collective-permute-done | bytes 65568 | tf_op jit(solution)/shard_map/ppermute | solution.py:450
  34.1 1.2 %shard_map.142.refs_0_ = f32[64,256]{1,0:T(8,128)S(1)} custom-call(f32[64,256]{1,0:T(8,128)S(1)} %shard_map.140.refs_0_, f32[64,256]{1,0:T(8,128)S(1)} %collective-permute-done.7.refs_1_, f32[64,256]{1,0:T(8,128)S(1)} %collective-permute-done.8.refs_2_, f32[64,256]{1,0:T(8,128)S(1)} %collective-permute-done.9.refs_3_, ...), custom_call_target="tpu_custom_call" | custom-call | flops 10000000 | bytes 1048576 | tf_op jit(solution)/shard_map/pallas_call | solution.py:540
  35.3 1.0 %collective-permute-start.14 = (f32[64,256]{1,0:T(8,128)S(1)}, f32[64,256]{1,0:T(8,128)S(1)}, u32[]{:S(2)}, u32[]{:S(2)}) collective-permute-start(f32[64,256]{1,0:T(8,128)S(1)} %shard_map.142.refs_0_), channel_id=1, source_target_pairs={{0,1},{1,0},{2,3},{3,2},{4,5},{5,4},{6,7},{7,6},{8,9},{9,8},{10,11... | collective-permute-start | bytes 196616 | tf_op jit(solution)/shard_map/ppermute | solution.py:450
  36.3 0.8 %collective-permute-start.15 = (f32[64,256]{1,0:T(8,128)S(1)}, f32[64,256]{1,0:T(8,128)S(1)}, u32[]{:S(2)}, u32[]{:S(2)}) collective-permute-start(f32[64,256]{1,0:T(8,128)S(1)} %shard_map.142.refs_0_), channel_id=1, source_target_pairs={{0,2},{1,3},{2,0},{3,1},{4,6},{5,7},{6,4},{7,5},{8,10},{9,11},{10,... | collective-permute-start | bytes 196616 | tf_op jit(solution)/shard_map/ppermute | solution.py:450
  37.2 1.7 %collective-permute-start.16 = (f32[64,256]{1,0:T(8,128)S(1)}, f32[64,256]{1,0:T(8,128)S(1)}, u32[]{:S(2)}, u32[]{:S(2)}) collective-permute-start(f32[64,256]{1,0:T(8,128)S(1)} %shard_map.142.refs_0_), channel_id=1, source_target_pairs={{0,3},{1,2},{2,1},{3,0},{4,7},{5,6},{6,5},{7,4},{8,11},{9,10},{10,... | collective-permute-start | bytes 196616 | tf_op jit(solution)/shard_map/ppermute | solution.py:450
  38.9 0.8 %collective-permute-done.14.refs_1_ = f32[64,256]{1,0:T(8,128)S(1)} collective-permute-done((f32[64,256]{1,0:T(8,128)S(1)}, f32[64,256]{1,0:T(8,128)S(1)}, u32[]{:S(2)}, u32[]{:S(2)}) %collective-permute-start.14) | collective-permute-done | bytes 65568 | tf_op jit(solution)/shard_map/ppermute | solution.py:450
  39.6 1.7 %collective-permute-done.15.refs_2_ = f32[64,256]{1,0:T(8,128)S(1)} collective-permute-done((f32[64,256]{1,0:T(8,128)S(1)}, f32[64,256]{1,0:T(8,128)S(1)}, u32[]{:S(2)}, u32[]{:S(2)}) %collective-permute-start.15) | collective-permute-done | bytes 65568 | tf_op jit(solution)/shard_map/ppermute | solution.py:450
  41.3 1.0 %collective-permute-done.16.refs_3_ = f32[64,256]{1,0:T(8,128)S(1)} collective-permute-done((f32[64,256]{1,0:T(8,128)S(1)}, f32[64,256]{1,0:T(8,128)S(1)}, u32[]{:S(2)}, u32[]{:S(2)}) %collective-permute-start.16) | collective-permute-done | bytes 65568 | tf_op jit(solution)/shard_map/ppermute | solution.py:450
  (34 shorter events, 4.6 us)
Async XLA Ops:
  1.5 7.7 %collective-permute-start = (f32[8,128]{1,0:T(8,128)S(1)}, f32[8,128]{1,0:T(8,128)S(1)}, u32[]{:S(2)}, u32[]{:S(2)}) collective-permute-start(f32[8,128]{1,0:T(8,128)S(1)} %get-tuple-element.17), channel_id=1, source_target_pairs={{0,1},{1,0},{2,3},{3,2},{4,5},{5,4},{6,7},{7,6},{8,9},{9,8},{10,11... | collective-permute-start | bytes 12296 | tf_op jit(solution)/shard_map/columns_around/ppermute | solution.py:476
  4.5 4.7 %collective-permute-start.1 = (f32[8,128]{1,0:T(8,128)S(1)}, f32[8,128]{1,0:T(8,128)S(1)}, u32[]{:S(2)}, u32[]{:S(2)}) collective-permute-start(f32[8,128]{1,0:T(8,128)S(1)} %get-tuple-element.18), channel_id=1, source_target_pairs={{0,3},{1,2},{2,1},{3,0},{4,7},{5,6},{6,5},{7,4},{8,11},{9,10},{10,... | collective-permute-start | bytes 12296 | tf_op jit(solution)/shard_map/columns_around/ppermute | solution.py:476
  9.3 5.6 %collective-permute-start.2 = (f32[8,384]{1,0:T(8,128)S(1)}, f32[8,384]{1,0:T(8,128)S(1)}, u32[]{:S(2)}, u32[]{:S(2)}) collective-permute-start(f32[8,384]{1,0:T(8,128)S(1)} %get-tuple-element.21), channel_id=1, source_target_pairs={{0,4},{4,0},{8,12},{12,8},{16,20},{20,16},{24,28},{28,24},{1,5},{5... | collective-permute-start | bytes 36872 | tf_op jit(solution)/shard_map/rows_around/ppermute | solution.py:476
  9.4 5.5 %collective-permute-start.3 = (f32[8,384]{1,0:T(8,128)S(1)}, f32[8,384]{1,0:T(8,128)S(1)}, u32[]{:S(2)}, u32[]{:S(2)}) collective-permute-start(f32[8,384]{1,0:T(8,128)S(1)} %get-tuple-element.22), channel_id=1, source_target_pairs={{0,28},{4,8},{8,4},{12,16},{16,12},{20,24},{24,20},{28,0},{1,29},{... | collective-permute-start | bytes 36872 | tf_op jit(solution)/shard_map/rows_around/ppermute | solution.py:476
  14.9 9.8 %copy-start = (bf16[256,512]{1,0:T(8,128)(2,1)S(1)}, bf16[256,512]{1,0:T(8,128)(2,1)}, u32[]{:S(2)}) copy-start(bf16[256,512]{1,0:T(8,128)(2,1)} %constant.10.clone.refs_5_.refs_10_) | copy-start | bytes 786436
  14.9 9.8 %copy-start.1 = (bf16[256,512]{1,0:T(8,128)(2,1)S(1)}, bf16[256,512]{1,0:T(8,128)(2,1)}, u32[]{:S(2)}) copy-start(bf16[256,512]{1,0:T(8,128)(2,1)} %constant.11.clone.refs_6_.refs_11_) | copy-start | bytes 786436
  14.9 9.8 %copy-start.3 = (f32[4,8,256]{2,1,0:T(8,128)S(1)}, f32[4,8,256]{2,1,0:T(8,128)}, u32[]{:S(2)}) copy-start(f32[4,8,256]{2,1,0:T(8,128)} %constant.13.clone.refs_4_) | copy-start | bytes 98308
  17.5 16.6 %copy-start.2 = (bf16[1024,256]{1,0:T(8,128)(2,1)S(1)}, bf16[1024,256]{1,0:T(8,128)(2,1)}, u32[]{:S(2)}) copy-start(bf16[1024,256]{1,0:T(8,128)(2,1)} %constant.12.clone.refs_9_) | copy-start | bytes 1572868
  17.5 4.5 %collective-permute-start.4 = (f32[64,256]{1,0:T(8,128)S(1)}, f32[64,256]{1,0:T(8,128)S(1)}, u32[]{:S(2)}, u32[]{:S(2)}) collective-permute-start(f32[64,256]{1,0:T(8,128)S(1)} %advance.3.refs_0_.refs_5_), channel_id=1, source_target_pairs={{0,1},{1,0},{2,3},{3,2},{4,5},{5,4},{6,7},{7,6},{8,9},{9,8},{10,11... | collective-permute-start | bytes 196616 | tf_op jit(solution)/shard_map/ppermute | solution.py:450
  19.0 4.3 %collective-permute-start.5 = (f32[64,256]{1,0:T(8,128)S(1)}, f32[64,256]{1,0:T(8,128)S(1)}, u32[]{:S(2)}, u32[]{:S(2)}) collective-permute-start(f32[64,256]{1,0:T(8,128)S(1)} %advance.3.refs_0_.refs_5_), channel_id=1, source_target_pairs={{0,2},{1,3},{2,0},{3,1},{4,6},{5,7},{6,4},{7,5},{8,10},{9,11},{10,... | collective-permute-start | bytes 196616 | tf_op jit(solution)/shard_map/ppermute | solution.py:450
  19.6 5.2 %collective-permute-start.6 = (f32[64,256]{1,0:T(8,128)S(1)}, f32[64,256]{1,0:T(8,128)S(1)}, u32[]{:S(2)}, u32[]{:S(2)}) collective-permute-start(f32[64,256]{1,0:T(8,128)S(1)} %advance.3.refs_0_.refs_5_), channel_id=1, source_target_pairs={{0,3},{1,2},{2,1},{3,0},{4,7},{5,6},{6,5},{7,4},{8,11},{9,10},{10,... | collective-permute-start | bytes 196616 | tf_op jit(solution)/shard_map/ppermute | solution.py:450
  25.0 7.2 %collective-permute-start.10 = (f32[64,256]{1,0:T(8,128)S(1)}, f32[64,256]{1,0:T(8,128)S(1)}, u32[]{:S(2)}, u32[]{:S(2)}) collective-permute-start(f32[64,256]{1,0:T(8,128)S(1)} %shard_map.140.refs_0_), channel_id=1, source_target_pairs={{0,16},{4,20},{8,24},{12,28},{16,0},{20,4},{24,8},{28,12},{1,17},{... | collective-permute-start | bytes 196616 | tf_op jit(solution)/shard_map/ppermute | solution.py:450
  25.3 6.9 %collective-permute-start.12 = (f32[64,256]{1,0:T(8,128)S(1)}, f32[64,256]{1,0:T(8,128)S(1)}, u32[]{:S(2)}, u32[]{:S(2)}) collective-permute-start(f32[64,256]{1,0:T(8,128)S(1)} %shard_map.140.refs_0_), channel_id=1, source_target_pairs={{0,24},{4,28},{8,16},{12,20},{16,8},{20,12},{24,0},{28,4},{1,25},{... | collective-permute-start | bytes 196616 | tf_op jit(solution)/shard_map/ppermute | solution.py:450
  26.6 6.2 %collective-permute-start.8 = (f32[64,256]{1,0:T(8,128)S(1)}, f32[64,256]{1,0:T(8,128)S(1)}, u32[]{:S(2)}, u32[]{:S(2)}) collective-permute-start(f32[64,256]{1,0:T(8,128)S(1)} %shard_map.140.refs_0_), channel_id=1, source_target_pairs={{0,8},{4,12},{8,0},{12,4},{16,24},{20,28},{24,16},{28,20},{1,9},{5... | collective-permute-start | bytes 196616 | tf_op jit(solution)/shard_map/ppermute | solution.py:450
  28.5 4.5 %collective-permute-start.7 = (f32[64,256]{1,0:T(8,128)S(1)}, f32[64,256]{1,0:T(8,128)S(1)}, u32[]{:S(2)}, u32[]{:S(2)}) collective-permute-start(f32[64,256]{1,0:T(8,128)S(1)} %shard_map.140.refs_0_), channel_id=1, source_target_pairs={{0,4},{4,0},{8,12},{12,8},{16,20},{20,16},{24,28},{28,24},{1,5},{5... | collective-permute-start | bytes 196616 | tf_op jit(solution)/shard_map/ppermute | solution.py:450
  32.2 1.3 %collective-permute-start.11 = (f32[64,256]{1,0:T(8,128)S(1)}, f32[64,256]{1,0:T(8,128)S(1)}, u32[]{:S(2)}, u32[]{:S(2)}) collective-permute-start(f32[64,256]{1,0:T(8,128)S(1)} %collective-permute-done.10.refs_4_), channel_id=1, source_target_pairs={{0,4},{4,0},{8,12},{12,8},{16,20},{20,16},{24,28},{28,24},{1,5},{5... | collective-permute-start | bytes 196616 | tf_op jit(solution)/shard_map/ppermute | solution.py:450
  32.2 1.4 %collective-permute-start.13 = (f32[64,256]{1,0:T(8,128)S(1)}, f32[64,256]{1,0:T(8,128)S(1)}, u32[]{:S(2)}, u32[]{:S(2)}) collective-permute-start(f32[64,256]{1,0:T(8,128)S(1)} %collective-permute-done.12.refs_6_), channel_id=1, source_target_pairs={{0,4},{4,0},{8,12},{12,8},{16,20},{20,16},{24,28},{28,24},{1,5},{5... | collective-permute-start | bytes 196616 | tf_op jit(solution)/shard_map/ppermute | solution.py:450
  32.8 1.3 %collective-permute-start.9 = (f32[64,256]{1,0:T(8,128)S(1)}, f32[64,256]{1,0:T(8,128)S(1)}, u32[]{:S(2)}, u32[]{:S(2)}) collective-permute-start(f32[64,256]{1,0:T(8,128)S(1)} %collective-permute-done.8.refs_2_), channel_id=1, source_target_pairs={{0,4},{4,0},{8,12},{12,8},{16,20},{20,16},{24,28},{28,24},{1,5},{5... | collective-permute-start | bytes 196616 | tf_op jit(solution)/shard_map/ppermute | solution.py:450
  33.0 9.3 %copy-start.4 = (f32[4,8,256]{2,1,0:T(8,128)S(1)}, f32[4,8,256]{2,1,0:T(8,128)}, u32[]{:S(2)}) copy-start(f32[4,8,256]{2,1,0:T(8,128)} %constant.14.clone.refs_4_) | copy-start | bytes 98308
  35.3 4.3 %collective-permute-start.14 = (f32[64,256]{1,0:T(8,128)S(1)}, f32[64,256]{1,0:T(8,128)S(1)}, u32[]{:S(2)}, u32[]{:S(2)}) collective-permute-start(f32[64,256]{1,0:T(8,128)S(1)} %shard_map.142.refs_0_), channel_id=1, source_target_pairs={{0,1},{1,0},{2,3},{3,2},{4,5},{5,4},{6,7},{7,6},{8,9},{9,8},{10,11... | collective-permute-start | bytes 196616 | tf_op jit(solution)/shard_map/ppermute | solution.py:450
  36.3 5.0 %collective-permute-start.15 = (f32[64,256]{1,0:T(8,128)S(1)}, f32[64,256]{1,0:T(8,128)S(1)}, u32[]{:S(2)}, u32[]{:S(2)}) collective-permute-start(f32[64,256]{1,0:T(8,128)S(1)} %shard_map.142.refs_0_), channel_id=1, source_target_pairs={{0,2},{1,3},{2,0},{3,1},{4,6},{5,7},{6,4},{7,5},{8,10},{9,11},{10,... | collective-permute-start | bytes 196616 | tf_op jit(solution)/shard_map/ppermute | solution.py:450
  37.2 5.2 %collective-permute-start.16 = (f32[64,256]{1,0:T(8,128)S(1)}, f32[64,256]{1,0:T(8,128)S(1)}, u32[]{:S(2)}, u32[]{:S(2)}) collective-permute-start(f32[64,256]{1,0:T(8,128)S(1)} %shard_map.142.refs_0_), channel_id=1, source_target_pairs={{0,3},{1,2},{2,1},{3,0},{4,7},{5,6},{6,5},{7,4},{8,11},{9,10},{10,... | collective-permute-start | bytes 196616 | tf_op jit(solution)/shard_map/ppermute | solution.py:450

commit v8 on v7

--- a/solution.py
+++ b/solution.py
@@ -107,7 +107,7 @@
         k1_ref[r] = block.astype(bf16)
 
 
-def other_weights_kernel(packed_ref, k2_ref, even_ref, odd_ref):
+def other_weights_kernel(packed_ref, order_ref, k2_ref, even_ref, odd_ref):
     slots = {-1: 5, 0: 0, 1: 1, 2: 2, 3: 3, 4: 6}
     blank = jnp.zeros((64, 64), f32)
     for c in range(3):
@@ -494,10 +494,6 @@
             ),
         )(taps, biases)
         packed = jnp.concatenate([w_second.reshape(576, 64), w_third.reshape(144, 64)], axis=0)
-        others = call(
-            other_weights_kernel,
-            (shape((256, 384), bf16), shape((512, 256), bf16), shape((512, 256), bf16)),
-        )(packed)
 
     with jax.named_scope("rows_around"):
         edge = shape((8, breadth + 128), f32)
@@ -505,6 +501,12 @@
             rows_kernel, (edge, edge, shape((2 * height, 128), f32)), (pltpu.VMEM((128, 128), f32),)
         )(both, near, far, biases[2], packed)
         near, far = swapped(near, far, "gx")
+
+    with jax.named_scope("weights"):
+        others = call(
+            other_weights_kernel,
+            (shape((256, 384), bf16), shape((512, 256), bf16), shape((512, 256), bf16)),
+        )(packed, beside)
 
     block = shape((2 * height, breadth), f32)
     padded = pltpu.VMEM((2, rows + 16, breadth + 128), f32)

time: 43.2 us -> 43.7 us (1.012)
  waiting for transfers between devices: 12 us -> 12.5 us
  transfers between devices with their start and end apart: 17 -> 17, of which waited for: 11 -> 11; matrix products, arithmetic and copies ran while one was open for 6% -> 6% of each run, Pallas kernels for 6% -> 5%
where the time goes in v8:
time: 43.7 us; the launch traced here: 43.5 us
  starting transfers between devices  19.5 us (45%)
  waiting for transfers between devices  12.5 us (29%)
  Pallas kernels  7.55 us (17%)
  other arithmetic  3.21 us (7%)
  between operations  0.77 us (2%)
    ppermute x13, waiting for transfers between devices, partner(): lax.ppermute(block, axis, [(i, i ^ k) for i in range(lax.axis_size(axis))])  12.2 us
    ppermute x13, starting transfers between devices, partner(): lax.ppermute(block, axis, [(i, i ^ k) for i in range(lax.axis_size(axis))])  11.2 us
    ppermute x2, starting transfers between devices, swapped(): lax.ppermute(far, axis, other_pairs)  5.19 us
    ppermute x2, starting transfers between devices, swapped(): lax.ppermute(near, axis, pairs)  3.08 us
    pallas_call x1, Pallas kernels, on_device(): call(advance_kernel, block, (padded, pltpu.VMEM((4, span, 256), bf16), pl...  2.59 us
    pallas_call x1, Pallas kernels, on_device(): call(inner_kernel, (shape((groups - 4, span, 256), bf16), shape((groups -...  1.79 us
    pallas_call x1, Pallas kernels, on_device(): call(row_kernel, block, (pltpu.VMEM((grid_x, 2 * breadth), f32),))  1.22 us
    concatenate x1, other arithmetic, on_device(): jnp.concatenate([w_second.reshape(576, 64), w_third.reshape(144, 64)], ax...  0.97 us
  transfers between devices with their start and end apart: 17, of which 11 were waited for; matrix products, arithmetic and copies ran while one was open for 6% of the time, Pallas kernels for 5%

profile of v8, /device:TPU:0, one launch (start us, length us, event | category | flops | bytes accessed | tf_op | source)
XLA Modules:
  0.0 43.5 jit_solution(8255409935727624623)
XLA Ops:
  0.6 0.8 %pad_maximum_fusion.1 = f32[2,32,256]{2,1,0:T(8,128)S(1)} fusion(f32[1,32,256]{2,1,0:T(8,128)} %bitcast.15, f32[1,32,256]{2,1,0:T(8,128)} %bitcast.16), kind=kLoop, calls=%fused_computation.1 | loop fusion | flops 16384 | bytes 131072 | tf_op jit(solution)/shard_map/columns_around/stack | solution.py:479
  1.5 3.0 %collective-permute-start = (f32[8,128]{1,0:T(8,128)S(1)}, f32[8,128]{1,0:T(8,128)S(1)}, u32[]{:S(2)}, u32[]{:S(2)}) collective-permute-start(f32[8,128]{1,0:T(8,128)S(1)} %get-tuple-element.17), channel_id=1, source_target_pairs={{0,1},{1,0},{2,3},{3,2},{4,5},{5,4},{6,7},{7,6},{8,9},{9,8},{10,11... | collective-permute-start | bytes 12296 | tf_op jit(solution)/shard_map/columns_around/ppermute | solution.py:476
  4.5 1.5 %collective-permute-start.1 = (f32[8,128]{1,0:T(8,128)S(1)}, f32[8,128]{1,0:T(8,128)S(1)}, u32[]{:S(2)}, u32[]{:S(2)}) collective-permute-start(f32[8,128]{1,0:T(8,128)S(1)} %get-tuple-element.18), channel_id=1, source_target_pairs={{0,3},{1,2},{2,1},{3,0},{4,7},{5,6},{6,5},{7,4},{8,11},{9,10},{10,... | collective-permute-start | bytes 12296 | tf_op jit(solution)/shard_map/columns_around/ppermute | solution.py:476
  6.7 1.0 %pad_maximum_fusion.order_too_ref.packed_ref = bf16[720,64]{1,0:T(8,128)(2,1)S(1)} fusion(bf16[144,64]{1,0:T(8,128)(2,1)} %bitcast.14, bf16[576,64]{1,0:T(8,128)(2,1)} %bitcast.13), kind=kLoop, calls=%fused_computation | loop fusion | flops 184320 | bytes 184320 | tf_op jit(solution)/shard_map/weights/concatenate | solution.py:496
  7.6 0.8 %pad_maximum_fusion.2 = f32[144]{0:T(256)S(1)} fusion(f32[16]{0:T(128)} %param.20, f32[64]{0:T(128)} %param.18, f32[64]{0:T(128)} %param.16), kind=kLoop, calls=%fused_computation.3 | loop fusion | flops 288 | bytes 1152 | tf_op jit(solution)/shard_map/weights/concatenate | solution.py:486
  9.6 3.7 %collective-permute-start.3 = (f32[8,384]{1,0:T(8,128)S(1)}, f32[8,384]{1,0:T(8,128)S(1)}, u32[]{:S(2)}, u32[]{:S(2)}) collective-permute-start(f32[8,384]{1,0:T(8,128)S(1)} %get-tuple-element.22), channel_id=1, source_target_pairs={{0,28},{4,8},{8,4},{12,16},{16,12},{20,24},{24,20},{28,0},{1,29},{... | collective-permute-start | bytes 36872 | tf_op jit(solution)/shard_map/rows_around/ppermute | solution.py:476
  13.3 1.8 %advance.2 = (bf16[6,272,256]{2,1,0:T(8,128)(2,1)S(1)}, bf16[4,272,256]{2,1,0:T(8,128)(2,1)S(1)}, f32[2,64,384]{2,1,0:T(8,128)S(1)}) custom-call(f32[64,256]{1,0:T(8,128)S(1)} %bitcast.10, f32[64,128]{1,0:T(8,128)S(1)} %get-tuple-element.20.order_ref.beside_ref, bf16[10,256,256]{2,1,0:T(8,128)(2,1)S(1)} %get-tuple-element.23.w1_ref, ...), custom_call_target="tpu_custom_call" | custom-call | flops 500000000 | bytes 1048576 | tf_op jit(solution)/shard_map/advance/pallas_call | solution.py:514
  15.2 2.6 %advance.3.refs_0_.refs_5_ = f32[64,256]{1,0:T(8,128)S(1)} custom-call(f32[64,256]{1,0:T(8,128)S(1)} %bitcast.11, f32[64,128]{1,0:T(8,128)S(1)} %get-tuple-element.20.order_ref.beside_ref, f32[8,384]{1,0:T(8,128)S(1)} %collective-permute-done.2.from_near_ref, f32[8,384]{1,0:T(8,128)S(1)} %collective-permute-done.3.from_far_ref, ...), custom_call_target="tpu_custom_call" | custom-call | flops 1000000000 | bytes 1048576 | tf_op jit(solution)/shard_map/advance/pallas_call | solution.py:524
  17.7 1.3 %collective-permute-start.4 = (f32[64,256]{1,0:T(8,128)S(1)}, f32[64,256]{1,0:T(8,128)S(1)}, u32[]{:S(2)}, u32[]{:S(2)}) collective-permute-start(f32[64,256]{1,0:T(8,128)S(1)} %advance.3.refs_0_.refs_5_), channel_id=1, source_target_pairs={{0,1},{1,0},{2,3},{3,2},{4,5},{5,4},{6,7},{7,6},{8,9},{9,8},{10,11... | collective-permute-start | bytes 196616 | tf_op jit(solution)/shard_map/ppermute | solution.py:450
  19.1 0.8 %collective-permute-start.5 = (f32[64,256]{1,0:T(8,128)S(1)}, f32[64,256]{1,0:T(8,128)S(1)}, u32[]{:S(2)}, u32[]{:S(2)}) collective-permute-start(f32[64,256]{1,0:T(8,128)S(1)} %advance.3.refs_0_.refs_5_), channel_id=1, source_target_pairs={{0,2},{1,3},{2,0},{3,1},{4,6},{5,7},{6,4},{7,5},{8,10},{9,11},{10,... | collective-permute-start | bytes 196616 | tf_op jit(solution)/shard_map/ppermute | solution.py:450
  19.8 1.4 %collective-permute-start.6 = (f32[64,256]{1,0:T(8,128)S(1)}, f32[64,256]{1,0:T(8,128)S(1)}, u32[]{:S(2)}, u32[]{:S(2)}) collective-permute-start(f32[64,256]{1,0:T(8,128)S(1)} %advance.3.refs_0_.refs_5_), channel_id=1, source_target_pairs={{0,3},{1,2},{2,1},{3,0},{4,7},{5,6},{6,5},{7,4},{8,11},{9,10},{10,... | collective-permute-start | bytes 196616 | tf_op jit(solution)/shard_map/ppermute | solution.py:450
  21.3 0.8 %collective-permute-done.4.refs_1_ = f32[64,256]{1,0:T(8,128)S(1)} collective-permute-done((f32[64,256]{1,0:T(8,128)S(1)}, f32[64,256]{1,0:T(8,128)S(1)}, u32[]{:S(2)}, u32[]{:S(2)}) %collective-permute-start.4) | collective-permute-done | bytes 65568 | tf_op jit(solution)/shard_map/ppermute | solution.py:450
  22.1 1.3 %collective-permute-done.5.refs_2_ = f32[64,256]{1,0:T(8,128)S(1)} collective-permute-done((f32[64,256]{1,0:T(8,128)S(1)}, f32[64,256]{1,0:T(8,128)S(1)}, u32[]{:S(2)}, u32[]{:S(2)}) %collective-permute-start.5) | collective-permute-done | bytes 65568 | tf_op jit(solution)/shard_map/ppermute | solution.py:450
  23.3 1.7 %collective-permute-done.6.refs_3_ = f32[64,256]{1,0:T(8,128)S(1)} collective-permute-done((f32[64,256]{1,0:T(8,128)S(1)}, f32[64,256]{1,0:T(8,128)S(1)}, u32[]{:S(2)}, u32[]{:S(2)}) %collective-permute-start.6) | collective-permute-done | bytes 65568 | tf_op jit(solution)/shard_map/ppermute | solution.py:450
  25.5 1.3 %collective-permute-start.12 = (f32[64,256]{1,0:T(8,128)S(1)}, f32[64,256]{1,0:T(8,128)S(1)}, u32[]{:S(2)}, u32[]{:S(2)}) collective-permute-start(f32[64,256]{1,0:T(8,128)S(1)} %shard_map.140.refs_0_), channel_id=1, source_target_pairs={{0,24},{4,28},{8,16},{12,20},{16,8},{20,12},{24,0},{28,4},{1,25},{... | collective-permute-start | bytes 196616 | tf_op jit(solution)/shard_map/ppermute | solution.py:450
  26.9 1.9 %collective-permute-start.8 = (f32[64,256]{1,0:T(8,128)S(1)}, f32[64,256]{1,0:T(8,128)S(1)}, u32[]{:S(2)}, u32[]{:S(2)}) collective-permute-start(f32[64,256]{1,0:T(8,128)S(1)} %shard_map.140.refs_0_), channel_id=1, source_target_pairs={{0,8},{4,12},{8,0},{12,4},{16,24},{20,28},{24,16},{28,20},{1,9},{5... | collective-permute-start | bytes 196616 | tf_op jit(solution)/shard_map/ppermute | solution.py:450
  28.8 3.4 %collective-permute-done.10.refs_4_ = f32[64,256]{1,0:T(8,128)S(1)} collective-permute-done((f32[64,256]{1,0:T(8,128)S(1)}, f32[64,256]{1,0:T(8,128)S(1)}, u32[]{:S(2)}, u32[]{:S(2)}) %collective-permute-start.10) | collective-permute-done | bytes 65568 | tf_op jit(solution)/shard_map/ppermute | solution.py:450
  34.0 1.2 %shard_map.142.refs_0_ = f32[64,256]{1,0:T(8,128)S(1)} custom-call(f32[64,256]{1,0:T(8,128)S(1)} %shard_map.140.refs_0_, f32[64,256]{1,0:T(8,128)S(1)} %collective-permute-done.7.refs_1_, f32[64,256]{1,0:T(8,128)S(1)} %collective-permute-done.8.refs_2_, f32[64,256]{1,0:T(8,128)S(1)} %collective-permute-done.9.refs_3_, ...), custom_call_target="tpu_custom_call" | custom-call | flops 10000000 | bytes 1048576 | tf_op jit(solution)/shard_map/pallas_call | solution.py:542
  35.2 1.6 %collective-permute-start.14 = (f32[64,256]{1,0:T(8,128)S(1)}, f32[64,256]{1,0:T(8,128)S(1)}, u32[]{:S(2)}, u32[]{:S(2)}) collective-permute-start(f32[64,256]{1,0:T(8,128)S(1)} %shard_map.142.refs_0_), channel_id=1, source_target_pairs={{0,1},{1,0},{2,3},{3,2},{4,5},{5,4},{6,7},{7,6},{8,9},{9,8},{10,11... | collective-permute-start | bytes 196616 | tf_op jit(solution)/shard_map/ppermute | solution.py:450
  36.8 0.9 %collective-permute-start.15 = (f32[64,256]{1,0:T(8,128)S(1)}, f32[64,256]{1,0:T(8,128)S(1)}, u32[]{:S(2)}, u32[]{:S(2)}) collective-permute-start(f32[64,256]{1,0:T(8,128)S(1)} %shard_map.142.refs_0_), channel_id=1, source_target_pairs={{0,2},{1,3},{2,0},{3,1},{4,6},{5,7},{6,4},{7,5},{8,10},{9,11},{10,... | collective-permute-start | bytes 196616 | tf_op jit(solution)/shard_map/ppermute | solution.py:450
  37.7 1.1 %collective-permute-start.16 = (f32[64,256]{1,0:T(8,128)S(1)}, f32[64,256]{1,0:T(8,128)S(1)}, u32[]{:S(2)}, u32[]{:S(2)}) collective-permute-start(f32[64,256]{1,0:T(8,128)S(1)} %shard_map.142.refs_0_), channel_id=1, source_target_pairs={{0,3},{1,2},{2,1},{3,0},{4,7},{5,6},{6,5},{7,4},{8,11},{9,10},{10,... | collective-permute-start | bytes 196616 | tf_op jit(solution)/shard_map/ppermute | solution.py:450
  38.8 0.8 %collective-permute-done.14.refs_1_ = f32[64,256]{1,0:T(8,128)S(1)} collective-permute-done((f32[64,256]{1,0:T(8,128)S(1)}, f32[64,256]{1,0:T(8,128)S(1)}, u32[]{:S(2)}, u32[]{:S(2)}) %collective-permute-start.14) | collective-permute-done | bytes 65568 | tf_op jit(solution)/shard_map/ppermute | solution.py:450
  39.5 2.2 %collective-permute-done.15.refs_2_ = f32[64,256]{1,0:T(8,128)S(1)} collective-permute-done((f32[64,256]{1,0:T(8,128)S(1)}, f32[64,256]{1,0:T(8,128)S(1)}, u32[]{:S(2)}, u32[]{:S(2)}) %collective-permute-start.15) | collective-permute-done | bytes 65568 | tf_op jit(solution)/shard_map/ppermute | solution.py:450
  41.7 1.1 %collective-permute-done.16.refs_3_ = f32[64,256]{1,0:T(8,128)S(1)} collective-permute-done((f32[64,256]{1,0:T(8,128)S(1)}, f32[64,256]{1,0:T(8,128)S(1)}, u32[]{:S(2)}, u32[]{:S(2)}) %collective-permute-start.16) | collective-permute-done | bytes 65568 | tf_op jit(solution)/shard_map/ppermute | solution.py:450
  (34 shorter events, 4.9 us)
Async XLA Ops:
  1.5 7.3 %collective-permute-start = (f32[8,128]{1,0:T(8,128)S(1)}, f32[8,128]{1,0:T(8,128)S(1)}, u32[]{:S(2)}, u32[]{:S(2)}) collective-permute-start(f32[8,128]{1,0:T(8,128)S(1)} %get-tuple-element.17), channel_id=1, source_target_pairs={{0,1},{1,0},{2,3},{3,2},{4,5},{5,4},{6,7},{7,6},{8,9},{9,8},{10,11... | collective-permute-start | bytes 12296 | tf_op jit(solution)/shard_map/columns_around/ppermute | solution.py:476
  4.5 4.5 %collective-permute-start.1 = (f32[8,128]{1,0:T(8,128)S(1)}, f32[8,128]{1,0:T(8,128)S(1)}, u32[]{:S(2)}, u32[]{:S(2)}) collective-permute-start(f32[8,128]{1,0:T(8,128)S(1)} %get-tuple-element.18), channel_id=1, source_target_pairs={{0,3},{1,2},{2,1},{3,0},{4,7},{5,6},{6,5},{7,4},{8,11},{9,10},{10,... | collective-permute-start | bytes 12296 | tf_op jit(solution)/shard_map/columns_around/ppermute | solution.py:476
  9.5 5.6 %collective-permute-start.2 = (f32[8,384]{1,0:T(8,128)S(1)}, f32[8,384]{1,0:T(8,128)S(1)}, u32[]{:S(2)}, u32[]{:S(2)}) collective-permute-start(f32[8,384]{1,0:T(8,128)S(1)} %get-tuple-element.21), channel_id=1, source_target_pairs={{0,4},{4,0},{8,12},{12,8},{16,20},{20,16},{24,28},{28,24},{1,5},{5... | collective-permute-start | bytes 36872 | tf_op jit(solution)/shard_map/rows_around/ppermute | solution.py:476
  9.6 5.5 %collective-permute-start.3 = (f32[8,384]{1,0:T(8,128)S(1)}, f32[8,384]{1,0:T(8,128)S(1)}, u32[]{:S(2)}, u32[]{:S(2)}) collective-permute-start(f32[8,384]{1,0:T(8,128)S(1)} %get-tuple-element.22), channel_id=1, source_target_pairs={{0,28},{4,8},{8,4},{12,16},{16,12},{20,24},{24,20},{28,0},{1,29},{... | collective-permute-start | bytes 36872 | tf_op jit(solution)/shard_map/rows_around/ppermute | solution.py:476
  15.1 9.9 %copy-start = (bf16[256,512]{1,0:T(8,128)(2,1)S(1)}, bf16[256,512]{1,0:T(8,128)(2,1)}, u32[]{:S(2)}) copy-start(bf16[256,512]{1,0:T(8,128)(2,1)} %constant.10.clone.refs_5_.refs_10_) | copy-start | bytes 786436
  15.1 9.9 %copy-start.1 = (bf16[256,512]{1,0:T(8,128)(2,1)S(1)}, bf16[256,512]{1,0:T(8,128)(2,1)}, u32[]{:S(2)}) copy-start(bf16[256,512]{1,0:T(8,128)(2,1)} %constant.11.clone.refs_6_.refs_11_) | copy-start | bytes 786436
  15.1 9.9 %copy-start.3 = (f32[4,8,256]{2,1,0:T(8,128)S(1)}, f32[4,8,256]{2,1,0:T(8,128)}, u32[]{:S(2)}) copy-start(f32[4,8,256]{2,1,0:T(8,128)} %constant.13.clone.refs_4_) | copy-start | bytes 98308
  17.7 16.2 %copy-start.2 = (bf16[1024,256]{1,0:T(8,128)(2,1)S(1)}, bf16[1024,256]{1,0:T(8,128)(2,1)}, u32[]{:S(2)}) copy-start(bf16[1024,256]{1,0:T(8,128)(2,1)} %constant.12.clone.refs_9_) | copy-start | bytes 1572868
  17.7 4.3 %collective-permute-start.4 = (f32[64,256]{1,0:T(8,128)S(1)}, f32[64,256]{1,0:T(8,128)S(1)}, u32[]{:S(2)}, u32[]{:S(2)}) collective-permute-start(f32[64,256]{1,0:T(8,128)S(1)} %advance.3.refs_0_.refs_5_), channel_id=1, source_target_pairs={{0,1},{1,0},{2,3},{3,2},{4,5},{5,4},{6,7},{7,6},{8,9},{9,8},{10,11... | collective-permute-start | bytes 196616 | tf_op jit(solution)/shard_map/ppermute | solution.py:450
  19.1 4.3 %collective-permute-start.5 = (f32[64,256]{1,0:T(8,128)S(1)}, f32[64,256]{1,0:T(8,128)S(1)}, u32[]{:S(2)}, u32[]{:S(2)}) collective-permute-start(f32[64,256]{1,0:T(8,128)S(1)} %advance.3.refs_0_.refs_5_), channel_id=1, source_target_pairs={{0,2},{1,3},{2,0},{3,1},{4,6},{5,7},{6,4},{7,5},{8,10},{9,11},{10,... | collective-permute-start | bytes 196616 | tf_op jit(solution)/shard_map/ppermute | solution.py:450
  19.8 5.2 %collective-permute-start.6 = (f32[64,256]{1,0:T(8,128)S(1)}, f32[64,256]{1,0:T(8,128)S(1)}, u32[]{:S(2)}, u32[]{:S(2)}) collective-permute-start(f32[64,256]{1,0:T(8,128)S(1)} %advance.3.refs_0_.refs_5_), channel_id=1, source_target_pairs={{0,3},{1,2},{2,1},{3,0},{4,7},{5,6},{6,5},{7,4},{8,11},{9,10},{10,... | collective-permute-start | bytes 196616 | tf_op jit(solution)/shard_map/ppermute | solution.py:450
  25.3 6.9 %collective-permute-start.10 = (f32[64,256]{1,0:T(8,128)S(1)}, f32[64,256]{1,0:T(8,128)S(1)}, u32[]{:S(2)}, u32[]{:S(2)}) collective-permute-start(f32[64,256]{1,0:T(8,128)S(1)} %shard_map.140.refs_0_), channel_id=1, source_target_pairs={{0,16},{4,20},{8,24},{12,28},{16,0},{20,4},{24,8},{28,12},{1,17},{... | collective-permute-start | bytes 196616 | tf_op jit(solution)/shard_map/ppermute | solution.py:450
  25.5 6.6 %collective-permute-start.12 = (f32[64,256]{1,0:T(8,128)S(1)}, f32[64,256]{1,0:T(8,128)S(1)}, u32[]{:S(2)}, u32[]{:S(2)}) collective-permute-start(f32[64,256]{1,0:T(8,128)S(1)} %shard_map.140.refs_0_), channel_id=1, source_target_pairs={{0,24},{4,28},{8,16},{12,20},{16,8},{20,12},{24,0},{28,4},{1,25},{... | collective-permute-start | bytes 196616 | tf_op jit(solution)/shard_map/ppermute | solution.py:450
  26.9 5.8 %collective-permute-start.8 = (f32[64,256]{1,0:T(8,128)S(1)}, f32[64,256]{1,0:T(8,128)S(1)}, u32[]{:S(2)}, u32[]{:S(2)}) collective-permute-start(f32[64,256]{1,0:T(8,128)S(1)} %shard_map.140.refs_0_), channel_id=1, source_target_pairs={{0,8},{4,12},{8,0},{12,4},{16,24},{20,28},{24,16},{28,20},{1,9},{5... | collective-permute-start | bytes 196616 | tf_op jit(solution)/shard_map/ppermute | solution.py:450
  28.8 4.1 %collective-permute-start.7 = (f32[64,256]{1,0:T(8,128)S(1)}, f32[64,256]{1,0:T(8,128)S(1)}, u32[]{:S(2)}, u32[]{:S(2)}) collective-permute-start(f32[64,256]{1,0:T(8,128)S(1)} %shard_map.140.refs_0_), channel_id=1, source_target_pairs={{0,4},{4,0},{8,12},{12,8},{16,20},{20,16},{24,28},{28,24},{1,5},{5... | collective-permute-start | bytes 196616 | tf_op jit(solution)/shard_map/ppermute | solution.py:450
  32.2 1.3 %collective-permute-start.11 = (f32[64,256]{1,0:T(8,128)S(1)}, f32[64,256]{1,0:T(8,128)S(1)}, u32[]{:S(2)}, u32[]{:S(2)}) collective-permute-start(f32[64,256]{1,0:T(8,128)S(1)} %collective-permute-done.10.refs_4_), channel_id=1, source_target_pairs={{0,4},{4,0},{8,12},{12,8},{16,20},{20,16},{24,28},{28,24},{1,5},{5... | collective-permute-start | bytes 196616 | tf_op jit(solution)/shard_map/ppermute | solution.py:450
  32.2 1.4 %collective-permute-start.13 = (f32[64,256]{1,0:T(8,128)S(1)}, f32[64,256]{1,0:T(8,128)S(1)}, u32[]{:S(2)}, u32[]{:S(2)}) collective-permute-start(f32[64,256]{1,0:T(8,128)S(1)} %collective-permute-done.12.refs_6_), channel_id=1, source_target_pairs={{0,4},{4,0},{8,12},{12,8},{16,20},{20,16},{24,28},{28,24},{1,5},{5... | collective-permute-start | bytes 196616 | tf_op jit(solution)/shard_map/ppermute | solution.py:450
  32.7 1.3 %collective-permute-start.9 = (f32[64,256]{1,0:T(8,128)S(1)}, f32[64,256]{1,0:T(8,128)S(1)}, u32[]{:S(2)}, u32[]{:S(2)}) collective-permute-start(f32[64,256]{1,0:T(8,128)S(1)} %collective-permute-done.8.refs_2_), channel_id=1, source_target_pairs={{0,4},{4,0},{8,12},{12,8},{16,20},{20,16},{24,28},{28,24},{1,5},{5... | collective-permute-start | bytes 196616 | tf_op jit(solution)/shard_map/ppermute | solution.py:450
  32.9 9.9 %copy-start.4 = (f32[4,8,256]{2,1,0:T(8,128)S(1)}, f32[4,8,256]{2,1,0:T(8,128)}, u32[]{:S(2)}) copy-start(f32[4,8,256]{2,1,0:T(8,128)} %constant.14.clone.refs_4_) | copy-start | bytes 98308
  35.2 4.3 %collective-permute-start.14 = (f32[64,256]{1,0:T(8,128)S(1)}, f32[64,256]{1,0:T(8,128)S(1)}, u32[]{:S(2)}, u32[]{:S(2)}) collective-permute-start(f32[64,256]{1,0:T(8,128)S(1)} %shard_map.142.refs_0_), channel_id=1, source_target_pairs={{0,1},{1,0},{2,3},{3,2},{4,5},{5,4},{6,7},{7,6},{8,9},{9,8},{10,11... | collective-permute-start | bytes 196616 | tf_op jit(solution)/shard_map/ppermute | solution.py:450
  36.8 5.0 %collective-permute-start.15 = (f32[64,256]{1,0:T(8,128)S(1)}, f32[64,256]{1,0:T(8,128)S(1)}, u32[]{:S(2)}, u32[]{:S(2)}) collective-permute-start(f32[64,256]{1,0:T(8,128)S(1)} %shard_map.142.refs_0_), channel_id=1, source_target_pairs={{0,2},{1,3},{2,0},{3,1},{4,6},{5,7},{6,4},{7,5},{8,10},{9,11},{10,... | collective-permute-start | bytes 196616 | tf_op jit(solution)/shard_map/ppermute | solution.py:450
  37.7 5.2 %collective-permute-start.16 = (f32[64,256]{1,0:T(8,128)S(1)}, f32[64,256]{1,0:T(8,128)S(1)}, u32[]{:S(2)}, u32[]{:S(2)}) collective-permute-start(f32[64,256]{1,0:T(8,128)S(1)} %shard_map.142.refs_0_), channel_id=1, source_target_pairs={{0,3},{1,2},{2,1},{3,0},{4,7},{5,6},{6,5},{7,4},{8,11},{9,10},{10,... | collective-permute-start | bytes 196616 | tf_op jit(solution)/shard_map/ppermute | solution.py:450

commit v9 on v7

--- a/solution.py
+++ b/solution.py
@@ -455,7 +455,8 @@
 
 
 def gather_x(block):
-    own = [block] + [partner(block, "gx", k) for k in range(2, lax.axis_size("gx"), 2)]
+    far_first = [partner(block, "gx", k) for k in reversed(range(2, lax.axis_size("gx"), 2))]
+    own = [block] + far_first[::-1]
     return [other for held in own for other in (held, partner(held, "gx", 1))]
 
 

time: 43.2 us -> 43.2 us (level)
  no operation moved by 1% of the time
where the time goes in v9:
time: 43.2 us; the launch traced here: 43 us
  starting transfers between devices  19.4 us (45%)
  waiting for transfers between devices  12 us (28%)
  Pallas kernels  7.57 us (18%)
  other arithmetic  3.21 us (7%)
  between operations  0.78 us (2%)
    ppermute x13, waiting for transfers between devices, partner(): lax.ppermute(block, axis, [(i, i ^ k) for i in range(lax.axis_size(axis))])  12 us
    ppermute x13, starting transfers between devices, partner(): lax.ppermute(block, axis, [(i, i ^ k) for i in range(lax.axis_size(axis))])  11.2 us
    ppermute x2, starting transfers between devices, swapped(): lax.ppermute(far, axis, other_pairs)  5.19 us
    ppermute x2, starting transfers between devices, swapped(): lax.ppermute(near, axis, pairs)  3.08 us
    pallas_call x1, Pallas kernels, on_device(): call(advance_kernel, block, (padded, pltpu.VMEM((4, span, 256), bf16), pl...  2.6 us
    pallas_call x1, Pallas kernels, on_device(): call(inner_kernel, (shape((groups - 4, span, 256), bf16), shape((groups -...  1.78 us
    pallas_call x1, Pallas kernels, on_device(): call(row_kernel, block, (pltpu.VMEM((grid_x, 2 * breadth), f32),))  1.22 us
    concatenate x1, other arithmetic, on_device(): jnp.concatenate([w_second.reshape(576, 64), w_third.reshape(144, 64)], ax...  0.97 us
  transfers between devices with their start and end apart: 17, of which 11 were waited for; matrix products, arithmetic and copies ran while one was open for 6% of the time, Pallas kernels for 6%

profile of v9, /device:TPU:0, one launch (start us, length us, event | category | flops | bytes accessed | tf_op | source)
XLA Modules:
  0.0 43.0 jit_solution(15674688894543730658)
XLA Ops:
  0.6 0.8 %pad_maximum_fusion.1 = f32[2,32,256]{2,1,0:T(8,128)S(1)} fusion(f32[1,32,256]{2,1,0:T(8,128)} %bitcast.15, f32[1,32,256]{2,1,0:T(8,128)} %bitcast.16), kind=kLoop, calls=%fused_computation.1 | loop fusion | flops 16384 | bytes 131072 | tf_op jit(solution)/shard_map/columns_around/stack | solution.py:480
  1.5 3.0 %collective-permute-start = (f32[8,128]{1,0:T(8,128)S(1)}, f32[8,128]{1,0:T(8,128)S(1)}, u32[]{:S(2)}, u32[]{:S(2)}) collective-permute-start(f32[8,128]{1,0:T(8,128)S(1)} %get-tuple-element.17), channel_id=1, source_target_pairs={{0,1},{1,0},{2,3},{3,2},{4,5},{5,4},{6,7},{7,6},{8,9},{9,8},{10,11... | collective-permute-start | bytes 12296 | tf_op jit(solution)/shard_map/columns_around/ppermute | solution.py:477
  4.5 1.5 %collective-permute-start.1 = (f32[8,128]{1,0:T(8,128)S(1)}, f32[8,128]{1,0:T(8,128)S(1)}, u32[]{:S(2)}, u32[]{:S(2)}) collective-permute-start(f32[8,128]{1,0:T(8,128)S(1)} %get-tuple-element.18), channel_id=1, source_target_pairs={{0,3},{1,2},{2,1},{3,0},{4,7},{5,6},{6,5},{7,4},{8,11},{9,10},{10,... | collective-permute-start | bytes 12296 | tf_op jit(solution)/shard_map/columns_around/ppermute | solution.py:477
  6.0 0.7 %convert_bitcast_fusion.taps_ref = f32[9,2,64]{2,1,0:T(2,128)S(1)} fusion(bf16[9,64,2]{1,2,0:T(2,128)(2,1)} %param.15), kind=kLoop, calls=%fused_computation.2 | loop fusion | flops 1152 | bytes 6912 | tf_op jit(solution)/shard_map/weights/convert_element_type | solution.py:486
  6.7 1.0 %pad_maximum_fusion.order_too_ref.packed_ref = bf16[720,64]{1,0:T(8,128)(2,1)S(1)} fusion(bf16[144,64]{1,0:T(8,128)(2,1)} %bitcast.14, bf16[576,64]{1,0:T(8,128)(2,1)} %bitcast.13), kind=kLoop, calls=%fused_computation | loop fusion | flops 184320 | bytes 184320 | tf_op jit(solution)/shard_map/weights/concatenate | solution.py:497
  7.6 0.8 %pad_maximum_fusion.2 = f32[144]{0:T(256)S(1)} fusion(f32[16]{0:T(128)} %param.20, f32[64]{0:T(128)} %param.18, f32[64]{0:T(128)} %param.16), kind=kLoop, calls=%fused_computation.3 | loop fusion | flops 288 | bytes 1152 | tf_op jit(solution)/shard_map/weights/concatenate | solution.py:487
  9.4 3.7 %collective-permute-start.3 = (f32[8,384]{1,0:T(8,128)S(1)}, f32[8,384]{1,0:T(8,128)S(1)}, u32[]{:S(2)}, u32[]{:S(2)}) collective-permute-start(f32[8,384]{1,0:T(8,128)S(1)} %get-tuple-element.22), channel_id=1, source_target_pairs={{0,28},{4,8},{8,4},{12,16},{16,12},{20,24},{24,20},{28,0},{1,29},{... | collective-permute-start | bytes 36872 | tf_op jit(solution)/shard_map/rows_around/ppermute | solution.py:477
  13.1 1.8 %advance.2 = (bf16[6,272,256]{2,1,0:T(8,128)(2,1)S(1)}, bf16[4,272,256]{2,1,0:T(8,128)(2,1)S(1)}, f32[2,64,384]{2,1,0:T(8,128)S(1)}) custom-call(f32[64,256]{1,0:T(8,128)S(1)} %bitcast.10, f32[64,128]{1,0:T(8,128)S(1)} %get-tuple-element.20.beside_ref, bf16[10,256,256]{2,1,0:T(8,128)(2,1)S(1)} %get-tuple-element.23.w1_ref, ...), custom_call_target="tpu_custom_call" | custom-call | flops 500000000 | bytes 1048576 | tf_op jit(solution)/shard_map/advance/pallas_call | solution.py:513
  14.9 2.6 %advance.3.refs_0_.refs_5_ = f32[64,256]{1,0:T(8,128)S(1)} custom-call(f32[64,256]{1,0:T(8,128)S(1)} %bitcast.11, f32[64,128]{1,0:T(8,128)S(1)} %get-tuple-element.20.beside_ref, f32[8,384]{1,0:T(8,128)S(1)} %collective-permute-done.2.from_near_ref, f32[8,384]{1,0:T(8,128)S(1)} %collective-permute-done.3.from_far_ref, ...), custom_call_target="tpu_custom_call" | custom-call | flops 1000000000 | bytes 1048576 | tf_op jit(solution)/shard_map/advance/pallas_call | solution.py:523
  17.5 1.5 %collective-permute-start.4 = (f32[64,256]{1,0:T(8,128)S(1)}, f32[64,256]{1,0:T(8,128)S(1)}, u32[]{:S(2)}, u32[]{:S(2)}) collective-permute-start(f32[64,256]{1,0:T(8,128)S(1)} %advance.3.refs_0_.refs_5_), channel_id=1, source_target_pairs={{0,1},{1,0},{2,3},{3,2},{4,5},{5,4},{6,7},{7,6},{8,9},{9,8},{10,11... | collective-permute-start | bytes 196616 | tf_op jit(solution)/shard_map/ppermute | solution.py:450
  19.6 1.5 %collective-permute-start.6 = (f32[64,256]{1,0:T(8,128)S(1)}, f32[64,256]{1,0:T(8,128)S(1)}, u32[]{:S(2)}, u32[]{:S(2)}) collective-permute-start(f32[64,256]{1,0:T(8,128)S(1)} %advance.3.refs_0_.refs_5_), channel_id=1, source_target_pairs={{0,3},{1,2},{2,1},{3,0},{4,7},{5,6},{6,5},{7,4},{8,11},{9,10},{10,... | collective-permute-start | bytes 196616 | tf_op jit(solution)/shard_map/ppermute | solution.py:450
  21.0 1.0 %collective-permute-done.4.refs_1_ = f32[64,256]{1,0:T(8,128)S(1)} collective-permute-done((f32[64,256]{1,0:T(8,128)S(1)}, f32[64,256]{1,0:T(8,128)S(1)}, u32[]{:S(2)}, u32[]{:S(2)}) %collective-permute-start.4) | collective-permute-done | bytes 65568 | tf_op jit(solution)/shard_map/ppermute | solution.py:450
  22.0 1.3 %collective-permute-done.5.refs_2_ = f32[64,256]{1,0:T(8,128)S(1)} collective-permute-done((f32[64,256]{1,0:T(8,128)S(1)}, f32[64,256]{1,0:T(8,128)S(1)}, u32[]{:S(2)}, u32[]{:S(2)}) %collective-permute-start.5) | collective-permute-done | bytes 65568 | tf_op jit(solution)/shard_map/ppermute | solution.py:450
  23.3 1.4 %collective-permute-done.6.refs_3_ = f32[64,256]{1,0:T(8,128)S(1)} collective-permute-done((f32[64,256]{1,0:T(8,128)S(1)}, f32[64,256]{1,0:T(8,128)S(1)}, u32[]{:S(2)}, u32[]{:S(2)}) %collective-permute-start.6) | collective-permute-done | bytes 65568 | tf_op jit(solution)/shard_map/ppermute | solution.py:450
  25.3 1.4 %collective-permute-start.12 = (f32[64,256]{1,0:T(8,128)S(1)}, f32[64,256]{1,0:T(8,128)S(1)}, u32[]{:S(2)}, u32[]{:S(2)}) collective-permute-start(f32[64,256]{1,0:T(8,128)S(1)} %shard_map.140.refs_0_), channel_id=1, source_target_pairs={{0,24},{4,28},{8,16},{12,20},{16,8},{20,12},{24,0},{28,4},{1,25},{... | collective-permute-start | bytes 196616 | tf_op jit(solution)/shard_map/ppermute | solution.py:450
  26.6 1.9 %collective-permute-start.8 = (f32[64,256]{1,0:T(8,128)S(1)}, f32[64,256]{1,0:T(8,128)S(1)}, u32[]{:S(2)}, u32[]{:S(2)}) collective-permute-start(f32[64,256]{1,0:T(8,128)S(1)} %shard_map.140.refs_0_), channel_id=1, source_target_pairs={{0,8},{4,12},{8,0},{12,4},{16,24},{20,28},{24,16},{28,20},{1,9},{5... | collective-permute-start | bytes 196616 | tf_op jit(solution)/shard_map/ppermute | solution.py:450
  28.5 3.6 %collective-permute-done.10.refs_4_ = f32[64,256]{1,0:T(8,128)S(1)} collective-permute-done((f32[64,256]{1,0:T(8,128)S(1)}, f32[64,256]{1,0:T(8,128)S(1)}, u32[]{:S(2)}, u32[]{:S(2)}) %collective-permute-start.10) | collective-permute-done | bytes 65568 | tf_op jit(solution)/shard_map/ppermute | solution.py:450
  34.1 1.2 %shard_map.142.refs_0_ = f32[64,256]{1,0:T(8,128)S(1)} custom-call(f32[64,256]{1,0:T(8,128)S(1)} %shard_map.140.refs_0_, f32[64,256]{1,0:T(8,128)S(1)} %collective-permute-done.7.refs_1_, f32[64,256]{1,0:T(8,128)S(1)} %collective-permute-done.8.refs_2_, f32[64,256]{1,0:T(8,128)S(1)} %collective-permute-done.9.refs_3_, ...), custom_call_target="tpu_custom_call" | custom-call | flops 10000000 | bytes 1048576 | tf_op jit(solution)/shard_map/pallas_call | solution.py:541
  35.3 1.0 %collective-permute-start.14 = (f32[64,256]{1,0:T(8,128)S(1)}, f32[64,256]{1,0:T(8,128)S(1)}, u32[]{:S(2)}, u32[]{:S(2)}) collective-permute-start(f32[64,256]{1,0:T(8,128)S(1)} %shard_map.142.refs_0_), channel_id=1, source_target_pairs={{0,1},{1,0},{2,3},{3,2},{4,5},{5,4},{6,7},{7,6},{8,9},{9,8},{10,11... | collective-permute-start | bytes 196616 | tf_op jit(solution)/shard_map/ppermute | solution.py:450
  36.3 0.8 %collective-permute-start.15 = (f32[64,256]{1,0:T(8,128)S(1)}, f32[64,256]{1,0:T(8,128)S(1)}, u32[]{:S(2)}, u32[]{:S(2)}) collective-permute-start(f32[64,256]{1,0:T(8,128)S(1)} %shard_map.142.refs_0_), channel_id=1, source_target_pairs={{0,2},{1,3},{2,0},{3,1},{4,6},{5,7},{6,4},{7,5},{8,10},{9,11},{10,... | collective-permute-start | bytes 196616 | tf_op jit(solution)/shard_map/ppermute | solution.py:450
  37.2 1.7 %collective-permute-start.16 = (f32[64,256]{1,0:T(8,128)S(1)}, f32[64,256]{1,0:T(8,128)S(1)}, u32[]{:S(2)}, u32[]{:S(2)}) collective-permute-start(f32[64,256]{1,0:T(8,128)S(1)} %shard_map.142.refs_0_), channel_id=1, source_target_pairs={{0,3},{1,2},{2,1},{3,0},{4,7},{5,6},{6,5},{7,4},{8,11},{9,10},{10,... | collective-permute-start | bytes 196616 | tf_op jit(solution)/shard_map/ppermute | solution.py:450
  38.9 0.8 %collective-permute-done.14.refs_1_ = f32[64,256]{1,0:T(8,128)S(1)} collective-permute-done((f32[64,256]{1,0:T(8,128)S(1)}, f32[64,256]{1,0:T(8,128)S(1)}, u32[]{:S(2)}, u32[]{:S(2)}) %collective-permute-start.14) | collective-permute-done | bytes 65568 | tf_op jit(solution)/shard_map/ppermute | solution.py:450
  39.6 1.7 %collective-permute-done.15.refs_2_ = f32[64,256]{1,0:T(8,128)S(1)} collective-permute-done((f32[64,256]{1,0:T(8,128)S(1)}, f32[64,256]{1,0:T(8,128)S(1)}, u32[]{:S(2)}, u32[]{:S(2)}) %collective-permute-start.15) | collective-permute-done | bytes 65568 | tf_op jit(solution)/shard_map/ppermute | solution.py:450
  41.3 1.0 %collective-permute-done.16.refs_3_ = f32[64,256]{1,0:T(8,128)S(1)} collective-permute-done((f32[64,256]{1,0:T(8,128)S(1)}, f32[64,256]{1,0:T(8,128)S(1)}, u32[]{:S(2)}, u32[]{:S(2)}) %collective-permute-start.16) | collective-permute-done | bytes 65568 | tf_op jit(solution)/shard_map/ppermute | solution.py:450
  (34 shorter events, 4.6 us)
Async XLA Ops:
  1.5 7.7 %collective-permute-start = (f32[8,128]{1,0:T(8,128)S(1)}, f32[8,128]{1,0:T(8,128)S(1)}, u32[]{:S(2)}, u32[]{:S(2)}) collective-permute-start(f32[8,128]{1,0:T(8,128)S(1)} %get-tuple-element.17), channel_id=1, source_target_pairs={{0,1},{1,0},{2,3},{3,2},{4,5},{5,4},{6,7},{7,6},{8,9},{9,8},{10,11... | collective-permute-start | bytes 12296 | tf_op jit(solution)/shard_map/columns_around/ppermute | solution.py:477
  4.5 4.7 %collective-permute-start.1 = (f32[8,128]{1,0:T(8,128)S(1)}, f32[8,128]{1,0:T(8,128)S(1)}, u32[]{:S(2)}, u32[]{:S(2)}) collective-permute-start(f32[8,128]{1,0:T(8,128)S(1)} %get-tuple-element.18), channel_id=1, source_target_pairs={{0,3},{1,2},{2,1},{3,0},{4,7},{5,6},{6,5},{7,4},{8,11},{9,10},{10,... | collective-permute-start | bytes 12296 | tf_op jit(solution)/shard_map/columns_around/ppermute | solution.py:477
  9.3 5.6 %collective-permute-start.2 = (f32[8,384]{1,0:T(8,128)S(1)}, f32[8,384]{1,0:T(8,128)S(1)}, u32[]{:S(2)}, u32[]{:S(2)}) collective-permute-start(f32[8,384]{1,0:T(8,128)S(1)} %get-tuple-element.21), channel_id=1, source_target_pairs={{0,4},{4,0},{8,12},{12,8},{16,20},{20,16},{24,28},{28,24},{1,5},{5... | collective-permute-start | bytes 36872 | tf_op jit(solution)/shard_map/rows_around/ppermute | solution.py:477
  9.4 5.5 %collective-permute-start.3 = (f32[8,384]{1,0:T(8,128)S(1)}, f32[8,384]{1,0:T(8,128)S(1)}, u32[]{:S(2)}, u32[]{:S(2)}) collective-permute-start(f32[8,384]{1,0:T(8,128)S(1)} %get-tuple-element.22), channel_id=1, source_target_pairs={{0,28},{4,8},{8,4},{12,16},{16,12},{20,24},{24,20},{28,0},{1,29},{... | collective-permute-start | bytes 36872 | tf_op jit(solution)/shard_map/rows_around/ppermute | solution.py:477
  14.9 9.8 %copy-start = (bf16[256,512]{1,0:T(8,128)(2,1)S(1)}, bf16[256,512]{1,0:T(8,128)(2,1)}, u32[]{:S(2)}) copy-start(bf16[256,512]{1,0:T(8,128)(2,1)} %constant.10.clone.refs_5_.refs_10_) | copy-start | bytes 786436
  14.9 9.8 %copy-start.1 = (bf16[256,512]{1,0:T(8,128)(2,1)S(1)}, bf16[256,512]{1,0:T(8,128)(2,1)}, u32[]{:S(2)}) copy-start(bf16[256,512]{1,0:T(8,128)(2,1)} %constant.11.clone.refs_6_.refs_11_) | copy-start | bytes 786436
  14.9 9.8 %copy-start.3 = (f32[4,8,256]{2,1,0:T(8,128)S(1)}, f32[4,8,256]{2,1,0:T(8,128)}, u32[]{:S(2)}) copy-start(f32[4,8,256]{2,1,0:T(8,128)} %constant.13.clone.refs_4_) | copy-start | bytes 98308
  17.5 16.6 %copy-start.2 = (bf16[1024,256]{1,0:T(8,128)(2,1)S(1)}, bf16[1024,256]{1,0:T(8,128)(2,1)}, u32[]{:S(2)}) copy-start(bf16[1024,256]{1,0:T(8,128)(2,1)} %constant.12.clone.refs_9_) | copy-start | bytes 1572868
  17.5 4.5 %collective-permute-start.4 = (f32[64,256]{1,0:T(8,128)S(1)}, f32[64,256]{1,0:T(8,128)S(1)}, u32[]{:S(2)}, u32[]{:S(2)}) collective-permute-start(f32[64,256]{1,0:T(8,128)S(1)} %advance.3.refs_0_.refs_5_), channel_id=1, source_target_pairs={{0,1},{1,0},{2,3},{3,2},{4,5},{5,4},{6,7},{7,6},{8,9},{9,8},{10,11... | collective-permute-start | bytes 196616 | tf_op jit(solution)/shard_map/ppermute | solution.py:450
  19.0 4.3 %collective-permute-start.5 = (f32[64,256]{1,0:T(8,128)S(1)}, f32[64,256]{1,0:T(8,128)S(1)}, u32[]{:S(2)}, u32[]{:S(2)}) collective-permute-start(f32[64,256]{1,0:T(8,128)S(1)} %advance.3.refs_0_.refs_5_), channel_id=1, source_target_pairs={{0,2},{1,3},{2,0},{3,1},{4,6},{5,7},{6,4},{7,5},{8,10},{9,11},{10,... | collective-permute-start | bytes 196616 | tf_op jit(solution)/shard_map/ppermute | solution.py:450
  19.6 5.2 %collective-permute-start.6 = (f32[64,256]{1,0:T(8,128)S(1)}, f32[64,256]{1,0:T(8,128)S(1)}, u32[]{:S(2)}, u32[]{:S(2)}) collective-permute-start(f32[64,256]{1,0:T(8,128)S(1)} %advance.3.refs_0_.refs_5_), channel_id=1, source_target_pairs={{0,3},{1,2},{2,1},{3,0},{4,7},{5,6},{6,5},{7,4},{8,11},{9,10},{10,... | collective-permute-start | bytes 196616 | tf_op jit(solution)/shard_map/ppermute | solution.py:450
  25.0 7.2 %collective-permute-start.10 = (f32[64,256]{1,0:T(8,128)S(1)}, f32[64,256]{1,0:T(8,128)S(1)}, u32[]{:S(2)}, u32[]{:S(2)}) collective-permute-start(f32[64,256]{1,0:T(8,128)S(1)} %shard_map.140.refs_0_), channel_id=1, source_target_pairs={{0,16},{4,20},{8,24},{12,28},{16,0},{20,4},{24,8},{28,12},{1,17},{... | collective-permute-start | bytes 196616 | tf_op jit(solution)/shard_map/ppermute | solution.py:450
  25.3 6.9 %collective-permute-start.12 = (f32[64,256]{1,0:T(8,128)S(1)}, f32[64,256]{1,0:T(8,128)S(1)}, u32[]{:S(2)}, u32[]{:S(2)}) collective-permute-start(f32[64,256]{1,0:T(8,128)S(1)} %shard_map.140.refs_0_), channel_id=1, source_target_pairs={{0,24},{4,28},{8,16},{12,20},{16,8},{20,12},{24,0},{28,4},{1,25},{... | collective-permute-start | bytes 196616 | tf_op jit(solution)/shard_map/ppermute | solution.py:450
  26.6 6.2 %collective-permute-start.8 = (f32[64,256]{1,0:T(8,128)S(1)}, f32[64,256]{1,0:T(8,128)S(1)}, u32[]{:S(2)}, u32[]{:S(2)}) collective-permute-start(f32[64,256]{1,0:T(8,128)S(1)} %shard_map.140.refs_0_), channel_id=1, source_target_pairs={{0,8},{4,12},{8,0},{12,4},{16,24},{20,28},{24,16},{28,20},{1,9},{5... | collective-permute-start | bytes 196616 | tf_op jit(solution)/shard_map/ppermute | solution.py:450
  28.5 4.5 %collective-permute-start.7 = (f32[64,256]{1,0:T(8,128)S(1)}, f32[64,256]{1,0:T(8,128)S(1)}, u32[]{:S(2)}, u32[]{:S(2)}) collective-permute-start(f32[64,256]{1,0:T(8,128)S(1)} %shard_map.140.refs_0_), channel_id=1, source_target_pairs={{0,4},{4,0},{8,12},{12,8},{16,20},{20,16},{24,28},{28,24},{1,5},{5... | collective-permute-start | bytes 196616 | tf_op jit(solution)/shard_map/ppermute | solution.py:450
  32.2 1.3 %collective-permute-start.11 = (f32[64,256]{1,0:T(8,128)S(1)}, f32[64,256]{1,0:T(8,128)S(1)}, u32[]{:S(2)}, u32[]{:S(2)}) collective-permute-start(f32[64,256]{1,0:T(8,128)S(1)} %collective-permute-done.10.refs_4_), channel_id=1, source_target_pairs={{0,4},{4,0},{8,12},{12,8},{16,20},{20,16},{24,28},{28,24},{1,5},{5... | collective-permute-start | bytes 196616 | tf_op jit(solution)/shard_map/ppermute | solution.py:450
  32.2 1.4 %collective-permute-start.13 = (f32[64,256]{1,0:T(8,128)S(1)}, f32[64,256]{1,0:T(8,128)S(1)}, u32[]{:S(2)}, u32[]{:S(2)}) collective-permute-start(f32[64,256]{1,0:T(8,128)S(1)} %collective-permute-done.12.refs_6_), channel_id=1, source_target_pairs={{0,4},{4,0},{8,12},{12,8},{16,20},{20,16},{24,28},{28,24},{1,5},{5... | collective-permute-start | bytes 196616 | tf_op jit(solution)/shard_map/ppermute | solution.py:450
  32.8 1.3 %collective-permute-start.9 = (f32[64,256]{1,0:T(8,128)S(1)}, f32[64,256]{1,0:T(8,128)S(1)}, u32[]{:S(2)}, u32[]{:S(2)}) collective-permute-start(f32[64,256]{1,0:T(8,128)S(1)} %collective-permute-done.8.refs_2_), channel_id=1, source_target_pairs={{0,4},{4,0},{8,12},{12,8},{16,20},{20,16},{24,28},{28,24},{1,5},{5... | collective-permute-start | bytes 196616 | tf_op jit(solution)/shard_map/ppermute | solution.py:450
  33.0 9.3 %copy-start.4 = (f32[4,8,256]{2,1,0:T(8,128)S(1)}, f32[4,8,256]{2,1,0:T(8,128)}, u32[]{:S(2)}) copy-start(f32[4,8,256]{2,1,0:T(8,128)} %constant.14.clone.refs_4_) | copy-start | bytes 98308
  35.3 4.3 %collective-permute-start.14 = (f32[64,256]{1,0:T(8,128)S(1)}, f32[64,256]{1,0:T(8,128)S(1)}, u32[]{:S(2)}, u32[]{:S(2)}) collective-permute-start(f32[64,256]{1,0:T(8,128)S(1)} %shard_map.142.refs_0_), channel_id=1, source_target_pairs={{0,1},{1,0},{2,3},{3,2},{4,5},{5,4},{6,7},{7,6},{8,9},{9,8},{10,11... | collective-permute-start | bytes 196616 | tf_op jit(solution)/shard_map/ppermute | solution.py:450
  36.3 5.0 %collective-permute-start.15 = (f32[64,256]{1,0:T(8,128)S(1)}, f32[64,256]{1,0:T(8,128)S(1)}, u32[]{:S(2)}, u32[]{:S(2)}) collective-permute-start(f32[64,256]{1,0:T(8,128)S(1)} %shard_map.142.refs_0_), channel_id=1, source_target_pairs={{0,2},{1,3},{2,0},{3,1},{4,6},{5,7},{6,4},{7,5},{8,10},{9,11},{10,... | collective-permute-start | bytes 196616 | tf_op jit(solution)/shard_map/ppermute | solution.py:450
  37.2 5.2 %collective-permute-start.16 = (f32[64,256]{1,0:T(8,128)S(1)}, f32[64,256]{1,0:T(8,128)S(1)}, u32[]{:S(2)}, u32[]{:S(2)}) collective-permute-start(f32[64,256]{1,0:T(8,128)S(1)} %shard_map.142.refs_0_), channel_id=1, source_target_pairs={{0,3},{1,2},{2,1},{3,0},{4,7},{5,6},{6,5},{7,4},{8,11},{9,10},{10,... | collective-permute-start | bytes 196616 | tf_op jit(solution)/shard_map/ppermute | solution.py:450
